TPU v7x, 32 devices: a whole 2x2x4 slice. The times are simulated.
32 devices in a mesh: dp: 2 (over x), ctx: 8 (over z, y), tp: 2 (over core).
Axes of the slice: x: 2, y: 2, z: 4, core: 2. Of those that a mesh axis runs over, the one named last changes fastest.
Arguments:
- hidden_in: bfloat16 [2, 2, 1024, 1024], P(None, 'dp', 'ctx'), may hold values from -6 to 6
- lengths: int32 [2, 2], P(None, 'dp'), may hold values from 256 to 1024, as said below
- positions: int32 [2, 2, 1024], P(None, 'dp', 'ctx'), may hold values from 0 to 3069, as said below
- attn_gain: bfloat16 [1024], P(('dp', 'ctx')), may hold values from 0.099609375 to 1.8984375
- w_query: bfloat16 [1024, 1024], P(('dp', 'ctx'), 'tp'), may hold values from -0.1875 to 0.1875
- w_key: bfloat16 [1024, 512], P(('dp', 'ctx'), 'tp'), may hold values from -0.1875 to 0.1875
- w_value: bfloat16 [1024, 512], P(('dp', 'ctx'), 'tp'), may hold values from -0.1875 to 0.1875
- q_gain: bfloat16 [64], replicated, may hold values from 0.099609375 to 1.8984375
- k_gain: bfloat16 [64], replicated, may hold values from 0.099609375 to 1.8984375
- w_output: bfloat16 [1024, 1024], P('tp', ('dp', 'ctx')), may hold values from -1.5 to 1.5
- ffn_gain: bfloat16 [1024], P(('dp', 'ctx')), may hold values from 0.099609375 to 1.8984375
- w_gate: bfloat16 [1024, 4608], P(('dp', 'ctx'), 'tp'), may hold values from -0.1875 to 0.1875
- w_up: bfloat16 [1024, 4608], P(('dp', 'ctx'), 'tp'), may hold values from -0.1875 to 0.1875
- w_down: bfloat16 [4608, 1024], P('tp', ('dp', 'ctx')), may hold values from -0.09375 to 0.09375
- grad_out: bfloat16 [2, 2, 1024, 1024], P(None, 'dp', 'ctx'), may hold values from -6 to 6
Outputs:
- out_hidden: bfloat16 [2, 2, 1024, 1024], P(None, 'dp', 'ctx')
- grad_hidden: bfloat16 [2, 2, 1024, 1024], P(None, 'dp', 'ctx')
- grad_attn_gain: float32 [1024], P(('dp', 'ctx'))
- grad_w_query: float32 [1024, 1024], P(('dp', 'ctx'), 'tp')
- grad_w_key: float32 [1024, 512], P(('dp', 'ctx'), 'tp')
- grad_w_value: float32 [1024, 512], P(('dp', 'ctx'), 'tp')
- grad_q_gain: float32 [64], replicated
- grad_k_gain: float32 [64], replicated
- grad_w_output: float32 [1024, 1024], P('tp', ('dp', 'ctx'))
- grad_ffn_gain: float32 [1024], P(('dp', 'ctx'))
- grad_w_gate: float32 [1024, 4608], P(('dp', 'ctx'), 'tp')
- grad_w_up: float32 [1024, 4608], P(('dp', 'ctx'), 'tp')
- grad_w_down: float32 [4608, 1024], P('tp', ('dp', 'ctx'))
Inputs may be any that keep to these rules, and one draw needn't show every extreme that they name: For every slot index s, at least one micro-batch has lengths[m, s] = 1024. positions[m, s, 0] = 0, and from each token to the next the position rises by 1, 2 or 3.
All inputs are finite; a program needn't handle non-finite values.
Results may differ from a plain program's by a relative error of at most 0.025.
Values may be sent and summed in bfloat16 or wider, within the bound.
No kernel may reach another device: no remote copies, remote signals or barrier semaphores. Data moves between devices by JAX's collectives and lax.ppermute only.
A program may use at most 256 MiB of HBM per device.

v0:
```python
import functools

import jax
import jax.numpy as jnp
from jax import lax
from jax.experimental import pallas as pl
from jax.experimental.pallas import tpu as pltpu
from jax.sharding import Mesh, PartitionSpec as P

HEADS = 16
KV_HEADS = 8
HEAD_DIM = 64
EPSILON = 1e-05
ROPE_BASE = 1000000.0
MASKED = -1e30
BF = jnp.bfloat16
F32 = jnp.float32
VMEM_BYTES = 60 * 2**20
LANES = 128
SMALL_COST = pl.CostEstimate(flops=1, bytes_accessed=1, transcendentals=0)


def dot(a, b, dims):
    return lax.dot_general(a, b, (dims, ((), ())), preferred_element_type=F32)


def mm(a, b):
    return dot(a, b, ((1,), (0,)))


def mm_nt(a, b):
    return dot(a, b, ((1,), (1,)))


def mm_tn(a, b):
    return dot(a, b, ((0,), (0,)))


def nothing(*refs):
    pass


def after(value, *others):
    anywhere = pl.BlockSpec(memory_space=pl.ANY)
    return pl.pallas_call(
        nothing,
        in_specs=[anywhere] * (1 + len(others)),
        out_specs=anywhere,
        out_shape=jax.ShapeDtypeStruct(value.shape, value.dtype),
        input_output_aliases={0: 0},
        cost_estimate=SMALL_COST,
        name="after",
    )(value, *others)


def swap(v, axis):
    return lax.ppermute(v, axis, [(0, 1), (1, 0)])


def add(a, b):
    return (a.astype(F32) + b.astype(F32)).astype(BF)


def norm_scale(vector):
    return lax.rsqrt(jnp.mean(vector * vector, -1, keepdims=True) + EPSILON)


def norm_back(vector, factor, gain, upstream):
    weighted = upstream * gain
    return factor * weighted - vector * factor * factor * factor * jnp.mean(
        vector * weighted, -1, keepdims=True
    )


def half_turn(vector):
    middle_index = vector.shape[-1] // 2
    return jnp.concatenate([-vector[..., middle_index:], vector[..., :middle_index]], -1)


def half_turn_back(vector):
    middle_index = vector.shape[-1] // 2
    return jnp.concatenate([vector[..., middle_index:], -vector[..., :middle_index]], -1)


def in_order(parts, index):
    bit = 1
    while bit < len(parts):
        flag = (index & bit) != 0
        parts = [jnp.where(flag, parts[i ^ bit], parts[i]) for i in range(len(parts))]
        bit *= 2
    return parts


def row_sums(square, low):
    left = jnp.sum(jnp.where(low, square, 0.0), -1, keepdims=True)
    right = jnp.sum(jnp.where(low, 0.0, square), -1, keepdims=True)
    return jnp.where(low, left, right)


def pair_scale(pair, low):
    return lax.rsqrt(row_sums(pair * pair, low) * (1.0 / HEAD_DIM) + EPSILON)


def lanes(shape):
    return lax.broadcasted_iota(jnp.int32, shape, 1)


def turned(pair, first):
    width = pair.shape[1]
    quarter = HEAD_DIM // 2
    return jnp.where(first, pltpu.roll(pair, width - quarter, 1), pltpu.roll(pair, quarter, 1))


def qkv_kernel(half_tiles, h0_ref, h1_ref, gain_ref, w_ref, qk_gain_ref, cos_ref, sin_ref,
               xa0_ref, xa1_ref, raw_ref, qkv_ref):
    def run(h_ref, xa_ref):
        hidden = h_ref[...].astype(F32)
        factor = lax.rsqrt(jnp.mean(hidden * hidden, -1, keepdims=True) + EPSILON)
        xa = (hidden * factor * gain_ref[...]).astype(BF)
        xa_ref[...] = xa
        raw = mm(xa, w_ref[:, :256])
        raw_ref[...] = raw
        lane = lanes((raw.shape[0], 128))
        low = lane < HEAD_DIM
        first = lane % HEAD_DIM < HEAD_DIM // 2
        cosine, sine = cos_ref[...], sin_ref[...]
        sine = jnp.where(first, -sine, sine)
        for p in range(2):
            pair = raw[:, 128 * p : 128 * (p + 1)]
            normed = pair * pair_scale(pair, low) * qk_gain_ref[p : p + 1, :]
            turned_pair = normed * cosine + turned(normed, first) * sine
            if p == 1:
                turned_pair = jnp.where(low, turned_pair, pair)
            qkv_ref[:, 128 * p : 128 * (p + 1)] = turned_pair.astype(BF)

    @pl.when(pl.program_id(0) < half_tiles)
    def _():
        run(h0_ref, xa0_ref)

    @pl.when(pl.program_id(0) >= half_tiles)
    def _():
        run(h1_ref, xa1_ref)


def qkv_call(h0, h1, gain, w, qk_gain, cosine, sine):
    half, d_model = h0.shape
    tile = min(256, half)
    n = half // tile
    own = pl.BlockSpec((tile, d_model), lambda i: (jnp.minimum(i, n - 1), 0))
    other = pl.BlockSpec((tile, d_model), lambda i: (jnp.maximum(i - n, 0), 0))
    def fixed(a):
        return pl.BlockSpec(a.shape, lambda i: (0, 0))
    def rows(width):
        return pl.BlockSpec((tile, width), lambda i: (i, 0))
    return pl.pallas_call(
        functools.partial(qkv_kernel, n),
        grid=(2 * n,),
        in_specs=[own, other, fixed(gain), fixed(w), fixed(qk_gain), rows(128), rows(128)],
        out_specs=[own, other, rows(256), rows(256)],
        out_shape=[
            jax.ShapeDtypeStruct(h0.shape, BF),
            jax.ShapeDtypeStruct(h0.shape, BF),
            jax.ShapeDtypeStruct((2 * half, 256), F32),
            jax.ShapeDtypeStruct((2 * half, 256), BF),
        ],
        compiler_params=pltpu.CompilerParams(vmem_limit_bytes=VMEM_BYTES),
        cost_estimate=SMALL_COST,
        name="qkv",
    )(h0, h1, gain, w, qk_gain, cosine, sine)


def blocks_of(tiles):
    return [(a, k) for a in range(tiles) for k in range(a + 1)]


def stacked(pair):
    return jnp.concatenate([pair[:, :HEAD_DIM], pair[:, HEAD_DIM:]], 0)


def attend_kernel(tile, tiles, at_ref, qkv_ref, mixed_ref, probs_ref):
    half = tiles // 2
    def place(t):
        return pl.multiple_of((t + half * at_ref[1]) % tiles * tile, tile)
    for a in range(tiles):
        query = stacked(qkv_ref[pl.ds(place(a), tile), :128])
        row = lax.broadcasted_iota(jnp.int32, (2 * tile, 1), 0) % tile + a * tile
        limit = jnp.minimum(row + 1, at_ref[0])
        scores = []
        for k in range(a + 1):
            key = qkv_ref[pl.ds(place(k), tile), 128 : 128 + HEAD_DIM]
            column = lax.broadcasted_iota(jnp.int32, (1, tile), 1) + k * tile
            scores.append(
                jnp.where(column < limit, mm_nt(query, key) * HEAD_DIM ** (-0.5), MASKED)
            )
        peak = functools.reduce(jnp.maximum, [jnp.max(s, -1, keepdims=True) for s in scores])
        exps = [jnp.exp(s - peak) for s in scores]
        total = functools.reduce(jnp.add, [jnp.sum(e, -1, keepdims=True) for e in exps])
        inverse = 1.0 / total
        mixed = 0.0
        for k in range(a + 1):
            probs = (exps[k] * inverse).astype(BF)
            probs_ref[blocks_of(tiles).index((a, k))] = probs
            value = qkv_ref[pl.ds(place(k), tile), 128 + HEAD_DIM :]
            mixed = mixed + mm(probs, value)
        mixed_ref[pl.ds(place(a), tile), :] = jnp.concatenate(
            [mixed[:tile], mixed[tile:]], 1
        ).astype(BF)


def attend_call(at, qkv):
    count = qkv.shape[0]
    tile = min(256, count // 2)
    tiles = count // tile
    pairs = len(blocks_of(tiles))
    return pl.pallas_call(
        functools.partial(attend_kernel, tile, tiles),
        in_specs=[pl.BlockSpec(memory_space=pltpu.SMEM), pl.BlockSpec(memory_space=pltpu.VMEM)],
        out_specs=[pl.BlockSpec(memory_space=pltpu.VMEM)] * 2,
        out_shape=[
            jax.ShapeDtypeStruct((count, 128), BF),
            jax.ShapeDtypeStruct((pairs, 2 * tile, tile), BF),
        ],
        compiler_params=pltpu.CompilerParams(vmem_limit_bytes=VMEM_BYTES),
        cost_estimate=SMALL_COST,
        name="attend",
    )(at, qkv)


def attend_back_kernel(tile, tiles, at_ref, qkv_ref, mixed_ref, probs_ref, raw_ref, g0_ref, g1_ref,
                       wo_ref, qk_gain_ref, cos_ref, sin_ref, out_ref, total_ref, dm_ref, dkv_ref):
    half = tiles // 2
    def place(t):
        return pl.multiple_of((t + half * at_ref[1]) % tiles * tile, tile)
    rows = half * tile
    dm_ref[:rows] = mm(g0_ref[...], wo_ref[...]).astype(BF)
    dm_ref[rows:] = mm(g1_ref[...], wo_ref[...]).astype(BF)
    scale = HEAD_DIM ** (-0.5)
    lane = lanes((tile, 128))
    low = lane < HEAD_DIM
    first = lane % HEAD_DIM < HEAD_DIM // 2

    def finish(t, p, grad):
        at = pl.ds(place(t), tile)
        cosine, sine = cos_ref[at], sin_ref[at]
        pair = raw_ref[at, 128 * p : 128 * (p + 1)]
        factor = pair_scale(pair, low)
        signed = grad * jnp.where(first, -sine, sine)
        upstream = grad * cosine + turned(signed, first)
        gain = qk_gain_ref[p : p + 1, :]
        weighted = upstream * gain
        mean = row_sums(pair * weighted, low) * (1.0 / HEAD_DIM)
        result = factor * weighted - pair * (factor * factor * factor * mean)
        terms = jnp.sum(upstream * pair * factor, 0, keepdims=True)
        if p == 1:
            result = jnp.where(low, result, grad)
        out_ref[at, 128 * p : 128 * (p + 1)] = result.astype(BF)
        total_ref[p : p + 1, :] += terms

    total_ref[...] = jnp.zeros_like(total_ref)
    dkv = [0.0] * tiles
    for a in range(tiles):
        at = pl.ds(place(a), tile)
        query = stacked(qkv_ref[at, :128])
        grad = stacked(dm_ref[at])
        mixed = stacked(mixed_ref[at, :])
        delta = jnp.sum(grad.astype(F32) * mixed.astype(F32), -1, keepdims=True)
        grad_query = 0.0
        for k in range(a + 1):
            keys = pl.ds(place(k), tile)
            key = qkv_ref[keys, 128 : 128 + HEAD_DIM]
            value = qkv_ref[keys, 128 + HEAD_DIM :]
            probs = probs_ref[blocks_of(tiles).index((a, k))]
            grad_scores = (probs.astype(F32) * (mm_nt(grad, value) - delta)).astype(BF)
            grad_query = grad_query + mm(grad_scores, key)
            grad_kv = jnp.concatenate(
                [mm_tn(grad_scores, query) * scale, mm_tn(probs, grad)], 1
            )
            if a == k:
                dkv_ref[k] = grad_kv
            else:
                dkv_ref[k] += grad_kv
        grad_query = grad_query * scale
        finish(a, 0, jnp.concatenate([grad_query[:tile], grad_query[tile:]], 1))
    for k in range(tiles):
        finish(k, 1, dkv_ref[k])


def attend_back_call(at, qkv, mixed, probs, raw, g0, g1, wo, qk_gain, cosine, sine):
    count = qkv.shape[0]
    tile = min(256, count // 2)
    tiles = count // tile
    vmem = pl.BlockSpec(memory_space=pltpu.VMEM)
    return pl.pallas_call(
        functools.partial(attend_back_kernel, tile, tiles),
        in_specs=[pl.BlockSpec(memory_space=pltpu.SMEM)] + [vmem] * 10,
        out_specs=[vmem] * 2,
        out_shape=[
            jax.ShapeDtypeStruct((count, 256), BF),
            jax.ShapeDtypeStruct((8, 128), F32),
        ],
        scratch_shapes=[pltpu.VMEM((count, 128), BF), pltpu.VMEM((tiles, tile, 128), F32)],
        compiler_params=pltpu.CompilerParams(vmem_limit_bytes=VMEM_BYTES),
        cost_estimate=SMALL_COST,
        name="attend_back",
    )(at, qkv, mixed, probs, raw, g0, g1, wo, qk_gain, cosine, sine)


def ffn_kernel(fw, part, x_ref, cot_ref, *refs):
    a_refs, b_refs, (w_ref, act_ref, grad_ref, grad_in_ref, out_ref) = refs[:3], refs[3:6], refs[6:]
    width = a_refs[0].shape[1]
    a_refs = [*a_refs[:2], w_ref.at[:, :width], a_refs[2]]
    b_refs = [*b_refs[:2], w_ref.at[:, width:], b_refs[2]]
    rest = 2 * fw - width
    pre_a, pre_b, grad_act = 0.0, 0.0, 0.0
    for p in range(4):
        cut = slice(p * part, (p + 1) * part)
        pre_a = pre_a + mm(x_ref[:, cut], a_refs[p][...])
        pre_b = pre_b + mm(x_ref[:, cut], b_refs[p][:, :rest])
        grad_act = grad_act + mm(cot_ref[:, cut], b_refs[p][:, rest : rest + fw])
    pre = jnp.concatenate([pre_a, pre_b], 1)
    gate, up = pre[:, :fw], pre[:, fw:]
    sigmoid = 1.0 / (1.0 + jnp.exp(-gate))
    silu = gate * sigmoid
    act = (silu * up).astype(BF)
    act_ref[...] = act
    grad_gate = grad_act * up * sigmoid * (1.0 + gate * (1.0 - sigmoid))
    grad = jnp.concatenate([grad_gate, grad_act * silu], 1).astype(BF)
    grad_ref[...] = grad
    for p in range(4):
        cut = slice(p * part, (p + 1) * part)
        grad_in = mm_nt(grad[:, :width], a_refs[p][...])
        grad_in = grad_in + mm_nt(grad[:, width:], b_refs[p][:, :rest])
        grad_in_ref[:, cut] = grad_in.astype(BF)
        out_ref[:, cut] = mm_nt(act, b_refs[p][:, rest : rest + fw]).astype(BF)


def ffn_call(fw, x, cot, w_a, w_b, w_own):
    count, d_model = x.shape
    part = w_a[0].shape[0]
    tile = min(256, count)
    shapes = [(count, fw), (count, 2 * fw), (count, d_model), (count, d_model)]
    return pl.pallas_call(
        functools.partial(ffn_kernel, fw, part),
        grid=(count // tile,),
        in_specs=[
            pl.BlockSpec((tile, d_model), lambda i: (i, 0)),
            pl.BlockSpec((tile, d_model), lambda i: (i, 0)),
        ]
        + [pl.BlockSpec(p.shape, lambda i: (0, 0)) for p in (*w_a, *w_b, w_own)],
        out_specs=[pl.BlockSpec((tile, s[1]), lambda i: (i, 0)) for s in shapes],
        out_shape=[jax.ShapeDtypeStruct(s, BF) for s in shapes],
        compiler_params=pltpu.CompilerParams(vmem_limit_bytes=VMEM_BYTES),
        cost_estimate=SMALL_COST,
        name="ffn",
    )(x, cot, *w_a, *w_b, w_own)


def ffn_grad_kernel(fw, width, whole, *refs):
    ins, outs = refs[:8], refs[8:]
    x0, x1, cot0, cot1, grad0, grad1, act0, act1 = (r[...] for r in ins)
    grad_in = (mm_tn(x0, grad0) + mm_tn(x1, grad1)).astype(BF)
    grad_out = (mm_tn(cot0, act0) + mm_tn(cot1, act1)).astype(BF)
    rest = 2 * fw - width

    def write(a_ref, b_ref):
        a_ref[...] = grad_in[:, :width]
        b_ref[:, :rest] = grad_in[:, width:]
        b_ref[:, rest : rest + fw] = grad_out
        left = width - rest - fw
        if left:
            b_ref[:, rest + fw :] = jnp.zeros((grad_out.shape[0], left), BF)

    @pl.when(pl.program_id(0) == 0)
    def _():
        if whole:
            write(outs[0].at[:, :width], outs[0].at[:, width:])
        else:
            write(*outs[:2])

    @pl.when(pl.program_id(0) == 1)
    def _():
        write(*outs[-2:])


def ffn_grad_call(p, width, whole, x, cot, grad, act):
    count, d_model = x[0].shape
    fw = act[0].shape[1]
    part = d_model // 4
    columns = pl.BlockSpec((count, part), lambda i: (0, p + i))
    operands = [pl.BlockSpec(a.shape, lambda i: (0, 0)) for a in (*grad, *act)]
    shapes = ([(part, 2 * width)] if whole else [(part, width)] * 2) + [(part, width)] * 2
    return pl.pallas_call(
        functools.partial(ffn_grad_kernel, fw, width, whole),
        grid=(2,),
        in_specs=[columns] * 4 + operands,
        out_specs=[pl.BlockSpec(s, lambda i: (0, 0)) for s in shapes],
        out_shape=[jax.ShapeDtypeStruct(s, BF) for s in shapes],
        compiler_params=pltpu.CompilerParams(vmem_limit_bytes=VMEM_BYTES),
        cost_estimate=SMALL_COST,
        name="ffn_grad",
    )(*x, *cot, *grad, *act)


def attn_grad_kernel(x0_ref, x1_ref, g0_ref, g1_ref, raw_ref, mixed_ref, *outs):
    side = x0_ref.shape[0]
    wide = raw_ref.shape[1]
    grad_qkv = mm_tn(x0_ref[...], raw_ref[:side]) + mm_tn(x1_ref[...], raw_ref[side:])
    grad_o = mm_tn(g0_ref[...], mixed_ref[:side]) + mm_tn(g1_ref[...], mixed_ref[side:])
    for p in range(4):

        @pl.when(pl.program_id(0) == p)
        def _():
            outs[p][:, :wide] = grad_qkv.astype(BF)
            outs[p][:, wide:] = grad_o.astype(BF)


def attn_grad_call(x, g, raw, mixed):
    count, d_model = x[0].shape
    part = d_model // 4
    shape = (part, raw.shape[1] + mixed.shape[1])
    columns = pl.BlockSpec((count, part), lambda i: (0, i))
    return pl.pallas_call(
        attn_grad_kernel,
        grid=(4,),
        in_specs=[columns] * 4 + [pl.BlockSpec(a.shape, lambda i: (0, 0)) for a in (raw, mixed)],
        out_specs=[pl.BlockSpec(shape, lambda i: (0, 0))] * 4,
        out_shape=[jax.ShapeDtypeStruct(shape, BF)] * 4,
        compiler_params=pltpu.CompilerParams(vmem_limit_bytes=VMEM_BYTES),
        cost_estimate=SMALL_COST,
        name="attn_grad",
    )(*x, *g, raw, mixed)


def merge_kernel(place_ref, near_a, near_b, got_a, got_b, opposite, *outs):
    height, width = outs[0].shape[0], near_a.shape[1]
    for d, out_ref in enumerate(outs):
        at = pl.ds(pl.multiple_of((place_ref[0] ^ d) * height, height), height)
        for near, got, start in ((near_a, got_a, 0), (near_b, got_b, width)):
            total = near[at, :].astype(F32) + got[at, :].astype(F32)
            total = total + opposite[at, start : start + width].astype(F32)
            out_ref[:, start : start + width] = total.astype(BF)


def merge_call(place, places, *arrays):
    rows, width = arrays[0].shape
    shape = jax.ShapeDtypeStruct((rows // places, 2 * width), BF)
    vmem = pl.BlockSpec(memory_space=pltpu.VMEM)
    return pl.pallas_call(
        merge_kernel,
        in_specs=[pl.BlockSpec(memory_space=pltpu.SMEM)] + [vmem] * 5,
        out_specs=[vmem] * places,
        out_shape=[shape] * places,
        compiler_params=pltpu.CompilerParams(vmem_limit_bytes=VMEM_BYTES),
        cost_estimate=SMALL_COST,
        name="merge",
    )(place, *arrays)


def final_kernel(
    qw, fw, place_ref, got_ref, p0_ref, p1_ref, p2_ref, p3_ref, wq_ref, wk_ref, wv_ref, wg_ref, wu_ref,
    q_ref, k_ref, v_ref, o_ref, gate_ref, up_ref, down_ref, sum_ref,
):
    places = got_ref.shape[0]

    def side_by_side(start, width):
        return jnp.concatenate(
            [got_ref[p, :, start : start + width] for p in range(places)], 1
        ).astype(F32)

    def rows(weight_ref, grad):
        return jnp.sum(weight_ref[...].astype(F32) * grad, 1, keepdims=True)

    query, key, value = side_by_side(0, qw), side_by_side(qw, HEAD_DIM), side_by_side(qw + HEAD_DIM, HEAD_DIM)
    q_ref[...], k_ref[...], v_ref[...] = query, key, value
    sum_attn = rows(wq_ref, query) + rows(wk_ref, key) + rows(wv_ref, value)
    start = qw + 2 * HEAD_DIM
    o_ref[...] = side_by_side(start, qw)
    pieces = in_order([r[...].astype(F32) for r in (p0_ref, p1_ref, p2_ref, p3_ref)], place_ref[0])
    gate, up, down = (
        jnp.concatenate([p[:, n * fw : (n + 1) * fw] for p in pieces], 1) for n in range(3)
    )
    gate_ref[...], up_ref[...] = gate, up
    sum_ffn = rows(wg_ref, gate) + rows(wu_ref, up)
    down_ref[...] = down
    lane = lanes(sum_ref.shape)
    sum_ref[...] = jnp.where(lane == 0, sum_attn, sum_ffn)


def final_call(qw, fw, place, got, pieces, wq, wk, wv, wg, wu):
    shard = got.shape[1]
    vmem = pl.BlockSpec(memory_space=pltpu.VMEM)
    shapes = [wq.shape, wk.shape, wv.shape, wq.shape, wg.shape, wu.shape, wg.shape]
    shapes.append((shard, LANES))
    return pl.pallas_call(
        functools.partial(final_kernel, qw, fw),
        in_specs=[pl.BlockSpec(memory_space=pltpu.SMEM)] + [vmem] * 10,
        out_specs=[vmem] * 8,
        out_shape=[jax.ShapeDtypeStruct(s, F32) for s in shapes],
        compiler_params=pltpu.CompilerParams(vmem_limit_bytes=VMEM_BYTES),
        cost_estimate=SMALL_COST,
        name="final",
    )(place, got, *pieces, wq, wk, wv, wg, wu)


def body(
    hidden_in,
    lengths,
    positions,
    attn_gain,
    w_query,
    w_key,
    w_value,
    q_gain,
    k_gain,
    w_output,
    ffn_gain,
    w_gate,
    w_up,
    w_down,
    grad_out,
):
    H, B, J, T = (lax.axis_size(a) for a in ("h", "b", "j", "tp"))
    ix, ih, ib, ij, it = (lax.axis_index(a) for a in ("dp", "h", "b", "j", "tp"))
    rows = hidden_in.shape[2]
    d_model = hidden_in.shape[3]
    shard = w_query.shape[0]
    group = HEADS // KV_HEADS
    qw = group * HEAD_DIM
    fw = w_gate.shape[1] // J
    count = T * J * rows
    side = J * rows
    ffn_width = -(-3 * fw // (2 * LANES)) * LANES
    score_scale = HEAD_DIM ** (-0.5)
    quarter = 2 * ix + ih
    part = d_model // 4

    def cut(array, p, width):
        return array[:, p * width : (p + 1) * width]

    def exchange(name, pieces):
        with jax.named_scope(name):
            return lax.all_to_all(pieces, "j", 0, 0)

    def exchange_beside(name, pieces):
        with jax.named_scope(name):
            pieces = in_order(pieces, ij)
            parts = [pieces[0]]
            for d in range(1, J):
                parts.append(lax.ppermute(pieces[d], "j", [(i, i ^ d) for i in range(J)]))
            return parts

    def two_numbers(values):
        high = values.astype(BF)
        low = (values - high.astype(F32)).astype(BF)
        return jnp.pad(jnp.concatenate([high, low], 0), ((0, 6), (0, 0)))

    def one_number(block):
        return block[..., 0:1, :].astype(F32) + block[..., 1:2, :].astype(F32)

    def relative(array):
        pieces = [array[..., p * part : (p + 1) * part] for p in range(4)]
        return jnp.concatenate(in_order(pieces, quarter), -1)

    turn = [(0, 0), (1, 2), (2, 1), (3, 3)]

    def fetch(name, array, *others):
        with jax.named_scope(name):
            mine = lax.dynamic_index_in_dim(array, it, 0, keepdims=False)[0]
            if others:
                mine = after(mine, *others)
            return lax.ppermute(mine, ("h", "tp"), turn)

    def give_back(name, block):
        with jax.named_scope(name):
            mine = lax.ppermute(block, ("h", "tp"), turn)
            both = in_order([mine, swap(mine, "tp")], it)
            return [jnp.stack([b[n] for b in both])[:, None] for n in range(block.shape[0])]

    def gather_half(name, block, *others):
        with jax.named_scope(name):
            sent = jnp.broadcast_to(block[None], (J, *block.shape))
            if others:
                sent = after(sent, *others)
            return lax.all_to_all(sent, "j", 0, 0).reshape(side, d_model)

    def sum_tokens(name, half, *others):
        with jax.named_scope(name):
            got = lax.all_to_all(half.reshape(J, rows, d_model), "j", 0, 0)
            if others:
                got = after(got, *others)
            return jnp.sum(got.astype(F32), 0)

    w_output_t = w_output.T
    w_down_t = w_down.T
    wide = 2 * qw + 2 * HEAD_DIM
    pos = positions[:, 0].reshape(1, H * rows)
    high = pos // 256
    extra = [jnp.concatenate([attn_gain, ffn_gain])[None], high.astype(BF), (pos - high * 256).astype(BF)]
    extra = [jnp.pad(e, ((0, 0), (0, wide - e.shape[1]))) for e in extra]
    extra = jnp.pad(jnp.concatenate(extra, 0), ((0, 5), (0, 0)))
    pack = [
        jnp.concatenate(
            [
                jnp.concatenate(
                    [
                        cut(w_query, p, qw),
                        cut(w_key, p, HEAD_DIM),
                        cut(w_value, p, HEAD_DIM),
                        cut(w_output_t, p, qw),
                    ],
                    1,
                ),
                extra,
            ],
            0,
        )
        for p in range(J)
    ]
    own = exchange("weights_attn", jnp.stack(pack))
    pack = [
        jnp.pad(
            jnp.concatenate([cut(w_gate, p, fw), cut(w_up, p, fw), cut(w_down_t, p, fw)], 1),
            ((0, 0), (0, 2 * ffn_width - 3 * fw)),
        )
        for p in range(J)
    ]
    ffn_own = exchange("weights_ffn", jnp.stack(pack))
    hidden_own = relative(fetch("fetch_hidden", hidden_in))

    def share(name, block):
        with jax.named_scope(name):
            return [block] + [
                lax.ppermute(block, "j", [(i, i ^ d) for i in range(J)]) for d in range(1, J)
            ]

    with jax.named_scope("weights_attn"):
        if B > 1:
            own = lax.all_gather(own, "b", axis=0, tiled=True)
        beside = swap(own, "h")
        opposite = swap(own, "dp")
    half = gather_half("tokens_hidden", hidden_own, ffn_own, beside)
    with jax.named_scope("weights_attn"):
        across = swap(beside, "dp")
    cot_own = relative(fetch("fetch_cot", grad_out, beside))
    with jax.named_scope("weights_attn"):
        parts = [own, beside, opposite, across]
        wa = jnp.stack([p[:, :shard] for p in parts]).reshape(d_model, wide)
        extra = jnp.stack([p[:, shard : shard + 3] for p in parts])
    gains = extra[:, :, 0, : 2 * shard].reshape(4, B * J, 2, shard)
    gains = gains.transpose(2, 0, 1, 3).reshape(2, d_model).astype(F32)
    gain_attn = gains[0]
    gain_ffn = gains[1]
    pos = extra[:2, :, 1:, : H * rows].astype(F32)
    pos = pos[:, :, 0] * 256.0 + pos[:, :, 1]
    pos = lax.dynamic_index_in_dim(pos.reshape(H, B, J, H, rows), ib, 1, keepdims=False)
    pos = jnp.where(ih == 0, pos[:, :, 0], pos[:, :, 1])
    pos = jnp.stack(in_order([pos[0], pos[1]], ih ^ it), 0)
    pos_all = pos.reshape(count)

    place = jnp.arange(T * J, dtype=jnp.int32)
    block_of = (it ^ (place // J)) * (B * J) + place % J
    row_of = jnp.arange(rows, dtype=jnp.int32)
    query_index = ((block_of + ib * J)[:, None] * rows + row_of[None, :]).reshape(count)
    key_index = (
        (block_of[None, :] + jnp.arange(B, dtype=jnp.int32)[:, None] * J)[..., None] * rows + row_of
    ).reshape(B * count)

    inverse = 1.0 / ROPE_BASE ** (jnp.arange(0, HEAD_DIM, 2, dtype=F32) / HEAD_DIM)
    if B == 1:
        inverse = jnp.tile(inverse, 2 * LANES // HEAD_DIM)
    angles = pos_all[:, None] * inverse[None, :]
    cosine = jnp.cos(angles)
    sine = jnp.sin(angles)

    half = after(half, wa, gains, cosine, sine, cot_own)
    with jax.named_scope("weights_ffn"):
        ffn_own = ffn_own.reshape(J * shard, 2 * ffn_width)
        if B > 1:
            ffn_own = lax.all_gather(ffn_own, "b", axis=0, tiled=True)
        w_a = [ffn_own[:, :ffn_width]]
        w_b = [ffn_own[:, ffn_width:]]
        w_a.append(swap(after(w_a[0], half), "h"))
        w_b.append(swap(after(w_b[0], w_a[1]), "h"))
        w_own = swap(after(ffn_own, half), "dp")
    with jax.named_scope("tokens_hidden"):
        hidden = [half, swap(half, "tp")]
    stream = hidden_own.astype(F32)
    valid_length = lax.dynamic_index_in_dim(lengths[:, 0], ih, 0, keepdims=False)

    attn_factor = norm_scale(stream)
    if B == 1:
        at = jnp.stack([valid_length, it])
        ones = jnp.ones((HEAD_DIM,), F32)
        qk_gain = jnp.stack(
            [jnp.concatenate([q_gain, q_gain]).astype(F32), jnp.concatenate([k_gain.astype(F32), ones])]
        )
        *normed, raw, qkv = qkv_call(*hidden, gain_attn[None], wa, qk_gain, cosine, sine)
        mixed, probs = attend_call(at, qkv)
    else:
        hidden = jnp.concatenate(hidden, 0).astype(F32)
        normed = (hidden * norm_scale(hidden) * gain_attn).astype(BF)
        cosine = jnp.concatenate([cosine, cosine], -1)[:, None, :]
        sine = jnp.concatenate([sine, sine], -1)[:, None, :]
        raw = mm(normed, wa[:, : qw + 2 * HEAD_DIM])
        normed = [normed[:side], normed[side:]]
        qk_raw = raw[:, : qw + HEAD_DIM].reshape(count, group + 1, HEAD_DIM)
        qk_gain = jnp.stack([q_gain] * group + [k_gain]).astype(F32)
        qk_factor = norm_scale(qk_raw)
        qk_normed = qk_raw * qk_factor * qk_gain
        qk = (qk_normed * cosine + half_turn(qk_normed) * sine).astype(BF)
        queries = qk[:, :group].transpose(1, 0, 2)
        keys = qk[:, group]
        values = raw[:, qw + HEAD_DIM :].astype(BF)
        if B > 1:
            keys = lax.all_gather(keys, "b", axis=0, tiled=True)
            values = lax.all_gather(values, "b", axis=0, tiled=True)
        visible = (key_index[None, :] <= query_index[:, None]) & (key_index[None, :] < valid_length)

        def scores_of(query_head):
            return jnp.where(visible, mm_nt(query_head, keys) * score_scale, MASKED)

        def attend(query_head):
            scores = scores_of(query_head)
            row_max = jnp.max(scores, -1, keepdims=True)
            exp_scores = jnp.exp(scores - row_max)
            row_total = jnp.sum(exp_scores, -1, keepdims=True)
            probs = (exp_scores / row_total).astype(BF)
            return mm(probs, values).astype(BF), row_max + jnp.log(row_total)

        heads = [attend(queries[g]) for g in range(group)]
        mixed = jnp.concatenate([h[0] for h in heads], -1)
    parts = share("tokens_cot", after(cot_own, half))
    mixed = after(mixed, w_a[1], w_own, *parts[1:])
    with jax.named_scope("tokens_cot"):
        cot_half = jnp.concatenate(in_order(parts, ij), 0)
    with jax.named_scope("sum_attn"):
        wo = wa[:, qw + 2 * HEAD_DIM :]
        low = swap(mm_nt(mixed[side:], wo).astype(BF), "tp")
        low = add(mm_nt(mixed[:side], wo), low)
        w_a.append(swap(w_a[1], "dp"))
        attn_branch = sum_tokens("sum_attn", low, w_b[1], w_a[2])

    middle = stream + attn_branch
    ffn_factor = norm_scale(middle)
    xf_own = (middle * ffn_factor * gain_ffn).astype(BF)
    ffn_half = gather_half("tokens_xf", xf_own)
    with jax.named_scope("weights_ffn"):
        w_b.append(swap(w_b[1], "dp"))
    ffn_half = after(ffn_half, w_b[2])
    ffn_in = [ffn_half, swap(ffn_half, "tp")]
    cot = [cot_half, swap(cot_half, "tp")]
    hidden_act, grad_pre, grad_in, branch = zip(
        *[ffn_call(fw, ffn_in[i], cot[i], w_a, w_b, w_own) for i in range(2)]
    )
    low = swap(grad_in[1], "tp")
    opposite, across_a, across_b = ffn_grad_call(
        2, ffn_width, True, ffn_in, cot, grad_pre, hidden_act
    )
    low = add(grad_in[0], after(low, across_b))
    with jax.named_scope("grads_ffn"):
        got_b, got_a = swap(across_b, "dp"), swap(across_a, "dp")
    near_a, near_b, beside_a, beside_b = ffn_grad_call(
        0, ffn_width, False, ffn_in, cot, grad_pre, hidden_act
    )
    grad_ffn_in = sum_tokens("sum_dxf", low, got_b, near_a)

    grad_middle = cot_own.astype(F32) + norm_back(middle, ffn_factor, gain_ffn, grad_ffn_in)
    with jax.named_scope("grads_ffn"):
        beside_b = add(beside_b, got_b)
    half = gather_half("tokens_dattn", grad_middle.astype(BF), beside_b)
    with jax.named_scope("sum_out"):
        low = add(branch[0], swap(after(branch[1], grad_ffn_in), "tp"))
    with jax.named_scope("grads_ffn"):
        got_b = swap(beside_b, "h")
        beside_a = add(beside_a, got_a)
        half = after(half, low, got_b, beside_a)
        got_a = swap(beside_a, "h")
        opposite = swap(after(opposite, beside_a), "dp")
    grad_attn = [half, swap(half, "tp")]
    with jax.named_scope("sum_out"):
        low = after(low, half).reshape(J, rows, d_model)
        parts = lax.all_to_all(low, "j", 0, 0)
    if B == 1:
        grad_raw, totals = attend_back_call(
            at, qkv, mixed, probs, raw, *grad_attn, wo, qk_gain, cosine, sine
        )
        totals = jnp.concatenate([totals[0, :HEAD_DIM] + totals[0, HEAD_DIM:], totals[1, :HEAD_DIM]])
    else:
        grad_mixed = mm(jnp.concatenate(grad_attn, 0), wo).astype(BF)
        grad_keys = jnp.zeros((B * count, HEAD_DIM), F32)
        grad_values = jnp.zeros((B * count, HEAD_DIM), F32)
        grad_queries = []
        for g in range(group):
            probs = jnp.exp(scores_of(queries[g]) - heads[g][1])
            grad_head = grad_mixed[:, g * HEAD_DIM : (g + 1) * HEAD_DIM]
            grad_probs = mm_nt(grad_head, values)
            row_delta = jnp.sum(grad_probs * probs, -1, keepdims=True)
            grad_scores = (probs * (grad_probs - row_delta)).astype(BF)
            grad_queries.append(mm(grad_scores, keys) * score_scale)
            grad_keys = grad_keys + mm_tn(grad_scores, queries[g]) * score_scale
            grad_values = grad_values + mm_tn(probs.astype(BF), grad_head)
        if B > 1:
            grad_keys = lax.psum_scatter(grad_keys, "b", scatter_dimension=0, tiled=True)
            grad_values = lax.psum_scatter(grad_values, "b", scatter_dimension=0, tiled=True)
        grad_rot = jnp.stack(grad_queries + [grad_keys], 1)
        grad_normed = grad_rot * cosine + half_turn_back(grad_rot * sine)
        grad_qk_raw = norm_back(qk_raw, qk_factor, qk_gain, grad_normed)
        terms = jnp.sum(grad_normed * qk_raw * qk_factor, 0)
        totals = jnp.concatenate([jnp.sum(terms[:group], 0), terms[group]])
        grad_raw = jnp.concatenate(
            [grad_qk_raw.reshape(count, qw + HEAD_DIM), grad_values], 1
        ).astype(BF)
    w_qkv = wa[:, : qw + 2 * HEAD_DIM]
    grad_raw = after(grad_raw, parts, got_a, opposite)
    low = swap(mm_nt(grad_raw[side:], w_qkv).astype(BF), "tp")
    grads_attn = attn_grad_call(normed, grad_attn, grad_raw, mixed)
    low = add(mm_nt(grad_raw[:side], w_qkv), after(low, *grads_attn[2:]))
    grad_normed_own = sum_tokens("sum_dxa", low)
    total = jnp.sum(after(parts, low).astype(F32), 0)
    out_own = relative((middle + total).astype(BF))
    with jax.named_scope("grads_ffn"):
        pieces = [near_a, near_b, got_a, got_b, opposite]
        if B == 1:
            pieces = list(merge_call(ij[None], J, after(near_a, low), *pieces[1:]))
        else:
            near = jnp.concatenate([add(near_a, got_a), add(near_b, got_b)], 1)
            near = lax.psum_scatter(add(near, opposite), "b", scatter_dimension=0, tiled=True)
            near = near.reshape(J, shard, 2 * ffn_width)
            pieces = [lax.dynamic_index_in_dim(near, ij ^ d, 0, keepdims=False) for d in range(J)]
        for d in range(1, J):
            pieces[d] = lax.ppermute(pieces[d], "j", [(i, i ^ d) for i in range(J)])
    grad_stream = grad_middle + norm_back(stream, attn_factor, gain_attn, grad_normed_own)
    sent = jnp.stack([out_own, relative(grad_stream.astype(BF))])
    out_hidden, grad_hidden = give_back("return", sent)
    with jax.named_scope("grads_attn"):
        totals = jnp.pad(totals[None], ((0, 0), (0, wide - 2 * HEAD_DIM)))
        near, beside, opposed, across = grads_attn
        got = swap(jnp.concatenate([across, two_numbers(totals)], 0), "dp")
        got_near = swap(opposed, "dp")
        got = after(got, low)
        totals = totals + one_number(got[part:])
        beside = jnp.concatenate([add(beside, got[:part]), two_numbers(totals)], 0)
        got = swap(beside, "h")
        totals = totals + one_number(got[part:])
    with jax.named_scope("grads"):
        got = after(got, grad_normed_own)
        near = add(near.astype(F32) + got_near.astype(F32), got[:part])
        extra = two_numbers(totals[:, :LANES])
        extra = jnp.pad(extra, ((0, shard - extra.shape[0]), (0, 0)))
        extra = jnp.broadcast_to(extra[None], (B * J, shard, LANES))
        near = jnp.concatenate([near.reshape(B * J, shard, near.shape[1]), extra], 2)
        if B > 1:
            near = lax.psum_scatter(near, "b", scatter_dimension=0, tiled=True)
        shards = lax.all_to_all(near, "j", 0, 0)
    totals = jnp.sum(one_number(shards[:, :, -LANES:]), (0, 1))
    *shard_grads, sums = final_call(qw, fw, ij[None], shards, pieces, w_query, w_key, w_value, w_gate, w_up)

    sums = jnp.concatenate([totals, sums[:, 0], sums[:, 1]])
    sums = sums + swap(sums, "tp")
    totals = sums[: 2 * HEAD_DIM].reshape(2, HEAD_DIM)
    sums = sums[2 * HEAD_DIM :].reshape(2, shard) / jnp.stack([attn_gain, ffn_gain]).astype(F32)

    shard_query, shard_key, shard_value, shard_output, shard_gate, shard_up, shard_down = shard_grads
    return (
        out_hidden,
        grad_hidden,
        sums[0],
        shard_query,
        shard_key,
        shard_value,
        totals[0],
        totals[1],
        shard_output.T,
        sums[1],
        shard_gate,
        shard_up,
        shard_down.T,
    )


def solution(mesh):
    places = KV_HEADS // mesh.shape["tp"]

    def run(*args):
        micro = args[0].shape[0]
        shape = (mesh.shape["dp"], micro, mesh.shape["ctx"] // (micro * places), places)
        fine = Mesh(
            mesh.devices.reshape(*shape, mesh.shape["tp"]), ("dp", "h", "b", "j", "tp")
        )
        ctx = ("h", "b", "j")
        rows = ("dp", "h", "b", "j")
        tokens = P(None, "dp", ctx, None)
        return jax.shard_map(
            body,
            mesh=fine,
            in_specs=(
                tokens,
                P(None, "dp"),
                P(None, "dp", ctx),
                P(rows),
                P(rows, "tp"),
                P(rows, "tp"),
                P(rows, "tp"),
                P(),
                P(),
                P("tp", rows),
                P(rows),
                P(rows, "tp"),
                P(rows, "tp"),
                P("tp", rows),
                tokens,
            ),
            out_specs=(
                tokens,
                tokens,
                P(rows),
                P(rows, "tp"),
                P(rows, "tp"),
                P(rows, "tp"),
                P(),
                P(),
                P("tp", rows),
                P(rows),
                P(rows, "tp"),
                P(rows, "tp"),
                P("tp", rows),
            ),
            check_vma=False,
        )(*args)

    return run
```

profile of v0, /device:TPU:0, one launch (start us, length us, event | category | flops | bytes accessed | tf_op | source)
XLA Modules:
  0.0 333.7 jit_solution(7723822991684836849)
XLA Ops:
  5.6 5.2 %all-to-all-start.1 = ((bf16[4,72,384]{2,1,0:T(8,128)(2,1)}), bf16[4,72,384]{2,1,0:T(8,128)(2,1)S(1)}, u32[]{:S(2)}, u32[]{:S(2)}) async-start(bf16[4,72,384]{2,1,0:T(8,128)(2,1)} %pad_maximum_fusion.7), calls=%async_computation.1 | async-start | bytes 442368 | tf_op jit(solution)/shard_map/weights_attn/all_to_all | solution.py:542
  16.2 3.5 %all-to-all-start = ((bf16[4,64,1792]{2,1,0:T(8,128)(2,1)}), bf16[4,64,1792]{2,1,0:T(8,128)(2,1)S(1)}, u32[]{:S(2)}, u32[]{:S(2)}) async-start(bf16[4,64,1792]{2,1,0:T(8,128)(2,1)} %pad_maximum_fusion.1), calls=%async_computation | async-start | bytes 1835008 | tf_op jit(solution)/shard_map/weights_ffn/all_to_all | solution.py:542
  19.7 9.6 %collective-permute-start.1 = (bf16[4,72,384]{2,1,0:T(8,128)(2,1)S(1)}, bf16[4,72,384]{2,1,0:T(8,128)(2,1)S(1)}, u32[]{:S(2)}, u32[]{:S(2)}) collective-permute-start(bf16[4,72,384]{2,1,0:T(8,128)(2,1)S(1)} %all-to-all-done.1), channel_id=1, source_target_pairs={{0,8},{8,0},{1,9},{9,1},{2,10},{10,2},{3,11},{11,3},{4,12},{12,4},... | collective-permute-start | bytes 663560 | tf_op jit(solution)/shard_map/weights_attn/ppermute | solution.py:57
  30.8 6.0 %collective-permute-done.1.refs_2_.refs_1_ = bf16[4,72,384]{2,1,0:T(8,128)(2,1)S(1)} collective-permute-done((bf16[4,72,384]{2,1,0:T(8,128)(2,1)S(1)}, bf16[4,72,384]{2,1,0:T(8,128)(2,1)S(1)}, u32[]{:S(2)}, u32[]{:S(2)}) %collective-permute-start.1) | collective-permute-done | bytes 221216 | tf_op jit(solution)/shard_map/weights_attn/ppermute | solution.py:57
  43.8 6.3 %all-to-all-start.2 = ((bf16[4,128,1024]{2,1,0:T(8,128)(2,1)}), bf16[4,128,1024]{2,1,0:T(8,128)(2,1)S(1)}, u32[]{:S(2)}, u32[]{:S(2)}) async-start(bf16[4,128,1024]{2,1,0:T(8,128)(2,1)} %after.23), calls=%async_computation.2 | async-start | bytes 2097152 | tf_op jit(solution)/shard_map/tokens_hidden/all_to_all | solution.py:584
  50.1 3.1 multiply_sine_fusion
  58.3 6.0 %all-to-all-done.2 = bf16[4,128,1024]{2,1,0:T(8,128)(2,1)S(1)} async-done(((bf16[4,128,1024]{2,1,0:T(8,128)(2,1)}), bf16[4,128,1024]{2,1,0:T(8,128)(2,1)S(1)}, u32[]{:S(2)}, u32[]{:S(2)}) %all-to-all-start.2) | async-done | bytes 1048608 | tf_op jit(solution)/shard_map/tokens_hidden/all_to_all | solution.py:584
  74.8 6.1 %qkv.1 = (bf16[512,1024]{1,0:T(8,128)(2,1)}, bf16[512,1024]{1,0:T(8,128)(2,1)}, f32[1024,256]{1,0:T(8,128)}, bf16[1024,256]{1,0:T(8,128)(2,1)}) custom-call(bf16[512,1024]{1,0:T(8,128)(2,1)} %after.25.h0_ref.refs_1_, bf16[512,1024]{1,0:T(8,128)(2,1)} %collective-permute-done.5.h1_ref, f32[1,1024]{1,0:T(1,128)} %slice.365.gain_ref, ...), custom_call_target="tpu_custom_call" | custom-call | flops 1 | bytes 1 | tf_op jit(solution)/shard_map/qkv/pallas_call | solution.py:155
  80.9 6.3 %attend.1 = (bf16[1024,128]{1,0:T(8,128)(2,1)}, bf16[10,512,256]{2,1,0:T(8,128)(2,1)}) custom-call(s32[2]{0:T(128)} %pad_add_fusion.at_ref, bf16[1024,256]{1,0:T(8,128)(2,1)} %get-tuple-element.52.qkv_ref), custom_call_target="tpu_custom_call" | custom-call | flops 1 | bytes 1 | tf_op jit(solution)/shard_map/attend/pallas_call | solution.py:215
  87.3 7.5 %collective-permute-done.10.refs_5_ = bf16[128,1024]{1,0:T(8,128)(2,1)} collective-permute-done((bf16[128,1024]{1,0:T(8,128)(2,1)}, bf16[128,1024]{1,0:T(8,128)(2,1)}, u32[]{:S(2)}, u32[]{:S(2)}) %collective-permute-start.10) | collective-permute-done | bytes 262176 | tf_op jit(solution)/shard_map/tokens_cot/ppermute | solution.py:633
  102.2 3.6 %all-to-all-start.3 = ((bf16[4,128,1024]{2,1,0:T(8,128)(2,1)}), bf16[4,128,1024]{2,1,0:T(8,128)(2,1)S(1)}, u32[]{:S(2)}, u32[]{:S(2)}) async-start(bf16[4,128,1024]{2,1,0:T(8,128)(2,1)} %bitcast.118), calls=%async_computation.3 | async-start | bytes 2097152 | tf_op jit(solution)/shard_map/sum_attn/sum_attn/all_to_all | solution.py:588
  110.0 17.9 %collective-permute-done.12.refs_1_.refs_4_ = bf16[256,896]{1,0:T(8,128)(2,1)} collective-permute-done((bf16[256,896]{1,0:T(8,128)(2,1)}, bf16[256,896]{1,0:T(8,128)(2,1)}, u32[]{:S(2)}, u32[]{:S(2)}) %collective-permute-start.12) | collective-permute-done | bytes 458784 | tf_op jit(solution)/shard_map/weights_ffn/ppermute | solution.py:57
  133.8 4.6 %all-to-all-start.4 = ((bf16[4,128,1024]{2,1,0:T(8,128)(2,1)}), bf16[4,128,1024]{2,1,0:T(8,128)(2,1)S(1)}, u32[]{:S(2)}, u32[]{:S(2)}) async-start(bf16[4,128,1024]{2,1,0:T(8,128)(2,1)} %broadcast_in_dim.20), calls=%async_computation.4 | async-start | bytes 2097152 | tf_op jit(solution)/shard_map/tokens_xf/all_to_all | solution.py:584
  141.2 8.7 %collective-permute-done.14.refs_1_.refs_5_ = bf16[256,896]{1,0:T(8,128)(2,1)} collective-permute-done((bf16[256,896]{1,0:T(8,128)(2,1)}, bf16[256,896]{1,0:T(8,128)(2,1)}, u32[]{:S(2)}, u32[]{:S(2)}) %collective-permute-start.14) | collective-permute-done | bytes 458784 | tf_op jit(solution)/shard_map/weights_ffn/ppermute | solution.py:57
  156.2 8.6 %ffn.3 = (bf16[512,576]{1,0:T(8,128)(2,1)}, bf16[512,1152]{1,0:T(8,128)(2,1)}, bf16[512,1024]{1,0:T(8,128)(2,1)}, bf16[512,1024]{1,0:T(8,128)(2,1)}) custom-call(bf16[512,1024]{1,0:T(8,128)(2,1)} %copy-done.11, bf16[512,1024]{1,0:T(8,128)(2,1)} %collective-permute-done.16.cot_ref.refs_3_, bf16[256,896]{1,0:T(8,128)(2,1)} %copy-done.18, ...), custom_call_target="tpu_custom_call" | custom-call | flops 1 | bytes 1 | tf_op jit(solution)/shard_map/ffn/pallas_call | solution.py:342
  164.9 8.7 %ffn.2 = (bf16[512,576]{1,0:T(8,128)(2,1)}, bf16[512,1152]{1,0:T(8,128)(2,1)}, bf16[512,1024]{1,0:T(8,128)(2,1)}, bf16[512,1024]{1,0:T(8,128)(2,1)}) custom-call(bf16[512,1024]{1,0:T(8,128)(2,1)} %after.32.x_ref.refs_0_, bf16[512,1024]{1,0:T(8,128)(2,1)} %copy-done.8, bf16[256,896]{1,0:T(8,128)(2,1)} %copy-done.18, bf16[256,896]{1,0:T(8,128)(2,1)} %copy-done.19, ...), custom_call_target="tpu_custom_call" | custom-call | flops 1 | bytes 1 | tf_op jit(solution)/shard_map/ffn/pallas_call | solution.py:342
  173.5 6.5 %ffn_grad.2 = (bf16[256,1792]{1,0:T(8,128)(2,1)}, bf16[256,896]{1,0:T(8,128)(2,1)}, bf16[256,896]{1,0:T(8,128)(2,1)}) custom-call(bf16[512,1024]{1,0:T(8,128)(2,1)} %after.32.x_ref.refs_0_, bf16[512,1024]{1,0:T(8,128)(2,1)} %copy-done.11, bf16[512,1024]{1,0:T(8,128)(2,1)} %copy-done.8, bf16[512,1024]{1,0:T(8,128)(2,1)} %collective-permute-done.16.cot_ref.refs_3_, ...), custom_call_target="tpu_custom_call" | custom-call | flops 1 | bytes 1 | tf_op jit(solution)/shard_map/ffn_grad/pallas_call | solution.py:392
  184.2 3.6 %all-to-all-start.5 = ((bf16[4,128,1024]{2,1,0:T(8,128)(2,1)}), bf16[4,128,1024]{2,1,0:T(8,128)(2,1)S(1)}, u32[]{:S(2)}, u32[]{:S(2)}) async-start(bf16[4,128,1024]{2,1,0:T(8,128)(2,1)} %bitcast.39), calls=%async_computation.5 | async-start | bytes 2097152 | tf_op jit(solution)/shard_map/sum_dxf/all_to_all | solution.py:588
  189.5 6.5 %ffn_grad.3 = (bf16[256,896]{1,0:T(8,128)(2,1)}, bf16[256,896]{1,0:T(8,128)(2,1)}, bf16[256,896]{1,0:T(8,128)(2,1)}, bf16[256,896]{1,0:T(8,128)(2,1)}) custom-call(bf16[512,1024]{1,0:T(8,128)(2,1)} %after.32.x_ref.refs_0_, bf16[512,1024]{1,0:T(8,128)(2,1)} %copy-done.11, bf16[512,1024]{1,0:T(8,128)(2,1)} %copy-done.8, ...), custom_call_target="tpu_custom_call" | custom-call | flops 1 | bytes 1 | tf_op jit(solution)/shard_map/ffn_grad/pallas_call | solution.py:392
  195.9 4.8 %collective-permute-done.18.refs_1_ = bf16[256,896]{1,0:T(8,128)(2,1)S(1)} collective-permute-done((bf16[256,896]{1,0:T(8,128)(2,1)S(1)}, bf16[256,896]{1,0:T(8,128)(2,1)S(1)}, u32[]{:S(2)}, u32[]{:S(2)}) %collective-permute-start.18) | collective-permute-done | bytes 458784 | tf_op jit(solution)/shard_map/grads_ffn/ppermute | solution.py:57
  208.4 3.9 %all-to-all-start.6 = ((bf16[4,128,1024]{2,1,0:T(8,128)(2,1)}), bf16[4,128,1024]{2,1,0:T(8,128)(2,1)S(1)}, u32[]{:S(2)}, u32[]{:S(2)}) async-start(bf16[4,128,1024]{2,1,0:T(8,128)(2,1)} %after.36), calls=%async_computation.6 | async-start | bytes 2097152 | tf_op jit(solution)/shard_map/tokens_dattn/all_to_all | solution.py:584
  215.7 9.8 %collective-permute-done.21 = bf16[256,896]{1,0:T(8,128)(2,1)S(1)} collective-permute-done((bf16[256,896]{1,0:T(8,128)(2,1)}, bf16[256,896]{1,0:T(8,128)(2,1)S(1)}, u32[]{:S(2)}, u32[]{:S(2)}) %collective-permute-start.21) | collective-permute-done | bytes 458784 | tf_op jit(solution)/shard_map/grads_ffn/ppermute | solution.py:57
  228.8 8.5 %collective-permute-done.20.refs_2_.got_b = bf16[256,896]{1,0:T(8,128)(2,1)S(1)} collective-permute-done((bf16[256,896]{1,0:T(8,128)(2,1)S(1)}, bf16[256,896]{1,0:T(8,128)(2,1)S(1)}, u32[]{:S(2)}, u32[]{:S(2)}) %collective-permute-start.20) | collective-permute-done | bytes 458784 | tf_op jit(solution)/shard_map/grads_ffn/ppermute | solution.py:57
  238.4 3.9 %all-to-all-start.7 = ((bf16[4,128,1024]{2,1,0:T(8,128)(2,1)}), bf16[4,128,1024]{2,1,0:T(8,128)(2,1)S(1)}, u32[]{:S(2)}, u32[]{:S(2)}) async-start(bf16[4,128,1024]{2,1,0:T(8,128)(2,1)} %bitcast.115), calls=%async_computation.7 | async-start | bytes 2097152 | tf_op jit(solution)/shard_map/sum_out/all_to_all | solution.py:782
  245.9 11.9 %attend_back.1 = (bf16[1024,256]{1,0:T(8,128)(2,1)}, f32[8,128]{1,0:T(8,128)}) custom-call(s32[2]{0:T(128)} %pad_add_fusion.at_ref, bf16[1024,256]{1,0:T(8,128)(2,1)} %get-tuple-element.52.qkv_ref, bf16[1024,128]{1,0:T(8,128)(2,1)} %after.29.mixed_ref, bf16[10,512,256]{2,1,0:T(8,128)(2,1)} %get-tuple-element.67.probs_ref, ...), custom_call_target="tpu_custom_call" | custom-call | flops 1 | bytes 1 | tf_op jit(solution)/shard_map/attend_back/pallas_call | solution.py:293
  257.8 5.1 %collective-permute-done.23.refs_2_.got_a = bf16[256,896]{1,0:T(8,128)(2,1)S(1)} collective-permute-done((bf16[256,896]{1,0:T(8,128)(2,1)}, bf16[256,896]{1,0:T(8,128)(2,1)S(1)}, u32[]{:S(2)}, u32[]{:S(2)}) %collective-permute-start.23) | collective-permute-done | bytes 458784 | tf_op jit(solution)/shard_map/grads_ffn/ppermute | solution.py:57
  269.9 5.3 %attn_grad.1 = (bf16[256,384]{1,0:T(8,128)(2,1)}, bf16[256,384]{1,0:T(8,128)(2,1)}, bf16[256,384]{1,0:T(8,128)(2,1)}, bf16[256,384]{1,0:T(8,128)(2,1)}) custom-call(bf16[512,1024]{1,0:T(8,128)(2,1)} %get-tuple-element.71.x0_ref, bf16[512,1024]{1,0:T(8,128)(2,1)} %get-tuple-element.72.x1_ref, bf16[512,1024]{1,0:T(8,128)(2,1)} %after.37.refs_1_.g0_ref, ...), custom_call_target="tpu_custom_call" | custom-call | flops 1 | bytes 1 | tf_op jit(solution)/shard_map/attn_grad/pallas_call | solution.py:422
  276.2 3.4 %collective-permute-start.29 = (bf16[264,384]{1,0:T(8,128)(2,1)S(1)}, bf16[264,384]{1,0:T(8,128)(2,1)S(1)}, u32[]{:S(2)}, u32[]{:S(2)}) collective-permute-start(bf16[264,384]{1,0:T(8,128)(2,1)S(1)} %pad_maximum_fusion.8), channel_id=1, source_target_pairs={{0,16},{16,0},{1,17},{17,1},{2,18},{18,2},{3,19},{19,3},{4,20},{20... | collective-permute-start | bytes 608264 | tf_op jit(solution)/shard_map/grads_attn/ppermute | solution.py:57
  283.3 3.6 %all-to-all-start.8 = ((bf16[4,128,1024]{2,1,0:T(8,128)(2,1)}), bf16[4,128,1024]{2,1,0:T(8,128)(2,1)S(1)}, u32[]{:S(2)}, u32[]{:S(2)}) async-start(bf16[4,128,1024]{2,1,0:T(8,128)(2,1)} %bitcast.43), calls=%async_computation.8 | async-start | bytes 2097152 | tf_op jit(solution)/shard_map/sum_dxa/all_to_all | solution.py:588
  309.5 5.7 %all-to-all-start.9 = ((bf16[4,64,512]{2,1,0:T(8,128)(2,1)}), bf16[4,64,512]{2,1,0:T(8,128)(2,1)S(1)}, u32[]{:S(2)}, u32[]{:S(2)}) async-start(bf16[4,64,512]{2,1,0:T(8,128)(2,1)} %pad_maximum_fusion.6), calls=%async_computation.9 | async-start | bytes 524288 | tf_op jit(solution)/shard_map/grads/all_to_all | solution.py:854
  316.5 5.1 %all-to-all-done.9.got_ref = bf16[4,64,512]{2,1,0:T(8,128)(2,1)S(1)} async-done(((bf16[4,64,512]{2,1,0:T(8,128)(2,1)}), bf16[4,64,512]{2,1,0:T(8,128)(2,1)S(1)}, u32[]{:S(2)}, u32[]{:S(2)}) %all-to-all-start.9) | async-done | bytes 262176 | tf_op jit(solution)/shard_map/grads/all_to_all | solution.py:854
  322.3 3.3 final.1
  (352 shorter events, 129.5 us)
Async XLA Ops:
  16.2 26.3 %all-to-all-start = ((bf16[4,64,1792]{2,1,0:T(8,128)(2,1)}), bf16[4,64,1792]{2,1,0:T(8,128)(2,1)S(1)}, u32[]{:S(2)}, u32[]{:S(2)}) async-start(bf16[4,64,1792]{2,1,0:T(8,128)(2,1)} %pad_maximum_fusion.1), calls=%async_computation | async-start | bytes 1835008 | tf_op jit(solution)/shard_map/weights_ffn/all_to_all | solution.py:542
  19.7 17.2 %collective-permute-start.1 = (bf16[4,72,384]{2,1,0:T(8,128)(2,1)S(1)}, bf16[4,72,384]{2,1,0:T(8,128)(2,1)S(1)}, u32[]{:S(2)}, u32[]{:S(2)}) collective-permute-start(bf16[4,72,384]{2,1,0:T(8,128)(2,1)S(1)} %all-to-all-done.1), channel_id=1, source_target_pairs={{0,8},{8,0},{1,9},{9,1},{2,10},{10,2},{3,11},{11,3},{4,12},{12,4},... | collective-permute-start | bytes 663560 | tf_op jit(solution)/shard_map/weights_attn/ppermute | solution.py:57
  29.3 13.1 %collective-permute-start.2 = (bf16[4,72,384]{2,1,0:T(8,128)(2,1)S(1)}, bf16[4,72,384]{2,1,0:T(8,128)(2,1)S(1)}, u32[]{:S(2)}, u32[]{:S(2)}) collective-permute-start(bf16[4,72,384]{2,1,0:T(8,128)(2,1)S(1)} %all-to-all-done.1), channel_id=1, source_target_pairs={{0,16},{16,0},{1,17},{17,1},{2,18},{18,2},{3,19},{19,3},{4,20},{20... | collective-permute-start | bytes 663560 | tf_op jit(solution)/shard_map/weights_attn/ppermute | solution.py:57
  38.3 19.1 %collective-permute-start.4 = (bf16[128,1024]{1,0:T(8,128)(2,1)}, bf16[128,1024]{1,0:T(8,128)(2,1)S(1)}, u32[]{:S(2)}, u32[]{:S(2)}) collective-permute-start(bf16[128,1024]{1,0:T(8,128)(2,1)} %after.24), channel_id=1, source_target_pairs={{0,0},{1,8},{8,1},{9,9},{2,2},{3,10},{10,3},{11,11},{4,4},{5,12},{... | collective-permute-start | bytes 786440 | tf_op jit(solution)/shard_map/fetch_cot/ppermute | solution.py:571
  39.9 14.0 %collective-permute-start.3 = (bf16[4,72,384]{2,1,0:T(8,128)(2,1)}, bf16[4,72,384]{2,1,0:T(8,128)(2,1)}, u32[]{:S(2)}, u32[]{:S(2)}) collective-permute-start(bf16[4,72,384]{2,1,0:T(8,128)(2,1)} %copy-done.33), channel_id=1, source_target_pairs={{0,16},{16,0},{1,17},{17,1},{2,18},{18,2},{3,19},{19,3},{4,20},{20... | collective-permute-start | bytes 663560 | tf_op jit(solution)/shard_map/weights_attn/ppermute | solution.py:57
  43.8 20.5 %all-to-all-start.2 = ((bf16[4,128,1024]{2,1,0:T(8,128)(2,1)}), bf16[4,128,1024]{2,1,0:T(8,128)(2,1)S(1)}, u32[]{:S(2)}, u32[]{:S(2)}) async-start(bf16[4,128,1024]{2,1,0:T(8,128)(2,1)} %after.23), calls=%async_computation.2 | async-start | bytes 2097152 | tf_op jit(solution)/shard_map/tokens_hidden/all_to_all | solution.py:584
  66.6 28.2 %collective-permute-start.7 = (bf16[256,1792]{1,0:T(8,128)(2,1)}, bf16[256,1792]{1,0:T(8,128)(2,1)S(1)}, u32[]{:S(2)}, u32[]{:S(2)}) collective-permute-start(bf16[256,1792]{1,0:T(8,128)(2,1)} %after.27), channel_id=1, source_target_pairs={{0,16},{16,0},{1,17},{17,1},{2,18},{18,2},{3,19},{19,3},{4,20},{20... | collective-permute-start | bytes 2752520 | tf_op jit(solution)/shard_map/weights_ffn/ppermute | solution.py:57
  67.9 26.8 %collective-permute-start.6 = (bf16[256,896]{1,0:T(8,128)(2,1)}, bf16[256,896]{1,0:T(8,128)(2,1)S(1)}, u32[]{:S(2)}, u32[]{:S(2)}) collective-permute-start(bf16[256,896]{1,0:T(8,128)(2,1)} %after.26), channel_id=1, source_target_pairs={{0,8},{8,0},{1,9},{9,1},{2,10},{10,2},{3,11},{11,3},{4,12},{12,4},... | collective-permute-start | bytes 1376264 | tf_op jit(solution)/shard_map/weights_ffn/ppermute | solution.py:57
  69.2 18.0 %collective-permute-start.8 = (bf16[128,1024]{1,0:T(8,128)(2,1)}, bf16[128,1024]{1,0:T(8,128)(2,1)S(1)}, u32[]{:S(2)}, u32[]{:S(2)}) collective-permute-start(bf16[128,1024]{1,0:T(8,128)(2,1)} %after.28), channel_id=1, source_target_pairs={{0,2},{2,0},{4,6},{6,4},{1,3},{3,1},{5,7},{7,5},{8,10},{10,8},{12,... | collective-permute-start | bytes 786440 | tf_op jit(solution)/shard_map/tokens_cot/ppermute | solution.py:633
  70.7 16.6 %collective-permute-start.9 = (bf16[128,1024]{1,0:T(8,128)(2,1)}, bf16[128,1024]{1,0:T(8,128)(2,1)}, u32[]{:S(2)}, u32[]{:S(2)}) collective-permute-start(bf16[128,1024]{1,0:T(8,128)(2,1)} %after.28), channel_id=1, source_target_pairs={{0,4},{2,6},{4,0},{6,2},{1,5},{3,7},{5,1},{7,3},{8,12},{10,14},{12... | collective-permute-start | bytes 786440 | tf_op jit(solution)/shard_map/tokens_cot/ppermute | solution.py:633
  72.4 22.3 %collective-permute-start.10 = (bf16[128,1024]{1,0:T(8,128)(2,1)}, bf16[128,1024]{1,0:T(8,128)(2,1)}, u32[]{:S(2)}, u32[]{:S(2)}) collective-permute-start(bf16[128,1024]{1,0:T(8,128)(2,1)} %after.28), channel_id=1, source_target_pairs={{0,6},{2,4},{4,2},{6,0},{1,7},{3,5},{5,3},{7,1},{8,14},{10,12},{12... | collective-permute-start | bytes 786440 | tf_op jit(solution)/shard_map/tokens_cot/ppermute | solution.py:633
  102.2 27.7 %all-to-all-start.3 = ((bf16[4,128,1024]{2,1,0:T(8,128)(2,1)}), bf16[4,128,1024]{2,1,0:T(8,128)(2,1)S(1)}, u32[]{:S(2)}, u32[]{:S(2)}) async-start(bf16[4,128,1024]{2,1,0:T(8,128)(2,1)} %bitcast.118), calls=%async_computation.3 | async-start | bytes 2097152 | tf_op jit(solution)/shard_map/sum_attn/sum_attn/all_to_all | solution.py:588
  106.7 21.2 %collective-permute-start.12 = (bf16[256,896]{1,0:T(8,128)(2,1)}, bf16[256,896]{1,0:T(8,128)(2,1)}, u32[]{:S(2)}, u32[]{:S(2)}) collective-permute-start(bf16[256,896]{1,0:T(8,128)(2,1)} %after.30), channel_id=1, source_target_pairs={{0,8},{8,0},{1,9},{9,1},{2,10},{10,2},{3,11},{11,3},{4,12},{12,4},... | collective-permute-start | bytes 1376264 | tf_op jit(solution)/shard_map/weights_ffn/ppermute | solution.py:57
  108.5 19.4 %collective-permute-start.13 = (bf16[256,896]{1,0:T(8,128)(2,1)S(1)}, bf16[256,896]{1,0:T(8,128)(2,1)S(1)}, u32[]{:S(2)}, u32[]{:S(2)}) collective-permute-start(bf16[256,896]{1,0:T(8,128)(2,1)S(1)} %copy-done.20), channel_id=1, source_target_pairs={{0,16},{16,0},{1,17},{17,1},{2,18},{18,2},{3,19},{19,3},{4,20},{20... | collective-permute-start | bytes 1376264 | tf_op jit(solution)/shard_map/sum_attn/ppermute | solution.py:57
  133.8 17.5 %all-to-all-start.4 = ((bf16[4,128,1024]{2,1,0:T(8,128)(2,1)}), bf16[4,128,1024]{2,1,0:T(8,128)(2,1)S(1)}, u32[]{:S(2)}, u32[]{:S(2)}) async-start(bf16[4,128,1024]{2,1,0:T(8,128)(2,1)} %broadcast_in_dim.20), calls=%async_computation.4 | async-start | bytes 2097152 | tf_op jit(solution)/shard_map/tokens_xf/all_to_all | solution.py:584
  164.7 15.3 %collective-permute-start.17 = (bf16[512,1024]{1,0:T(8,128)(2,1)}, bf16[512,1024]{1,0:T(8,128)(2,1)S(1)}, u32[]{:S(2)}, u32[]{:S(2)}) collective-permute-start(bf16[512,1024]{1,0:T(8,128)(2,1)} %get-tuple-element.57), channel_id=1, source_target_pairs={{0,1},{1,0},{2,3},{3,2},{4,5},{5,4},{6,7},{7,6},{8,9},{9,8},{10,11... | collective-permute-start | bytes 3145736 | tf_op jit(solution)/shard_map/ppermute | solution.py:57
  184.2 18.6 %all-to-all-start.5 = ((bf16[4,128,1024]{2,1,0:T(8,128)(2,1)}), bf16[4,128,1024]{2,1,0:T(8,128)(2,1)S(1)}, u32[]{:S(2)}, u32[]{:S(2)}) async-start(bf16[4,128,1024]{2,1,0:T(8,128)(2,1)} %bitcast.39), calls=%async_computation.5 | async-start | bytes 2097152 | tf_op jit(solution)/shard_map/sum_dxf/all_to_all | solution.py:588
  187.9 12.9 %collective-permute-start.18 = (bf16[256,896]{1,0:T(8,128)(2,1)S(1)}, bf16[256,896]{1,0:T(8,128)(2,1)S(1)}, u32[]{:S(2)}, u32[]{:S(2)}) collective-permute-start(bf16[256,896]{1,0:T(8,128)(2,1)S(1)} %copy-done.55), channel_id=1, source_target_pairs={{0,16},{16,0},{1,17},{17,1},{2,18},{18,2},{3,19},{19,3},{4,20},{20... | collective-permute-start | bytes 1376264 | tf_op jit(solution)/shard_map/grads_ffn/ppermute | solution.py:57
  208.4 28.9 %all-to-all-start.6 = ((bf16[4,128,1024]{2,1,0:T(8,128)(2,1)}), bf16[4,128,1024]{2,1,0:T(8,128)(2,1)S(1)}, u32[]{:S(2)}, u32[]{:S(2)}) async-start(bf16[4,128,1024]{2,1,0:T(8,128)(2,1)} %after.36), calls=%async_computation.6 | async-start | bytes 2097152 | tf_op jit(solution)/shard_map/tokens_dattn/all_to_all | solution.py:584
  212.4 15.0 %collective-permute-start.19 = (bf16[512,1024]{1,0:T(8,128)(2,1)}, bf16[512,1024]{1,0:T(8,128)(2,1)S(1)}, u32[]{:S(2)}, u32[]{:S(2)}) collective-permute-start(bf16[512,1024]{1,0:T(8,128)(2,1)} %after.35), channel_id=1, source_target_pairs={{0,1},{1,0},{2,3},{3,2},{4,5},{5,4},{6,7},{7,6},{8,9},{9,8},{10,11... | collective-permute-start | bytes 3145736 | tf_op jit(solution)/shard_map/sum_out/ppermute | solution.py:57
  212.4 13.1 %collective-permute-start.21 = (bf16[256,896]{1,0:T(8,128)(2,1)}, bf16[256,896]{1,0:T(8,128)(2,1)S(1)}, u32[]{:S(2)}, u32[]{:S(2)}) collective-permute-start(bf16[256,896]{1,0:T(8,128)(2,1)} %get-tuple-element.66), channel_id=1, source_target_pairs={{0,16},{16,0},{1,17},{17,1},{2,18},{18,2},{3,19},{19,3},{4,20},{20... | collective-permute-start | bytes 1376264 | tf_op jit(solution)/shard_map/grads_ffn/ppermute | solution.py:57
  213.9 23.4 %collective-permute-start.20 = (bf16[256,896]{1,0:T(8,128)(2,1)S(1)}, bf16[256,896]{1,0:T(8,128)(2,1)S(1)}, u32[]{:S(2)}, u32[]{:S(2)}) collective-permute-start(bf16[256,896]{1,0:T(8,128)(2,1)S(1)} %copy-done.34), channel_id=1, source_target_pairs={{0,8},{8,0},{1,9},{9,1},{2,10},{10,2},{3,11},{11,3},{4,12},{12,4},... | collective-permute-start | bytes 1376264 | tf_op jit(solution)/shard_map/grads_ffn/ppermute | solution.py:57
  238.4 27.1 %all-to-all-start.7 = ((bf16[4,128,1024]{2,1,0:T(8,128)(2,1)}), bf16[4,128,1024]{2,1,0:T(8,128)(2,1)S(1)}, u32[]{:S(2)}, u32[]{:S(2)}) async-start(bf16[4,128,1024]{2,1,0:T(8,128)(2,1)} %bitcast.115), calls=%async_computation.7 | async-start | bytes 2097152 | tf_op jit(solution)/shard_map/sum_out/all_to_all | solution.py:782
  242.4 23.1 %collective-permute-start.24 = (bf16[256,1792]{1,0:T(8,128)(2,1)}, bf16[256,1792]{1,0:T(8,128)(2,1)}, u32[]{:S(2)}, u32[]{:S(2)}) collective-permute-start(bf16[256,1792]{1,0:T(8,128)(2,1)} %after.39), channel_id=1, source_target_pairs={{0,16},{16,0},{1,17},{17,1},{2,18},{18,2},{3,19},{19,3},{4,20},{20... | collective-permute-start | bytes 2752520 | tf_op jit(solution)/shard_map/grads_ffn/ppermute | solution.py:57
  242.5 20.4 %collective-permute-start.23 = (bf16[256,896]{1,0:T(8,128)(2,1)}, bf16[256,896]{1,0:T(8,128)(2,1)S(1)}, u32[]{:S(2)}, u32[]{:S(2)}) collective-permute-start(bf16[256,896]{1,0:T(8,128)(2,1)} %add_convert_fusion.4.refs_3_.refs_1_), channel_id=1, source_target_pairs={{0,8},{8,0},{1,9},{9,1},{2,10},{10,2},{3,11},{11,3},{4,12},{12,4},... | collective-permute-start | bytes 1376264 | tf_op jit(solution)/shard_map/grads_ffn/ppermute | solution.py:57
  283.3 23.0 %all-to-all-start.8 = ((bf16[4,128,1024]{2,1,0:T(8,128)(2,1)}), bf16[4,128,1024]{2,1,0:T(8,128)(2,1)S(1)}, u32[]{:S(2)}, u32[]{:S(2)}) async-start(bf16[4,128,1024]{2,1,0:T(8,128)(2,1)} %bitcast.43), calls=%async_computation.8 | async-start | bytes 2097152 | tf_op jit(solution)/shard_map/sum_dxa/all_to_all | solution.py:588
  289.4 14.3 %collective-permute-start.30 = (bf16[264,384]{1,0:T(8,128)(2,1)S(1)}, bf16[264,384]{1,0:T(8,128)(2,1)S(1)}, u32[]{:S(2)}, u32[]{:S(2)}) collective-permute-start(bf16[264,384]{1,0:T(8,128)(2,1)S(1)} %pad_maximum_fusion.9), channel_id=1, source_target_pairs={{0,8},{8,0},{1,9},{9,1},{2,10},{10,2},{3,11},{11,3},{4,12},{12,4},... | collective-permute-start | bytes 608264 | tf_op jit(solution)/shard_map/grads_attn/ppermute | solution.py:57
  292.3 15.0 %collective-permute-start.28 = (bf16[256,384]{1,0:T(8,128)(2,1)}, bf16[256,384]{1,0:T(8,128)(2,1)}, u32[]{:S(2)}, u32[]{:S(2)}) collective-permute-start(bf16[256,384]{1,0:T(8,128)(2,1)} %get-tuple-element.73.refs_1_), channel_id=1, source_target_pairs={{0,16},{16,0},{1,17},{17,1},{2,18},{18,2},{3,19},{19,3},{4,20},{20... | collective-permute-start | bytes 589832 | tf_op jit(solution)/shard_map/grads_attn/ppermute | solution.py:57
  295.7 20.3 %collective-permute-start.31 = (bf16[64,1792]{1,0:T(8,128)(2,1)}, bf16[64,1792]{1,0:T(8,128)(2,1)}, u32[]{:S(2)}, u32[]{:S(2)}) collective-permute-start(bf16[64,1792]{1,0:T(8,128)(2,1)} %get-tuple-element.80), channel_id=1, source_target_pairs={{0,2},{2,0},{4,6},{6,4},{1,3},{3,1},{5,7},{7,5},{8,10},{10,8},{12,... | collective-permute-start | bytes 688136 | tf_op jit(solution)/shard_map/grads_ffn/ppermute | solution.py:831
  297.7 18.3 %collective-permute-start.32 = (bf16[64,1792]{1,0:T(8,128)(2,1)}, bf16[64,1792]{1,0:T(8,128)(2,1)}, u32[]{:S(2)}, u32[]{:S(2)}) collective-permute-start(bf16[64,1792]{1,0:T(8,128)(2,1)} %get-tuple-element.81), channel_id=1, source_target_pairs={{0,4},{2,6},{4,0},{6,2},{1,5},{3,7},{5,1},{7,3},{8,12},{10,14},{12... | collective-permute-start | bytes 688136 | tf_op jit(solution)/shard_map/grads_ffn/ppermute | solution.py:831
  299.2 17.3 %collective-permute-start.33 = (bf16[64,1792]{1,0:T(8,128)(2,1)}, bf16[64,1792]{1,0:T(8,128)(2,1)}, u32[]{:S(2)}, u32[]{:S(2)}) collective-permute-start(bf16[64,1792]{1,0:T(8,128)(2,1)} %get-tuple-element.82), channel_id=1, source_target_pairs={{0,6},{2,4},{4,2},{6,0},{1,7},{3,5},{5,3},{7,1},{8,14},{10,12},{12... | collective-permute-start | bytes 688136 | tf_op jit(solution)/shard_map/grads_ffn/ppermute | solution.py:831
  315.3 13.3 %collective-permute-start.26 = (bf16[2,128,1024]{2,1,0:T(8,128)(2,1)S(1)}, bf16[2,128,1024]{2,1,0:T(8,128)(2,1)S(1)}, u32[]{:S(2)}, u32[]{:S(2)}) collective-permute-start(bf16[2,128,1024]{2,1,0:T(8,128)(2,1)S(1)} %pad_maximum_fusion.3), channel_id=1, source_target_pairs={{0,0},{1,8},{8,1},{9,9},{2,2},{3,10},{10,3},{11,11},{4,4},{5,12},{... | collective-permute-start | bytes 1572872 | tf_op jit(solution)/shard_map/return/ppermute | solution.py:575
  (80 other events, 659.7 us)
where the time goes:
time: 336 us; the launch traced here: 334 us
  waiting for transfers between devices  98.1 us (29%)
  starting transfers between devices  89.5 us (27%)
  Pallas kernels  65.8 us (20%)
  other arithmetic  35.9 us (11%)
  local copies, waits for them, and re-layouts  33.8 us (10%)
  matrix products  8.76 us (3%)
    ppermute x26, waiting for transfers between devices, swap(): return lax.ppermute(v, axis, [(0, 1), (1, 0)])  72.6 us
    ppermute x26, starting transfers between devices, swap(): return lax.ppermute(v, axis, [(0, 1), (1, 0)])  35.3 us
    unnamed x136, local copies, waits for them, and re-layouts  17.4 us
    pallas_call x2, Pallas kernels, ffn_call(): pl.pallas_call(functools.partial(ffn_kernel, fw, part), grid=(count // ti...  17.2 us
    all_to_all x3, starting transfers between devices, gather_half(): return lax.all_to_all(sent, 'j', 0, 0).reshape(side, d_model)  14.8 us
    pallas_call x2, Pallas kernels, ffn_grad_call(): pl.pallas_call(functools.partial(ffn_grad_kernel, fw, width, whole), grid...  12.9 us
    pallas_call x1, Pallas kernels, attend_back_call(): pl.pallas_call(functools.partial(attend_back_kernel, tile, tiles), in_spe...  11.9 us
    all_to_all x3, starting transfers between devices, sum_tokens(): got = lax.all_to_all(half.reshape(J, rows, d_model), 'j', 0, 0)  10.9 us
  transfers between devices with their start and end apart: 45, of which 21 were waited for; matrix products, arithmetic and copies ran while one was open for 12% of the time, Pallas kernels for 17%

commit v1 on v0

--- a/solution.py
+++ b/solution.py
@@ -227,13 +227,15 @@
 
 
 def attend_back_kernel(tile, tiles, at_ref, qkv_ref, mixed_ref, probs_ref, raw_ref, g0_ref, g1_ref,
-                       wo_ref, qk_gain_ref, cos_ref, sin_ref, out_ref, total_ref, dm_ref, dkv_ref):
+                       wa_ref, qk_gain_ref, cos_ref, sin_ref, out_ref, total_ref, give0_ref,
+                       give1_ref, keep_ref, dm_ref, dkv_ref):
     half = tiles // 2
     def place(t):
         return pl.multiple_of((t + half * at_ref[1]) % tiles * tile, tile)
     rows = half * tile
-    dm_ref[:rows] = mm(g0_ref[...], wo_ref[...]).astype(BF)
-    dm_ref[rows:] = mm(g1_ref[...], wo_ref[...]).astype(BF)
+    wide = out_ref.shape[1]
+    dm_ref[:rows] = mm(g0_ref[...], wa_ref[:, wide:]).astype(BF)
+    dm_ref[rows:] = mm(g1_ref[...], wa_ref[:, wide:]).astype(BF)
     scale = HEAD_DIM ** (-0.5)
     lane = lanes((tile, 128))
     low = lane < HEAD_DIM
@@ -283,26 +285,34 @@
         finish(a, 0, jnp.concatenate([grad_query[:tile], grad_query[tile:]], 1))
     for k in range(tiles):
         finish(k, 1, dkv_ref[k])
-
-
-def attend_back_call(at, qkv, mixed, probs, raw, g0, g1, wo, qk_gain, cosine, sine):
-    count = qkv.shape[0]
+    w = wa_ref[:, :wide]
+    middle = rows + rows // 2
+    give0_ref[...] = mm_nt(out_ref[rows:middle], w).astype(BF)
+    give1_ref[...] = mm_nt(out_ref[middle:], w).astype(BF)
+    keep_ref[...] = mm_nt(out_ref[:rows], w).astype(BF)
+
+
+def attend_back_call(at, qkv, mixed, probs, raw, g0, g1, wa, qk_gain, cosine, sine):
+    count, d_model = qkv.shape[0], g0.shape[1]
     tile = min(256, count // 2)
     tiles = count // tile
     vmem = pl.BlockSpec(memory_space=pltpu.VMEM)
     return pl.pallas_call(
         functools.partial(attend_back_kernel, tile, tiles),
         in_specs=[pl.BlockSpec(memory_space=pltpu.SMEM)] + [vmem] * 10,
-        out_specs=[vmem] * 2,
+        out_specs=[vmem] * 5,
         out_shape=[
             jax.ShapeDtypeStruct((count, 256), BF),
             jax.ShapeDtypeStruct((8, 128), F32),
+            jax.ShapeDtypeStruct((count // 4, d_model), BF),
+            jax.ShapeDtypeStruct((count // 4, d_model), BF),
+            jax.ShapeDtypeStruct((count // 2, d_model), BF),
         ],
         scratch_shapes=[pltpu.VMEM((count, 128), BF), pltpu.VMEM((tiles, tile, 128), F32)],
         compiler_params=pltpu.CompilerParams(vmem_limit_bytes=VMEM_BYTES),
         cost_estimate=SMALL_COST,
         name="attend_back",
-    )(at, qkv, mixed, probs, raw, g0, g1, wo, qk_gain, cosine, sine)
+    )(at, qkv, mixed, probs, raw, g0, g1, wa, qk_gain, cosine, sine)
 
 
 def ffn_kernel(fw, part, x_ref, cot_ref, *refs):
@@ -399,6 +409,25 @@
         cost_estimate=SMALL_COST,
         name="ffn_grad",
     )(*x, *cot, *grad, *act)
+
+
+def add_kernel(keep_ref, got0_ref, got1_ref, out_ref):
+    rows = got0_ref.shape[0]
+    out_ref[:rows] = (keep_ref[:rows].astype(F32) + got0_ref[...].astype(F32)).astype(BF)
+    out_ref[rows:] = (keep_ref[rows:].astype(F32) + got1_ref[...].astype(F32)).astype(BF)
+
+
+def add_call(keep, got0, got1):
+    vmem = pl.BlockSpec(memory_space=pltpu.VMEM)
+    return pl.pallas_call(
+        add_kernel,
+        in_specs=[vmem] * 3,
+        out_specs=vmem,
+        out_shape=jax.ShapeDtypeStruct(keep.shape, BF),
+        compiler_params=pltpu.CompilerParams(vmem_limit_bytes=VMEM_BYTES),
+        cost_estimate=SMALL_COST,
+        name="add",
+    )(keep, got0, got1)
 
 
 def attn_grad_kernel(x0_ref, x1_ref, g0_ref, g1_ref, raw_ref, mixed_ref, *outs):
@@ -638,7 +667,7 @@
             own = lax.all_gather(own, "b", axis=0, tiled=True)
         beside = swap(own, "h")
         opposite = swap(own, "dp")
-    half = gather_half("tokens_hidden", hidden_own, ffn_own, beside)
+    half = gather_half("tokens_hidden", hidden_own, ffn_own)
     with jax.named_scope("weights_attn"):
         across = swap(beside, "dp")
     cot_own = relative(fetch("fetch_cot", grad_out, beside))
@@ -672,7 +701,13 @@
     cosine = jnp.cos(angles)
     sine = jnp.sin(angles)
 
-    half = after(half, wa, gains, cosine, sine, cot_own)
+    valid_length = lax.dynamic_index_in_dim(lengths[:, 0], ih, 0, keepdims=False)
+    at = jnp.stack([valid_length, it])
+    ones = jnp.ones((HEAD_DIM,), F32)
+    qk_gain = jnp.stack(
+        [jnp.concatenate([q_gain, q_gain]).astype(F32), jnp.concatenate([k_gain.astype(F32), ones])]
+    )
+    half = after(half, wa, gains, cosine, sine, cot_own, at, qk_gain)
     with jax.named_scope("weights_ffn"):
         ffn_own = ffn_own.reshape(J * shard, 2 * ffn_width)
         if B > 1:
@@ -685,15 +720,9 @@
     with jax.named_scope("tokens_hidden"):
         hidden = [half, swap(half, "tp")]
     stream = hidden_own.astype(F32)
-    valid_length = lax.dynamic_index_in_dim(lengths[:, 0], ih, 0, keepdims=False)
 
     attn_factor = norm_scale(stream)
     if B == 1:
-        at = jnp.stack([valid_length, it])
-        ones = jnp.ones((HEAD_DIM,), F32)
-        qk_gain = jnp.stack(
-            [jnp.concatenate([q_gain, q_gain]).astype(F32), jnp.concatenate([k_gain.astype(F32), ones])]
-        )
         *normed, raw, qkv = qkv_call(*hidden, gain_attn[None], wa, qk_gain, cosine, sine)
         mixed, probs = attend_call(at, qkv)
     else:
@@ -738,9 +767,10 @@
         low = swap(mm_nt(mixed[side:], wo).astype(BF), "tp")
         low = add(mm_nt(mixed[:side], wo), low)
         w_a.append(swap(w_a[1], "dp"))
-        attn_branch = sum_tokens("sum_attn", low, w_b[1], w_a[2])
+        attn_branch = sum_tokens("sum_attn", low)
 
     middle = stream + attn_branch
+    gain_ffn = after(gain_ffn, w_b[1], w_a[2])
     ffn_factor = norm_scale(middle)
     xf_own = (middle * ffn_factor * gain_ffn).astype(BF)
     ffn_half = gather_half("tokens_xf", xf_own)
@@ -749,9 +779,9 @@
     ffn_half = after(ffn_half, w_b[2])
     ffn_in = [ffn_half, swap(ffn_half, "tp")]
     cot = [cot_half, swap(cot_half, "tp")]
-    hidden_act, grad_pre, grad_in, branch = zip(
-        *[ffn_call(fw, ffn_in[i], cot[i], w_a, w_b, w_own) for i in range(2)]
-    )
+    first = ffn_call(fw, ffn_in[0], cot[0], w_a, w_b, w_own)
+    second = ffn_call(fw, after(ffn_in[1], first[0]), cot[1], w_a, w_b, w_own)
+    hidden_act, grad_pre, grad_in, branch = zip(first, second)
     low = swap(grad_in[1], "tp")
     opposite, across_a, across_b = ffn_grad_call(
         2, ffn_width, True, ffn_in, cot, grad_pre, hidden_act
@@ -762,27 +792,28 @@
     near_a, near_b, beside_a, beside_b = ffn_grad_call(
         0, ffn_width, False, ffn_in, cot, grad_pre, hidden_act
     )
-    grad_ffn_in = sum_tokens("sum_dxf", low, got_b, near_a)
+    grad_ffn_in = sum_tokens("sum_dxf", low)
+    gain_ffn = after(gain_ffn, got_b, near_a)
 
     grad_middle = cot_own.astype(F32) + norm_back(middle, ffn_factor, gain_ffn, grad_ffn_in)
     with jax.named_scope("grads_ffn"):
         beside_b = add(beside_b, got_b)
     half = gather_half("tokens_dattn", grad_middle.astype(BF), beside_b)
     with jax.named_scope("sum_out"):
-        low = add(branch[0], swap(after(branch[1], grad_ffn_in), "tp"))
+        low = swap(after(branch[1], grad_ffn_in), "tp")
+        low = add(branch[0], low)
     with jax.named_scope("grads_ffn"):
         got_b = swap(beside_b, "h")
         beside_a = add(beside_a, got_a)
         half = after(half, low, got_b, beside_a)
         got_a = swap(beside_a, "h")
-        opposite = swap(after(opposite, beside_a), "dp")
+        opposite = swap(after(opposite, half), "dp")
     grad_attn = [half, swap(half, "tp")]
     with jax.named_scope("sum_out"):
-        low = after(low, half).reshape(J, rows, d_model)
-        parts = lax.all_to_all(low, "j", 0, 0)
+        parts = lax.all_to_all(after(low, half).reshape(J, rows, d_model), "j", 0, 0)
     if B == 1:
-        grad_raw, totals = attend_back_call(
-            at, qkv, mixed, probs, raw, *grad_attn, wo, qk_gain, cosine, sine
+        grad_raw, totals, *gives, keep = attend_back_call(
+            at, qkv, mixed, probs, raw, *grad_attn, wa, qk_gain, cosine, sine
         )
         totals = jnp.concatenate([totals[0, :HEAD_DIM] + totals[0, HEAD_DIM:], totals[1, :HEAD_DIM]])
     else:
@@ -810,11 +841,16 @@
         grad_raw = jnp.concatenate(
             [grad_qk_raw.reshape(count, qw + HEAD_DIM), grad_values], 1
         ).astype(BF)
-    w_qkv = wa[:, : qw + 2 * HEAD_DIM]
-    grad_raw = after(grad_raw, parts, got_a, opposite)
-    low = swap(mm_nt(grad_raw[side:], w_qkv).astype(BF), "tp")
+    if B > 1:
+        w_qkv = wa[:, : qw + 2 * HEAD_DIM]
+        gives = [mm_nt(g, w_qkv).astype(BF) for g in jnp.split(grad_raw[side:], 2)]
+        keep = mm_nt(grad_raw[:side], w_qkv).astype(BF)
+    grad_raw = after(grad_raw, got_a)
+    gives = [swap(after(g, grad_raw), "tp") for g in gives]
     grads_attn = attn_grad_call(normed, grad_attn, grad_raw, mixed)
-    low = add(mm_nt(grad_raw[:side], w_qkv), after(low, *grads_attn[2:]))
+    gives[0] = after(gives[0], parts, *grads_attn[2:])
+    gives[1] = after(gives[1], opposite)
+    low = add_call(keep, *gives)
     grad_normed_own = sum_tokens("sum_dxa", low)
     total = jnp.sum(after(parts, low).astype(F32), 0)
     out_own = relative((middle + total).astype(BF))

time: 336 us -> 332 us (0.988)
  matrix products: 8.76 us -> 3.69 us
    ppermute x26 -> x27, starting transfers between devices: 35.3 us -> 29.6 us  [swap(): return lax.ppermute(v, axis, [(0, 1), (1, 0)])]
    dot_general x4 -> x2, matrix products: 8.76 us -> 3.69 us  [dot(): return lax.dot_general(a, b, (dims, ((), ())), preferred_element_type=F32)]
    ppermute x26 -> x27, waiting for transfers between devices: 72.6 us -> 75.2 us  [swap(): return lax.ppermute(v, axis, [(0, 1), (1, 0)])]
    unnamed x136 -> x155, local copies, waits for them, and re-layouts: 17.4 us -> 17.7 us
  transfers between devices with their start and end apart: 45 -> 46, of which waited for: 21 -> 19; matrix products, arithmetic and copies ran while one was open for 12% -> 12% of each run, Pallas kernels for 17% -> 18%
where the time goes in v1:
time: 332 us; the launch traced here: 329 us
  waiting for transfers between devices  98.1 us (30%)
  starting transfers between devices  86.9 us (26%)
  Pallas kernels  68.4 us (21%)
  other arithmetic  35.7 us (11%)
  local copies, waits for them, and re-layouts  34.8 us (10%)
  matrix products  3.69 us (1%)
    ppermute x27, waiting for transfers between devices, swap(): return lax.ppermute(v, axis, [(0, 1), (1, 0)])  75.2 us
    ppermute x27, starting transfers between devices, swap(): return lax.ppermute(v, axis, [(0, 1), (1, 0)])  29.6 us
    unnamed x155, local copies, waits for them, and re-layouts  17.7 us
    pallas_call x2, Pallas kernels, ffn_call(): pl.pallas_call(functools.partial(ffn_kernel, fw, part), grid=(count // ti...  17.2 us
    all_to_all x3, starting transfers between devices, gather_half(): return lax.all_to_all(sent, 'j', 0, 0).reshape(side, d_model)  15.9 us
    all_to_all x3, starting transfers between devices, sum_tokens(): got = lax.all_to_all(half.reshape(J, rows, d_model), 'j', 0, 0)  13.2 us
    pallas_call x2, Pallas kernels, ffn_grad_call(): pl.pallas_call(functools.partial(ffn_grad_kernel, fw, width, whole), grid...  12.9 us
    pallas_call x1, Pallas kernels, attend_back_call(): pl.pallas_call(functools.partial(attend_back_kernel, tile, tiles), in_spe...  11.7 us
  transfers between devices with their start and end apart: 46, of which 19 were waited for; matrix products, arithmetic and copies ran while one was open for 12% of the time, Pallas kernels for 18%

profile of v1, /device:TPU:0, one launch (start us, length us, event | category | flops | bytes accessed | tf_op | source)
XLA Modules:
  0.0 329.4 jit_solution(2580788350135866024)
XLA Ops:
  5.7 5.2 %all-to-all-start.2 = ((bf16[4,72,384]{2,1,0:T(8,128)(2,1)}), bf16[4,72,384]{2,1,0:T(8,128)(2,1)S(1)}, u32[]{:S(2)}, u32[]{:S(2)}) async-start(bf16[4,72,384]{2,1,0:T(8,128)(2,1)} %pad_maximum_fusion.7), calls=%async_computation.2 | async-start | bytes 442368 | tf_op jit(solution)/shard_map/weights_attn/all_to_all | solution.py:571
  17.1 4.2 %all-to-all-start = ((bf16[4,64,1792]{2,1,0:T(8,128)(2,1)}), bf16[4,64,1792]{2,1,0:T(8,128)(2,1)S(1)}, u32[]{:S(2)}, u32[]{:S(2)}) async-start(bf16[4,64,1792]{2,1,0:T(8,128)(2,1)} %pad_maximum_fusion.1), calls=%async_computation | async-start | bytes 1835008 | tf_op jit(solution)/shard_map/weights_ffn/all_to_all | solution.py:571
  22.9 8.0 %collective-permute-start.1 = (bf16[4,72,384]{2,1,0:T(8,128)(2,1)S(1)}, bf16[4,72,384]{2,1,0:T(8,128)(2,1)S(1)}, u32[]{:S(2)}, u32[]{:S(2)}) collective-permute-start(bf16[4,72,384]{2,1,0:T(8,128)(2,1)S(1)} %all-to-all-done.2), channel_id=1, source_target_pairs={{0,8},{8,0},{1,9},{9,1},{2,10},{10,2},{3,11},{11,3},{4,12},{12,4},... | collective-permute-start | bytes 663560 | tf_op jit(solution)/shard_map/weights_attn/ppermute | solution.py:57
  30.9 7.2 %collective-permute-done.1.refs_1_ = bf16[4,72,384]{2,1,0:T(8,128)(2,1)S(1)} collective-permute-done((bf16[4,72,384]{2,1,0:T(8,128)(2,1)S(1)}, bf16[4,72,384]{2,1,0:T(8,128)(2,1)S(1)}, u32[]{:S(2)}, u32[]{:S(2)}) %collective-permute-start.1) | collective-permute-done | bytes 221216 | tf_op jit(solution)/shard_map/weights_attn/ppermute | solution.py:57
  44.2 6.4 %all-to-all-start.1 = ((bf16[4,128,1024]{2,1,0:T(8,128)(2,1)}), bf16[4,128,1024]{2,1,0:T(8,128)(2,1)S(1)}, u32[]{:S(2)}, u32[]{:S(2)}) async-start(bf16[4,128,1024]{2,1,0:T(8,128)(2,1)} %after.27), calls=%async_computation.1 | async-start | bytes 2097152 | tf_op jit(solution)/shard_map/tokens_hidden/all_to_all | solution.py:613
  50.6 3.1 multiply_sine_fusion
  58.8 5.8 %all-to-all-done.1 = bf16[4,128,1024]{2,1,0:T(8,128)(2,1)S(1)} async-done(((bf16[4,128,1024]{2,1,0:T(8,128)(2,1)}), bf16[4,128,1024]{2,1,0:T(8,128)(2,1)S(1)}, u32[]{:S(2)}, u32[]{:S(2)}) %all-to-all-start.1) | async-done | bytes 1048608 | tf_op jit(solution)/shard_map/tokens_hidden/all_to_all | solution.py:613
  73.7 6.1 %qkv.1 = (bf16[512,1024]{1,0:T(8,128)(2,1)}, bf16[512,1024]{1,0:T(8,128)(2,1)}, f32[1024,256]{1,0:T(8,128)}, bf16[1024,256]{1,0:T(8,128)(2,1)}) custom-call(bf16[512,1024]{1,0:T(8,128)(2,1)} %after.29.h0_ref.refs_1_, bf16[512,1024]{1,0:T(8,128)(2,1)} %collective-permute-done.5.h1_ref, f32[1,1024]{1,0:T(1,128)} %slice.354.gain_ref, ...), custom_call_target="tpu_custom_call" | custom-call | flops 1 | bytes 1 | tf_op jit(solution)/shard_map/qkv/pallas_call | solution.py:155
  79.8 6.3 %attend.1 = (bf16[1024,128]{1,0:T(8,128)(2,1)}, bf16[10,512,256]{2,1,0:T(8,128)(2,1)}) custom-call(s32[2]{0:T(128)} %pad_add_fusion.refs_6_.at_ref, bf16[1024,256]{1,0:T(8,128)(2,1)} %get-tuple-element.55.qkv_ref), custom_call_target="tpu_custom_call" | custom-call | flops 1 | bytes 1 | tf_op jit(solution)/shard_map/attend/pallas_call | solution.py:215
  86.1 8.4 %collective-permute-done.9.refs_4_ = bf16[128,1024]{1,0:T(8,128)(2,1)S(1)} collective-permute-done((bf16[128,1024]{1,0:T(8,128)(2,1)}, bf16[128,1024]{1,0:T(8,128)(2,1)S(1)}, u32[]{:S(2)}, u32[]{:S(2)}) %collective-permute-start.9) | collective-permute-done | bytes 262176 | tf_op jit(solution)/shard_map/tokens_cot/ppermute | solution.py:662
  102.2 3.6 %all-to-all-start.3 = ((bf16[4,128,1024]{2,1,0:T(8,128)(2,1)}), bf16[4,128,1024]{2,1,0:T(8,128)(2,1)S(1)}, u32[]{:S(2)}, u32[]{:S(2)}) async-start(bf16[4,128,1024]{2,1,0:T(8,128)(2,1)} %bitcast.117), calls=%async_computation.3 | async-start | bytes 2097152 | tf_op jit(solution)/shard_map/sum_attn/sum_attn/all_to_all | solution.py:617
  109.6 18.2 %collective-permute-done.12.refs_1_.refs_4_ = bf16[256,896]{1,0:T(8,128)(2,1)S(1)} collective-permute-done((bf16[256,896]{1,0:T(8,128)(2,1)}, bf16[256,896]{1,0:T(8,128)(2,1)S(1)}, u32[]{:S(2)}, u32[]{:S(2)}) %collective-permute-start.12) | collective-permute-done | bytes 458784 | tf_op jit(solution)/shard_map/weights_ffn/ppermute | solution.py:57
  131.5 5.6 %all-to-all-start.4 = ((bf16[4,128,1024]{2,1,0:T(8,128)(2,1)}), bf16[4,128,1024]{2,1,0:T(8,128)(2,1)S(1)}, u32[]{:S(2)}, u32[]{:S(2)}) async-start(bf16[4,128,1024]{2,1,0:T(8,128)(2,1)} %broadcast_in_dim.20), calls=%async_computation.4 | async-start | bytes 2097152 | tf_op jit(solution)/shard_map/tokens_xf/all_to_all | solution.py:613
  139.9 8.7 %collective-permute-done.14.refs_1_.refs_5_ = bf16[256,896]{1,0:T(8,128)(2,1)S(1)} collective-permute-done((bf16[256,896]{1,0:T(8,128)(2,1)S(1)}, bf16[256,896]{1,0:T(8,128)(2,1)S(1)}, u32[]{:S(2)}, u32[]{:S(2)}) %collective-permute-start.14) | collective-permute-done | bytes 458784 | tf_op jit(solution)/shard_map/weights_ffn/ppermute | solution.py:57
  153.5 8.6 %ffn.2 = (bf16[512,576]{1,0:T(8,128)(2,1)}, bf16[512,1152]{1,0:T(8,128)(2,1)}, bf16[512,1024]{1,0:T(8,128)(2,1)}, bf16[512,1024]{1,0:T(8,128)(2,1)}) custom-call(bf16[512,1024]{1,0:T(8,128)(2,1)} %after.36.x_ref.refs_0_, bf16[512,1024]{1,0:T(8,128)(2,1)} %copy-done.7, bf16[256,896]{1,0:T(8,128)(2,1)} %copy-done.14, bf16[256,896]{1,0:T(8,128)(2,1)} %copy-done.16, ...), custom_call_target="tpu_custom_call" | custom-call | flops 1 | bytes 1 | tf_op jit(solution)/shard_map/ffn/pallas_call | solution.py:352
  163.4 8.7 %ffn.3 = (bf16[512,576]{1,0:T(8,128)(2,1)}, bf16[512,1152]{1,0:T(8,128)(2,1)}, bf16[512,1024]{1,0:T(8,128)(2,1)}, bf16[512,1024]{1,0:T(8,128)(2,1)}) custom-call(bf16[512,1024]{1,0:T(8,128)(2,1)} %after.37.x_ref, bf16[512,1024]{1,0:T(8,128)(2,1)} %collective-permute-done.16.cot_ref.refs_3_, bf16[256,896]{1,0:T(8,128)(2,1)} %copy-done.14, ...), custom_call_target="tpu_custom_call" | custom-call | flops 1 | bytes 1 | tf_op jit(solution)/shard_map/ffn/pallas_call | solution.py:352
  172.6 6.5 %ffn_grad.2 = (bf16[256,1792]{1,0:T(8,128)(2,1)}, bf16[256,896]{1,0:T(8,128)(2,1)}, bf16[256,896]{1,0:T(8,128)(2,1)}) custom-call(bf16[512,1024]{1,0:T(8,128)(2,1)} %after.36.x_ref.refs_0_, bf16[512,1024]{1,0:T(8,128)(2,1)} %copy-done.10, bf16[512,1024]{1,0:T(8,128)(2,1)} %copy-done.7, bf16[512,1024]{1,0:T(8,128)(2,1)} %collective-permute-done.16.cot_ref.refs_3_, ...), custom_call_target="tpu_custom_call" | custom-call | flops 1 | bytes 1 | tf_op jit(solution)/shard_map/ffn_grad/pallas_call | solution.py:402
  183.3 3.5 %all-to-all-start.5 = ((bf16[4,128,1024]{2,1,0:T(8,128)(2,1)}), bf16[4,128,1024]{2,1,0:T(8,128)(2,1)S(1)}, u32[]{:S(2)}, u32[]{:S(2)}) async-start(bf16[4,128,1024]{2,1,0:T(8,128)(2,1)} %bitcast.39), calls=%async_computation.5 | async-start | bytes 2097152 | tf_op jit(solution)/shard_map/sum_dxf/all_to_all | solution.py:617
  187.5 6.5 %ffn_grad.3 = (bf16[256,896]{1,0:T(8,128)(2,1)}, bf16[256,896]{1,0:T(8,128)(2,1)}, bf16[256,896]{1,0:T(8,128)(2,1)}, bf16[256,896]{1,0:T(8,128)(2,1)}) custom-call(bf16[512,1024]{1,0:T(8,128)(2,1)} %after.36.x_ref.refs_0_, bf16[512,1024]{1,0:T(8,128)(2,1)} %copy-done.10, bf16[512,1024]{1,0:T(8,128)(2,1)} %copy-done.7, ...), custom_call_target="tpu_custom_call" | custom-call | flops 1 | bytes 1 | tf_op jit(solution)/shard_map/ffn_grad/pallas_call | solution.py:402
  194.0 5.4 %collective-permute-done.19.refs_1_ = bf16[256,896]{1,0:T(8,128)(2,1)S(1)} collective-permute-done((bf16[256,896]{1,0:T(8,128)(2,1)S(1)}, bf16[256,896]{1,0:T(8,128)(2,1)S(1)}, u32[]{:S(2)}, u32[]{:S(2)}) %collective-permute-start.19) | collective-permute-done | bytes 458784 | tf_op jit(solution)/shard_map/grads_ffn/ppermute | solution.py:57
  204.9 3.9 %all-to-all-start.6 = ((bf16[4,128,1024]{2,1,0:T(8,128)(2,1)}), bf16[4,128,1024]{2,1,0:T(8,128)(2,1)S(1)}, u32[]{:S(2)}, u32[]{:S(2)}) async-start(bf16[4,128,1024]{2,1,0:T(8,128)(2,1)} %after.41), calls=%async_computation.6 | async-start | bytes 2097152 | tf_op jit(solution)/shard_map/tokens_dattn/all_to_all | solution.py:613
  211.0 11.0 %collective-permute-done.21 = bf16[256,896]{1,0:T(8,128)(2,1)S(1)} collective-permute-done((bf16[256,896]{1,0:T(8,128)(2,1)}, bf16[256,896]{1,0:T(8,128)(2,1)S(1)}, u32[]{:S(2)}, u32[]{:S(2)}) %collective-permute-start.21) | collective-permute-done | bytes 458784 | tf_op jit(solution)/shard_map/grads_ffn/ppermute | solution.py:57
  225.4 7.4 %collective-permute-done.20.refs_2_.got_b = bf16[256,896]{1,0:T(8,128)(2,1)S(1)} collective-permute-done((bf16[256,896]{1,0:T(8,128)(2,1)S(1)}, bf16[256,896]{1,0:T(8,128)(2,1)S(1)}, u32[]{:S(2)}, u32[]{:S(2)}) %collective-permute-start.20) | collective-permute-done | bytes 458784 | tf_op jit(solution)/shard_map/grads_ffn/ppermute | solution.py:57
  234.0 3.7 %all-to-all-start.7 = ((bf16[4,128,1024]{2,1,0:T(8,128)(2,1)}), bf16[4,128,1024]{2,1,0:T(8,128)(2,1)S(1)}, u32[]{:S(2)}, u32[]{:S(2)}) async-start(bf16[4,128,1024]{2,1,0:T(8,128)(2,1)} %bitcast.114), calls=%async_computation.7 | async-start | bytes 2097152 | tf_op jit(solution)/shard_map/sum_out/all_to_all | solution.py:813
  242.1 11.7 %attend_back.1 = (bf16[1024,256]{1,0:T(8,128)(2,1)}, f32[8,128]{1,0:T(8,128)}, bf16[256,1024]{1,0:T(8,128)(2,1)}, bf16[256,1024]{1,0:T(8,128)(2,1)}, bf16[512,1024]{1,0:T(8,128)(2,1)}) custom-call(s32[2]{0:T(128)} %pad_add_fusion.refs_6_.at_ref, bf16[1024,256]{1,0:T(8,128)(2,1)} %get-tuple-element.55.qkv_ref, bf16[1024,128]{1,0:T(8,128)(2,1)} %after.33.mixed_ref, ...), custom_call_target="tpu_custom_call" | custom-call | flops 1 | bytes 1 | tf_op jit(solution)/shard_map/attend_back/pallas_call | solution.py:300
  253.8 6.3 %collective-permute-done.23.refs_1_.got_a = bf16[256,896]{1,0:T(8,128)(2,1)S(1)} collective-permute-done((bf16[256,896]{1,0:T(8,128)(2,1)}, bf16[256,896]{1,0:T(8,128)(2,1)S(1)}, u32[]{:S(2)}, u32[]{:S(2)}) %collective-permute-start.23) | collective-permute-done | bytes 458784 | tf_op jit(solution)/shard_map/grads_ffn/ppermute | solution.py:57
  261.4 5.3 %attn_grad.1 = (bf16[256,384]{1,0:T(8,128)(2,1)}, bf16[256,384]{1,0:T(8,128)(2,1)}, bf16[256,384]{1,0:T(8,128)(2,1)}, bf16[256,384]{1,0:T(8,128)(2,1)}) custom-call(bf16[512,1024]{1,0:T(8,128)(2,1)} %get-tuple-element.75.x0_ref, bf16[512,1024]{1,0:T(8,128)(2,1)} %get-tuple-element.76.x1_ref, bf16[512,1024]{1,0:T(8,128)(2,1)} %after.42.refs_1_.g0_ref, ...), custom_call_target="tpu_custom_call" | custom-call | flops 1 | bytes 1 | tf_op jit(solution)/shard_map/attn_grad/pallas_call | solution.py:451
  277.2 6.0 %all-to-all-start.8 = ((bf16[4,128,1024]{2,1,0:T(8,128)(2,1)}), bf16[4,128,1024]{2,1,0:T(8,128)(2,1)S(1)}, u32[]{:S(2)}, u32[]{:S(2)}) async-start(bf16[4,128,1024]{2,1,0:T(8,128)(2,1)} %bitcast.107), calls=%async_computation.8 | async-start | bytes 2097152 | tf_op jit(solution)/shard_map/sum_dxa/all_to_all | solution.py:617
  293.9 6.2 %collective-permute-done.31.refs_0_ = bf16[264,384]{1,0:T(8,128)(2,1)S(1)} collective-permute-done((bf16[264,384]{1,0:T(8,128)(2,1)S(1)}, bf16[264,384]{1,0:T(8,128)(2,1)S(1)}, u32[]{:S(2)}, u32[]{:S(2)}) %collective-permute-start.31) | collective-permute-done | bytes 202784 | tf_op jit(solution)/shard_map/grads_attn/ppermute | solution.py:57
  305.2 4.7 %all-to-all-start.9 = ((bf16[4,64,512]{2,1,0:T(8,128)(2,1)}), bf16[4,64,512]{2,1,0:T(8,128)(2,1)S(1)}, u32[]{:S(2)}, u32[]{:S(2)}) async-start(bf16[4,64,512]{2,1,0:T(8,128)(2,1)} %pad_maximum_fusion.6), calls=%async_computation.9 | async-start | bytes 524288 | tf_op jit(solution)/shard_map/grads/all_to_all | solution.py:890
  312.2 4.5 %all-to-all-done.9.got_ref = bf16[4,64,512]{2,1,0:T(8,128)(2,1)S(1)} async-done(((bf16[4,64,512]{2,1,0:T(8,128)(2,1)}), bf16[4,64,512]{2,1,0:T(8,128)(2,1)S(1)}, u32[]{:S(2)}, u32[]{:S(2)}) %all-to-all-start.9) | async-done | bytes 262176 | tf_op jit(solution)/shard_map/grads/all_to_all | solution.py:890
  317.3 3.3 final.1
  (375 shorter events, 117.7 us)
Async XLA Ops:
  17.1 25.8 %all-to-all-start = ((bf16[4,64,1792]{2,1,0:T(8,128)(2,1)}), bf16[4,64,1792]{2,1,0:T(8,128)(2,1)S(1)}, u32[]{:S(2)}, u32[]{:S(2)}) async-start(bf16[4,64,1792]{2,1,0:T(8,128)(2,1)} %pad_maximum_fusion.1), calls=%async_computation | async-start | bytes 1835008 | tf_op jit(solution)/shard_map/weights_ffn/all_to_all | solution.py:571
  21.3 21.4 %collective-permute-start.2 = (bf16[4,72,384]{2,1,0:T(8,128)(2,1)S(1)}, bf16[4,72,384]{2,1,0:T(8,128)(2,1)S(1)}, u32[]{:S(2)}, u32[]{:S(2)}) collective-permute-start(bf16[4,72,384]{2,1,0:T(8,128)(2,1)S(1)} %all-to-all-done.2), channel_id=1, source_target_pairs={{0,16},{16,0},{1,17},{17,1},{2,18},{18,2},{3,19},{19,3},{4,20},{20... | collective-permute-start | bytes 663560 | tf_op jit(solution)/shard_map/weights_attn/ppermute | solution.py:57
  22.9 15.3 %collective-permute-start.1 = (bf16[4,72,384]{2,1,0:T(8,128)(2,1)S(1)}, bf16[4,72,384]{2,1,0:T(8,128)(2,1)S(1)}, u32[]{:S(2)}, u32[]{:S(2)}) collective-permute-start(bf16[4,72,384]{2,1,0:T(8,128)(2,1)S(1)} %all-to-all-done.2), channel_id=1, source_target_pairs={{0,8},{8,0},{1,9},{9,1},{2,10},{10,2},{3,11},{11,3},{4,12},{12,4},... | collective-permute-start | bytes 663560 | tf_op jit(solution)/shard_map/weights_attn/ppermute | solution.py:57
  39.6 18.3 %collective-permute-start.4 = (bf16[128,1024]{1,0:T(8,128)(2,1)}, bf16[128,1024]{1,0:T(8,128)(2,1)S(1)}, u32[]{:S(2)}, u32[]{:S(2)}) collective-permute-start(bf16[128,1024]{1,0:T(8,128)(2,1)} %after.28), channel_id=1, source_target_pairs={{0,0},{1,8},{8,1},{9,9},{2,2},{3,10},{10,3},{11,11},{4,4},{5,12},{... | collective-permute-start | bytes 786440 | tf_op jit(solution)/shard_map/fetch_cot/ppermute | solution.py:600
  41.2 13.1 %collective-permute-start.3 = (bf16[4,72,384]{2,1,0:T(8,128)(2,1)}, bf16[4,72,384]{2,1,0:T(8,128)(2,1)}, u32[]{:S(2)}, u32[]{:S(2)}) collective-permute-start(bf16[4,72,384]{2,1,0:T(8,128)(2,1)} %copy-done.48), channel_id=1, source_target_pairs={{0,16},{16,0},{1,17},{17,1},{2,18},{18,2},{3,19},{19,3},{4,20},{20... | collective-permute-start | bytes 663560 | tf_op jit(solution)/shard_map/weights_attn/ppermute | solution.py:57
  44.2 20.4 %all-to-all-start.1 = ((bf16[4,128,1024]{2,1,0:T(8,128)(2,1)}), bf16[4,128,1024]{2,1,0:T(8,128)(2,1)S(1)}, u32[]{:S(2)}, u32[]{:S(2)}) async-start(bf16[4,128,1024]{2,1,0:T(8,128)(2,1)} %after.27), calls=%async_computation.1 | async-start | bytes 2097152 | tf_op jit(solution)/shard_map/tokens_hidden/all_to_all | solution.py:613
  66.8 27.7 %collective-permute-start.7 = (bf16[256,1792]{1,0:T(8,128)(2,1)}, bf16[256,1792]{1,0:T(8,128)(2,1)S(1)}, u32[]{:S(2)}, u32[]{:S(2)}) collective-permute-start(bf16[256,1792]{1,0:T(8,128)(2,1)} %after.31), channel_id=1, source_target_pairs={{0,16},{16,0},{1,17},{17,1},{2,18},{18,2},{3,19},{19,3},{4,20},{20... | collective-permute-start | bytes 2752520 | tf_op jit(solution)/shard_map/weights_ffn/ppermute | solution.py:57
  69.0 25.4 %collective-permute-start.6 = (bf16[256,896]{1,0:T(8,128)(2,1)}, bf16[256,896]{1,0:T(8,128)(2,1)S(1)}, u32[]{:S(2)}, u32[]{:S(2)}) collective-permute-start(bf16[256,896]{1,0:T(8,128)(2,1)} %after.30), channel_id=1, source_target_pairs={{0,8},{8,0},{1,9},{9,1},{2,10},{10,2},{3,11},{11,3},{4,12},{12,4},... | collective-permute-start | bytes 1376264 | tf_op jit(solution)/shard_map/weights_ffn/ppermute | solution.py:57
  69.0 17.1 %collective-permute-start.10 = (bf16[128,1024]{1,0:T(8,128)(2,1)}, bf16[128,1024]{1,0:T(8,128)(2,1)S(1)}, u32[]{:S(2)}, u32[]{:S(2)}) collective-permute-start(bf16[128,1024]{1,0:T(8,128)(2,1)} %after.32), channel_id=1, source_target_pairs={{0,6},{2,4},{4,2},{6,0},{1,7},{3,5},{5,3},{7,1},{8,14},{10,12},{12... | collective-permute-start | bytes 786440 | tf_op jit(solution)/shard_map/tokens_cot/ppermute | solution.py:662
  71.3 23.2 %collective-permute-start.9 = (bf16[128,1024]{1,0:T(8,128)(2,1)}, bf16[128,1024]{1,0:T(8,128)(2,1)S(1)}, u32[]{:S(2)}, u32[]{:S(2)}) collective-permute-start(bf16[128,1024]{1,0:T(8,128)(2,1)} %after.32), channel_id=1, source_target_pairs={{0,4},{2,6},{4,0},{6,2},{1,5},{3,7},{5,1},{7,3},{8,12},{10,14},{12... | collective-permute-start | bytes 786440 | tf_op jit(solution)/shard_map/tokens_cot/ppermute | solution.py:662
  71.9 22.6 %collective-permute-start.8 = (bf16[128,1024]{1,0:T(8,128)(2,1)}, bf16[128,1024]{1,0:T(8,128)(2,1)S(1)}, u32[]{:S(2)}, u32[]{:S(2)}) collective-permute-start(bf16[128,1024]{1,0:T(8,128)(2,1)} %after.32), channel_id=1, source_target_pairs={{0,2},{2,0},{4,6},{6,4},{1,3},{3,1},{5,7},{7,5},{8,10},{10,8},{12,... | collective-permute-start | bytes 786440 | tf_op jit(solution)/shard_map/tokens_cot/ppermute | solution.py:662
  102.2 27.7 %all-to-all-start.3 = ((bf16[4,128,1024]{2,1,0:T(8,128)(2,1)}), bf16[4,128,1024]{2,1,0:T(8,128)(2,1)S(1)}, u32[]{:S(2)}, u32[]{:S(2)}) async-start(bf16[4,128,1024]{2,1,0:T(8,128)(2,1)} %bitcast.117), calls=%async_computation.3 | async-start | bytes 2097152 | tf_op jit(solution)/shard_map/sum_attn/sum_attn/all_to_all | solution.py:617
  106.6 21.2 %collective-permute-start.12 = (bf16[256,896]{1,0:T(8,128)(2,1)}, bf16[256,896]{1,0:T(8,128)(2,1)S(1)}, u32[]{:S(2)}, u32[]{:S(2)}) collective-permute-start(bf16[256,896]{1,0:T(8,128)(2,1)} %after.34), channel_id=1, source_target_pairs={{0,8},{8,0},{1,9},{9,1},{2,10},{10,2},{3,11},{11,3},{4,12},{12,4},... | collective-permute-start | bytes 1376264 | tf_op jit(solution)/shard_map/weights_ffn/ppermute | solution.py:57
  108.3 19.5 %collective-permute-start.13 = (bf16[256,896]{1,0:T(8,128)(2,1)S(1)}, bf16[256,896]{1,0:T(8,128)(2,1)S(1)}, u32[]{:S(2)}, u32[]{:S(2)}) collective-permute-start(bf16[256,896]{1,0:T(8,128)(2,1)S(1)} %copy-done.17), channel_id=1, source_target_pairs={{0,16},{16,0},{1,17},{17,1},{2,18},{18,2},{3,19},{19,3},{4,20},{20... | collective-permute-start | bytes 1376264 | tf_op jit(solution)/shard_map/sum_attn/ppermute | solution.py:57
  131.5 18.7 %all-to-all-start.4 = ((bf16[4,128,1024]{2,1,0:T(8,128)(2,1)}), bf16[4,128,1024]{2,1,0:T(8,128)(2,1)S(1)}, u32[]{:S(2)}, u32[]{:S(2)}) async-start(bf16[4,128,1024]{2,1,0:T(8,128)(2,1)} %broadcast_in_dim.20), calls=%async_computation.4 | async-start | bytes 2097152 | tf_op jit(solution)/shard_map/tokens_xf/all_to_all | solution.py:613
  137.1 11.5 %collective-permute-start.14 = (bf16[256,896]{1,0:T(8,128)(2,1)S(1)}, bf16[256,896]{1,0:T(8,128)(2,1)S(1)}, u32[]{:S(2)}, u32[]{:S(2)}) collective-permute-start(bf16[256,896]{1,0:T(8,128)(2,1)S(1)} %copy-done.30), channel_id=1, source_target_pairs={{0,16},{16,0},{1,17},{17,1},{2,18},{18,2},{3,19},{19,3},{4,20},{20... | collective-permute-start | bytes 1376264 | tf_op jit(solution)/shard_map/weights_ffn/ppermute | solution.py:57
  183.3 18.9 %all-to-all-start.5 = ((bf16[4,128,1024]{2,1,0:T(8,128)(2,1)}), bf16[4,128,1024]{2,1,0:T(8,128)(2,1)S(1)}, u32[]{:S(2)}, u32[]{:S(2)}) async-start(bf16[4,128,1024]{2,1,0:T(8,128)(2,1)} %bitcast.39), calls=%async_computation.5 | async-start | bytes 2097152 | tf_op jit(solution)/shard_map/sum_dxf/all_to_all | solution.py:617
  186.8 12.5 %collective-permute-start.19 = (bf16[256,896]{1,0:T(8,128)(2,1)S(1)}, bf16[256,896]{1,0:T(8,128)(2,1)S(1)}, u32[]{:S(2)}, u32[]{:S(2)}) collective-permute-start(bf16[256,896]{1,0:T(8,128)(2,1)S(1)} %copy-done.60), channel_id=1, source_target_pairs={{0,16},{16,0},{1,17},{17,1},{2,18},{18,2},{3,19},{19,3},{4,20},{20... | collective-permute-start | bytes 1376264 | tf_op jit(solution)/shard_map/grads_ffn/ppermute | solution.py:57
  204.9 28.0 %all-to-all-start.6 = ((bf16[4,128,1024]{2,1,0:T(8,128)(2,1)}), bf16[4,128,1024]{2,1,0:T(8,128)(2,1)S(1)}, u32[]{:S(2)}, u32[]{:S(2)}) async-start(bf16[4,128,1024]{2,1,0:T(8,128)(2,1)} %after.41), calls=%async_computation.6 | async-start | bytes 2097152 | tf_op jit(solution)/shard_map/tokens_dattn/all_to_all | solution.py:613
  208.8 14.0 %collective-permute-start.18 = (bf16[512,1024]{1,0:T(8,128)(2,1)}, bf16[512,1024]{1,0:T(8,128)(2,1)S(1)}, u32[]{:S(2)}, u32[]{:S(2)}) collective-permute-start(bf16[512,1024]{1,0:T(8,128)(2,1)} %after.39), channel_id=1, source_target_pairs={{0,1},{1,0},{2,3},{3,2},{4,5},{5,4},{6,7},{7,6},{8,9},{9,8},{10,11... | collective-permute-start | bytes 3145736 | tf_op jit(solution)/shard_map/sum_out/ppermute | solution.py:57
  208.8 13.1 %collective-permute-start.21 = (bf16[256,896]{1,0:T(8,128)(2,1)}, bf16[256,896]{1,0:T(8,128)(2,1)S(1)}, u32[]{:S(2)}, u32[]{:S(2)}) collective-permute-start(bf16[256,896]{1,0:T(8,128)(2,1)} %get-tuple-element.69), channel_id=1, source_target_pairs={{0,16},{16,0},{1,17},{17,1},{2,18},{18,2},{3,19},{19,3},{4,20},{20... | collective-permute-start | bytes 1376264 | tf_op jit(solution)/shard_map/grads_ffn/ppermute | solution.py:57
  209.4 23.4 %collective-permute-start.20 = (bf16[256,896]{1,0:T(8,128)(2,1)S(1)}, bf16[256,896]{1,0:T(8,128)(2,1)S(1)}, u32[]{:S(2)}, u32[]{:S(2)}) collective-permute-start(bf16[256,896]{1,0:T(8,128)(2,1)S(1)} %copy-done.35), channel_id=1, source_target_pairs={{0,8},{8,0},{1,9},{9,1},{2,10},{10,2},{3,11},{11,3},{4,12},{12,4},... | collective-permute-start | bytes 1376264 | tf_op jit(solution)/shard_map/grads_ffn/ppermute | solution.py:57
  234.0 37.0 %all-to-all-start.7 = ((bf16[4,128,1024]{2,1,0:T(8,128)(2,1)}), bf16[4,128,1024]{2,1,0:T(8,128)(2,1)S(1)}, u32[]{:S(2)}, u32[]{:S(2)}) async-start(bf16[4,128,1024]{2,1,0:T(8,128)(2,1)} %bitcast.114), calls=%async_computation.7 | async-start | bytes 2097152 | tf_op jit(solution)/shard_map/sum_out/all_to_all | solution.py:813
  237.8 22.4 %collective-permute-start.23 = (bf16[256,896]{1,0:T(8,128)(2,1)}, bf16[256,896]{1,0:T(8,128)(2,1)S(1)}, u32[]{:S(2)}, u32[]{:S(2)}) collective-permute-start(bf16[256,896]{1,0:T(8,128)(2,1)} %add_convert_fusion.3.refs_3_), channel_id=1, source_target_pairs={{0,8},{8,0},{1,9},{9,1},{2,10},{10,2},{3,11},{11,3},{4,12},{12,4},... | collective-permute-start | bytes 1376264 | tf_op jit(solution)/shard_map/grads_ffn/ppermute | solution.py:57
  239.7 30.5 %collective-permute-start.26 = (bf16[256,1792]{1,0:T(8,128)(2,1)}, bf16[256,1792]{1,0:T(8,128)(2,1)}, u32[]{:S(2)}, u32[]{:S(2)}) collective-permute-start(bf16[256,1792]{1,0:T(8,128)(2,1)} %after.48), channel_id=1, source_target_pairs={{0,16},{16,0},{1,17},{17,1},{2,18},{18,2},{3,19},{19,3},{4,20},{20... | collective-permute-start | bytes 2752520 | tf_op jit(solution)/shard_map/grads_ffn/ppermute | solution.py:57
  277.2 24.4 %all-to-all-start.8 = ((bf16[4,128,1024]{2,1,0:T(8,128)(2,1)}), bf16[4,128,1024]{2,1,0:T(8,128)(2,1)S(1)}, u32[]{:S(2)}, u32[]{:S(2)}) async-start(bf16[4,128,1024]{2,1,0:T(8,128)(2,1)} %bitcast.107), calls=%async_computation.8 | async-start | bytes 2097152 | tf_op jit(solution)/shard_map/sum_dxa/all_to_all | solution.py:617
  283.3 16.9 %collective-permute-start.31 = (bf16[264,384]{1,0:T(8,128)(2,1)S(1)}, bf16[264,384]{1,0:T(8,128)(2,1)S(1)}, u32[]{:S(2)}, u32[]{:S(2)}) collective-permute-start(bf16[264,384]{1,0:T(8,128)(2,1)S(1)} %pad_maximum_fusion.9), channel_id=1, source_target_pairs={{0,8},{8,0},{1,9},{9,1},{2,10},{10,2},{3,11},{11,3},{4,12},{12,4},... | collective-permute-start | bytes 608264 | tf_op jit(solution)/shard_map/grads_attn/ppermute | solution.py:57
  284.7 18.6 %collective-permute-start.29 = (bf16[256,384]{1,0:T(8,128)(2,1)}, bf16[256,384]{1,0:T(8,128)(2,1)}, u32[]{:S(2)}, u32[]{:S(2)}) collective-permute-start(bf16[256,384]{1,0:T(8,128)(2,1)} %get-tuple-element.77.refs_2_), channel_id=1, source_target_pairs={{0,16},{16,0},{1,17},{17,1},{2,18},{18,2},{3,19},{19,3},{4,20},{20... | collective-permute-start | bytes 589832 | tf_op jit(solution)/shard_map/grads_attn/ppermute | solution.py:57
  289.0 21.9 %collective-permute-start.32 = (bf16[64,1792]{1,0:T(8,128)(2,1)}, bf16[64,1792]{1,0:T(8,128)(2,1)}, u32[]{:S(2)}, u32[]{:S(2)}) collective-permute-start(bf16[64,1792]{1,0:T(8,128)(2,1)} %get-tuple-element.86), channel_id=1, source_target_pairs={{0,2},{2,0},{4,6},{6,4},{1,3},{3,1},{5,7},{7,5},{8,10},{10,8},{12,... | collective-permute-start | bytes 688136 | tf_op jit(solution)/shard_map/grads_ffn/ppermute | solution.py:867
  290.9 19.9 %collective-permute-start.33 = (bf16[64,1792]{1,0:T(8,128)(2,1)}, bf16[64,1792]{1,0:T(8,128)(2,1)}, u32[]{:S(2)}, u32[]{:S(2)}) collective-permute-start(bf16[64,1792]{1,0:T(8,128)(2,1)} %get-tuple-element.87), channel_id=1, source_target_pairs={{0,4},{2,6},{4,0},{6,2},{1,5},{3,7},{5,1},{7,3},{8,12},{10,14},{12... | collective-permute-start | bytes 688136 | tf_op jit(solution)/shard_map/grads_ffn/ppermute | solution.py:867
  292.4 19.7 %collective-permute-start.34 = (bf16[64,1792]{1,0:T(8,128)(2,1)}, bf16[64,1792]{1,0:T(8,128)(2,1)}, u32[]{:S(2)}, u32[]{:S(2)}) collective-permute-start(bf16[64,1792]{1,0:T(8,128)(2,1)} %get-tuple-element.88), channel_id=1, source_target_pairs={{0,6},{2,4},{4,2},{6,0},{1,7},{3,5},{5,3},{7,1},{8,14},{10,12},{12... | collective-permute-start | bytes 688136 | tf_op jit(solution)/shard_map/grads_ffn/ppermute | solution.py:867
  310.1 13.6 %collective-permute-start.27 = (bf16[2,128,1024]{2,1,0:T(8,128)(2,1)S(1)}, bf16[2,128,1024]{2,1,0:T(8,128)(2,1)S(1)}, u32[]{:S(2)}, u32[]{:S(2)}) collective-permute-start(bf16[2,128,1024]{2,1,0:T(8,128)(2,1)S(1)} %pad_maximum_fusion.3), channel_id=1, source_target_pairs={{0,0},{1,8},{8,1},{9,9},{2,2},{3,10},{10,3},{11,11},{4,4},{5,12},{... | collective-permute-start | bytes 1572872 | tf_op jit(solution)/shard_map/return/ppermute | solution.py:604
  (90 other events, 637.8 us)

commit v2 on v1

--- a/solution.py
+++ b/solution.py
@@ -428,6 +428,27 @@
         cost_estimate=SMALL_COST,
         name="add",
     )(keep, got0, got1)
+
+
+def add_cut_kernel(place_ref, a_ref, b_ref, *outs):
+    height = outs[0].shape[0]
+    for d, out_ref in enumerate(outs):
+        at = pl.ds(pl.multiple_of((place_ref[0] ^ d) * height, height), height)
+        out_ref[...] = (a_ref[at, :].astype(F32) + b_ref[at, :].astype(F32)).astype(BF)
+
+
+def add_cut_call(place, places, a, b):
+    vmem = pl.BlockSpec(memory_space=pltpu.VMEM)
+    shape = jax.ShapeDtypeStruct((a.shape[0] // places, a.shape[1]), BF)
+    return pl.pallas_call(
+        add_cut_kernel,
+        in_specs=[pl.BlockSpec(memory_space=pltpu.SMEM)] + [vmem] * 2,
+        out_specs=[vmem] * places,
+        out_shape=[shape] * places,
+        compiler_params=pltpu.CompilerParams(vmem_limit_bytes=VMEM_BYTES),
+        cost_estimate=SMALL_COST,
+        name="add_cut",
+    )(place, a, b)
 
 
 def attn_grad_kernel(x0_ref, x1_ref, g0_ref, g1_ref, raw_ref, mixed_ref, *outs):
@@ -765,9 +786,12 @@
     with jax.named_scope("sum_attn"):
         wo = wa[:, qw + 2 * HEAD_DIM :]
         low = swap(mm_nt(mixed[side:], wo).astype(BF), "tp")
-        low = add(mm_nt(mixed[:side], wo), low)
+        keep = mm_nt(mixed[:side], wo).astype(BF)
+        parts = list(add_cut_call(ij[None], J, keep, low))
+        for d in range(1, J):
+            parts[d] = lax.ppermute(parts[d], "j", [(i, i ^ d) for i in range(J)])
         w_a.append(swap(w_a[1], "dp"))
-        attn_branch = sum_tokens("sum_attn", low)
+        attn_branch = sum(p.astype(F32) for p in parts)
 
     middle = stream + attn_branch
     gain_ffn = after(gain_ffn, w_b[1], w_a[2])
@@ -793,19 +817,18 @@
         0, ffn_width, False, ffn_in, cot, grad_pre, hidden_act
     )
     grad_ffn_in = sum_tokens("sum_dxf", low)
-    gain_ffn = after(gain_ffn, got_b, near_a)
+    with jax.named_scope("sum_out"):
+        low = add(branch[0], swap(branch[1], "tp"))
+    gain_ffn = after(gain_ffn, got_b, near_a, low)
 
     grad_middle = cot_own.astype(F32) + norm_back(middle, ffn_factor, gain_ffn, grad_ffn_in)
     with jax.named_scope("grads_ffn"):
         beside_b = add(beside_b, got_b)
-    half = gather_half("tokens_dattn", grad_middle.astype(BF), beside_b)
-    with jax.named_scope("sum_out"):
-        low = swap(after(branch[1], grad_ffn_in), "tp")
-        low = add(branch[0], low)
+    half = jnp.concatenate(in_order(share("tokens_dattn", grad_middle.astype(BF)), ij), 0)
     with jax.named_scope("grads_ffn"):
         got_b = swap(beside_b, "h")
         beside_a = add(beside_a, got_a)
-        half = after(half, low, got_b, beside_a)
+        half = after(half, got_b, beside_a)
         got_a = swap(beside_a, "h")
         opposite = swap(after(opposite, half), "dp")
     grad_attn = [half, swap(half, "tp")]

time: 332 us -> 327 us (0.985)
  waiting for transfers between devices: 98.1 us -> 92.2 us
    ppermute x27, waiting for transfers between devices: 75.2 us -> 50 us  [swap(): return lax.ppermute(v, axis, [(0, 1), (1, 0)])]
    ppermute x3 -> x6, waiting for transfers between devices: 8.38 us -> 22.3 us  [share(): lax.ppermute(block, 'j', [(i, i ^ d) for i in range(J)])]
    all_to_all x3 -> x2, starting transfers between devices: 15.9 us -> 10.1 us  [gather_half(): return lax.all_to_all(sent, 'j', 0, 0).reshape(side, d_model)]
    ppermute x0 -> x3, waiting for transfers between devices: none -> 5.77 us  [body(): parts[d] = lax.ppermute(parts[d], 'j', [(i, i ^ d) for i in range(J)])]
    all_to_all x3 -> x2, starting transfers between devices: 13.2 us -> 9.09 us  [sum_tokens(): got = lax.all_to_all(half.reshape(J, rows, d_model), 'j', 0, 0)]
    ppermute x0 -> x3, starting transfers between devices: none -> 3.49 us  [body(): parts[d] = lax.ppermute(parts[d], 'j', [(i, i ^ d) for i in range(J)])]
    ppermute x3 -> x6, starting transfers between devices: 3.92 us -> 7.41 us  [share(): lax.ppermute(block, 'j', [(i, i ^ d) for i in range(J)])]
    all_to_all x3 -> x2, waiting for transfers between devices: 7.47 us -> 7.12 us  [gather_half(): return lax.all_to_all(sent, 'j', 0, 0).reshape(side, d_model)]
  transfers between devices with their start and end apart: 46 -> 50, of which waited for: 19 -> 20; matrix products, arithmetic and copies ran while one was open for 12% -> 14% of each run, Pallas kernels for 18% -> 19%
where the time goes in v2:
time: 327 us; the launch traced here: 324 us
  waiting for transfers between devices  92.2 us (28%)
  starting transfers between devices  83.6 us (26%)
  Pallas kernels  71.3 us (22%)
  other arithmetic  38.4 us (12%)
  local copies, waits for them, and re-layouts  33.2 us (10%)
  matrix products  3.82 us (1%)
    ppermute x27, waiting for transfers between devices, swap(): return lax.ppermute(v, axis, [(0, 1), (1, 0)])  50 us
    ppermute x27, starting transfers between devices, swap(): return lax.ppermute(v, axis, [(0, 1), (1, 0)])  29.4 us
    ppermute x6, waiting for transfers between devices, share(): lax.ppermute(block, 'j', [(i, i ^ d) for i in range(J)])  22.3 us
    unnamed x165, local copies, waits for them, and re-layouts  18 us
    pallas_call x2, Pallas kernels, ffn_call(): pl.pallas_call(functools.partial(ffn_kernel, fw, part), grid=(count // ti...  17.3 us
    pallas_call x2, Pallas kernels, ffn_grad_call(): pl.pallas_call(functools.partial(ffn_grad_kernel, fw, width, whole), grid...  13 us
    pallas_call x1, Pallas kernels, attend_back_call(): pl.pallas_call(functools.partial(attend_back_kernel, tile, tiles), in_spe...  11.7 us
    all_to_all x2, starting transfers between devices, gather_half(): return lax.all_to_all(sent, 'j', 0, 0).reshape(side, d_model)  10.1 us
  transfers between devices with their start and end apart: 50, of which 20 were waited for; matrix products, arithmetic and copies ran while one was open for 14% of the time, Pallas kernels for 19%

profile of v2, /device:TPU:0, one launch (start us, length us, event | category | flops | bytes accessed | tf_op | source)
XLA Modules:
  0.0 324.5 jit_solution(6915925354753031740)
XLA Ops:
  5.7 5.2 %all-to-all-start.2 = ((bf16[4,72,384]{2,1,0:T(8,128)(2,1)}), bf16[4,72,384]{2,1,0:T(8,128)(2,1)S(1)}, u32[]{:S(2)}, u32[]{:S(2)}) async-start(bf16[4,72,384]{2,1,0:T(8,128)(2,1)} %pad_maximum_fusion.8), calls=%async_computation.2 | async-start | bytes 442368 | tf_op jit(solution)/shard_map/weights_attn/all_to_all | solution.py:592
  17.2 4.2 %all-to-all-start = ((bf16[4,64,1792]{2,1,0:T(8,128)(2,1)}), bf16[4,64,1792]{2,1,0:T(8,128)(2,1)S(1)}, u32[]{:S(2)}, u32[]{:S(2)}) async-start(bf16[4,64,1792]{2,1,0:T(8,128)(2,1)} %pad_maximum_fusion.2), calls=%async_computation | async-start | bytes 1835008 | tf_op jit(solution)/shard_map/weights_ffn/all_to_all | solution.py:592
  22.9 8.0 %collective-permute-start.1 = (bf16[4,72,384]{2,1,0:T(8,128)(2,1)S(1)}, bf16[4,72,384]{2,1,0:T(8,128)(2,1)S(1)}, u32[]{:S(2)}, u32[]{:S(2)}) collective-permute-start(bf16[4,72,384]{2,1,0:T(8,128)(2,1)S(1)} %all-to-all-done.2), channel_id=1, source_target_pairs={{0,8},{8,0},{1,9},{9,1},{2,10},{10,2},{3,11},{11,3},{4,12},{12,4},... | collective-permute-start | bytes 663560 | tf_op jit(solution)/shard_map/weights_attn/ppermute | solution.py:57
  30.9 7.2 %collective-permute-done.1.refs_1_ = bf16[4,72,384]{2,1,0:T(8,128)(2,1)S(1)} collective-permute-done((bf16[4,72,384]{2,1,0:T(8,128)(2,1)S(1)}, bf16[4,72,384]{2,1,0:T(8,128)(2,1)S(1)}, u32[]{:S(2)}, u32[]{:S(2)}) %collective-permute-start.1) | collective-permute-done | bytes 221216 | tf_op jit(solution)/shard_map/weights_attn/ppermute | solution.py:57
  44.2 6.4 %all-to-all-start.1 = ((bf16[4,128,1024]{2,1,0:T(8,128)(2,1)}), bf16[4,128,1024]{2,1,0:T(8,128)(2,1)S(1)}, u32[]{:S(2)}, u32[]{:S(2)}) async-start(bf16[4,128,1024]{2,1,0:T(8,128)(2,1)} %after.25), calls=%async_computation.1 | async-start | bytes 2097152 | tf_op jit(solution)/shard_map/tokens_hidden/all_to_all | solution.py:634
  50.6 3.1 multiply_sine_fusion
  58.8 5.8 %all-to-all-done.1 = bf16[4,128,1024]{2,1,0:T(8,128)(2,1)S(1)} async-done(((bf16[4,128,1024]{2,1,0:T(8,128)(2,1)}), bf16[4,128,1024]{2,1,0:T(8,128)(2,1)S(1)}, u32[]{:S(2)}, u32[]{:S(2)}) %all-to-all-start.1) | async-done | bytes 1048608 | tf_op jit(solution)/shard_map/tokens_hidden/all_to_all | solution.py:634
  73.7 6.1 %qkv.1 = (bf16[512,1024]{1,0:T(8,128)(2,1)}, bf16[512,1024]{1,0:T(8,128)(2,1)}, f32[1024,256]{1,0:T(8,128)}, bf16[1024,256]{1,0:T(8,128)(2,1)}) custom-call(bf16[512,1024]{1,0:T(8,128)(2,1)} %after.27.h0_ref.refs_1_, bf16[512,1024]{1,0:T(8,128)(2,1)} %collective-permute-done.5.h1_ref, f32[1,1024]{1,0:T(1,128)} %slice.354.gain_ref, ...), custom_call_target="tpu_custom_call" | custom-call | flops 1 | bytes 1 | tf_op jit(solution)/shard_map/qkv/pallas_call | solution.py:155
  79.8 6.3 %attend.1 = (bf16[1024,128]{1,0:T(8,128)(2,1)}, bf16[10,512,256]{2,1,0:T(8,128)(2,1)}) custom-call(s32[2]{0:T(128)} %pad_add_fusion.refs_6_.at_ref, bf16[1024,256]{1,0:T(8,128)(2,1)} %get-tuple-element.59.qkv_ref), custom_call_target="tpu_custom_call" | custom-call | flops 1 | bytes 1 | tf_op jit(solution)/shard_map/attend/pallas_call | solution.py:215
  86.1 8.4 %collective-permute-done.9.refs_4_ = bf16[128,1024]{1,0:T(8,128)(2,1)S(1)} collective-permute-done((bf16[128,1024]{1,0:T(8,128)(2,1)}, bf16[128,1024]{1,0:T(8,128)(2,1)S(1)}, u32[]{:S(2)}, u32[]{:S(2)}) %collective-permute-start.9) | collective-permute-done | bytes 262176 | tf_op jit(solution)/shard_map/tokens_cot/ppermute | solution.py:683
  102.6 2.7 add_cut.1
  109.5 13.3 %collective-permute-done.15.refs_1_.refs_4_ = bf16[256,896]{1,0:T(8,128)(2,1)S(1)} collective-permute-done((bf16[256,896]{1,0:T(8,128)(2,1)}, bf16[256,896]{1,0:T(8,128)(2,1)S(1)}, u32[]{:S(2)}, u32[]{:S(2)}) %collective-permute-start.15) | collective-permute-done | bytes 458784 | tf_op jit(solution)/shard_map/weights_ffn/ppermute | solution.py:57
  124.9 5.2 %collective-permute-done.14 = bf16[128,1024]{1,0:T(8,128)(2,1)S(1)} collective-permute-done((bf16[128,1024]{1,0:T(8,128)(2,1)}, bf16[128,1024]{1,0:T(8,128)(2,1)S(1)}, u32[]{:S(2)}, u32[]{:S(2)}) %collective-permute-start.14) | collective-permute-done | bytes 262176 | tf_op jit(solution)/shard_map/sum_attn/ppermute | solution.py:792
  133.4 3.7 %all-to-all-start.3 = ((bf16[4,128,1024]{2,1,0:T(8,128)(2,1)}), bf16[4,128,1024]{2,1,0:T(8,128)(2,1)S(1)}, u32[]{:S(2)}, u32[]{:S(2)}) async-start(bf16[4,128,1024]{2,1,0:T(8,128)(2,1)} %broadcast_in_dim.19), calls=%async_computation.3 | async-start | bytes 2097152 | tf_op jit(solution)/shard_map/tokens_xf/all_to_all | solution.py:634
  140.7 7.6 %collective-permute-done.17.refs_1_.refs_5_ = bf16[256,896]{1,0:T(8,128)(2,1)S(1)} collective-permute-done((bf16[256,896]{1,0:T(8,128)(2,1)S(1)}, bf16[256,896]{1,0:T(8,128)(2,1)S(1)}, u32[]{:S(2)}, u32[]{:S(2)}) %collective-permute-start.17) | collective-permute-done | bytes 458784 | tf_op jit(solution)/shard_map/weights_ffn/ppermute | solution.py:57
  152.9 8.6 %ffn.2 = (bf16[512,576]{1,0:T(8,128)(2,1)}, bf16[512,1152]{1,0:T(8,128)(2,1)}, bf16[512,1024]{1,0:T(8,128)(2,1)}, bf16[512,1024]{1,0:T(8,128)(2,1)}) custom-call(bf16[512,1024]{1,0:T(8,128)(2,1)} %after.34.x_ref.refs_0_, bf16[512,1024]{1,0:T(8,128)(2,1)} %copy-done.6, bf16[256,896]{1,0:T(8,128)(2,1)} %copy-done.14, bf16[256,896]{1,0:T(8,128)(2,1)} %copy-done.15, ...), custom_call_target="tpu_custom_call" | custom-call | flops 1 | bytes 1 | tf_op jit(solution)/shard_map/ffn/pallas_call | solution.py:352
  162.9 8.6 %ffn.3 = (bf16[512,576]{1,0:T(8,128)(2,1)}, bf16[512,1152]{1,0:T(8,128)(2,1)}, bf16[512,1024]{1,0:T(8,128)(2,1)}, bf16[512,1024]{1,0:T(8,128)(2,1)}) custom-call(bf16[512,1024]{1,0:T(8,128)(2,1)} %after.35.x_ref, bf16[512,1024]{1,0:T(8,128)(2,1)} %collective-permute-done.19.cot_ref.refs_3_, bf16[256,896]{1,0:T(8,128)(2,1)} %copy-done.14, ...), custom_call_target="tpu_custom_call" | custom-call | flops 1 | bytes 1 | tf_op jit(solution)/shard_map/ffn/pallas_call | solution.py:352
  172.1 6.5 %ffn_grad.2 = (bf16[256,1792]{1,0:T(8,128)(2,1)}, bf16[256,896]{1,0:T(8,128)(2,1)}, bf16[256,896]{1,0:T(8,128)(2,1)}) custom-call(bf16[512,1024]{1,0:T(8,128)(2,1)} %after.34.x_ref.refs_0_, bf16[512,1024]{1,0:T(8,128)(2,1)} %copy-done.9, bf16[512,1024]{1,0:T(8,128)(2,1)} %copy-done.6, bf16[512,1024]{1,0:T(8,128)(2,1)} %collective-permute-done.19.cot_ref.refs_3_, ...), custom_call_target="tpu_custom_call" | custom-call | flops 1 | bytes 1 | tf_op jit(solution)/shard_map/ffn_grad/pallas_call | solution.py:402
  182.8 3.5 %all-to-all-start.4 = ((bf16[4,128,1024]{2,1,0:T(8,128)(2,1)}), bf16[4,128,1024]{2,1,0:T(8,128)(2,1)S(1)}, u32[]{:S(2)}, u32[]{:S(2)}) async-start(bf16[4,128,1024]{2,1,0:T(8,128)(2,1)} %bitcast.39), calls=%async_computation.4 | async-start | bytes 2097152 | tf_op jit(solution)/shard_map/sum_dxf/all_to_all | solution.py:638
  188.5 6.5 %ffn_grad.3 = (bf16[256,896]{1,0:T(8,128)(2,1)}, bf16[256,896]{1,0:T(8,128)(2,1)}, bf16[256,896]{1,0:T(8,128)(2,1)}, bf16[256,896]{1,0:T(8,128)(2,1)}) custom-call(bf16[512,1024]{1,0:T(8,128)(2,1)} %after.34.x_ref.refs_0_, bf16[512,1024]{1,0:T(8,128)(2,1)} %copy-done.9, bf16[512,1024]{1,0:T(8,128)(2,1)} %copy-done.6, ...), custom_call_target="tpu_custom_call" | custom-call | flops 1 | bytes 1 | tf_op jit(solution)/shard_map/ffn_grad/pallas_call | solution.py:402
  211.2 11.9 %collective-permute-done.24 = bf16[128,1024]{1,0:T(8,128)(2,1)S(1)} collective-permute-done((bf16[128,1024]{1,0:T(8,128)(2,1)S(1)}, bf16[128,1024]{1,0:T(8,128)(2,1)S(1)}, u32[]{:S(2)}, u32[]{:S(2)}) %collective-permute-start.24) | collective-permute-done | bytes 262176 | tf_op jit(solution)/shard_map/tokens_dattn/ppermute | solution.py:683
  229.1 3.7 %all-to-all-start.5 = ((bf16[4,128,1024]{2,1,0:T(8,128)(2,1)}), bf16[4,128,1024]{2,1,0:T(8,128)(2,1)S(1)}, u32[]{:S(2)}, u32[]{:S(2)}) async-start(bf16[4,128,1024]{2,1,0:T(8,128)(2,1)} %bitcast.111), calls=%async_computation.5 | async-start | bytes 2097152 | tf_op jit(solution)/shard_map/sum_out/all_to_all | solution.py:836
  236.8 11.7 %attend_back.1 = (bf16[1024,256]{1,0:T(8,128)(2,1)}, f32[8,128]{1,0:T(8,128)}, bf16[256,1024]{1,0:T(8,128)(2,1)}, bf16[256,1024]{1,0:T(8,128)(2,1)}, bf16[512,1024]{1,0:T(8,128)(2,1)}) custom-call(s32[2]{0:T(128)} %pad_add_fusion.refs_6_.at_ref, bf16[1024,256]{1,0:T(8,128)(2,1)} %get-tuple-element.59.qkv_ref, bf16[1024,128]{1,0:T(8,128)(2,1)} %after.31.mixed_ref, ...), custom_call_target="tpu_custom_call" | custom-call | flops 1 | bytes 1 | tf_op jit(solution)/shard_map/attend_back/pallas_call | solution.py:300
  248.5 6.6 %collective-permute-done.29.refs_1_.got_a = bf16[256,896]{1,0:T(8,128)(2,1)} collective-permute-done((bf16[256,896]{1,0:T(8,128)(2,1)}, bf16[256,896]{1,0:T(8,128)(2,1)}, u32[]{:S(2)}, u32[]{:S(2)}) %collective-permute-start.29) | collective-permute-done | bytes 458784 | tf_op jit(solution)/shard_map/grads_ffn/ppermute | solution.py:57
  255.7 5.3 %attn_grad.1 = (bf16[256,384]{1,0:T(8,128)(2,1)}, bf16[256,384]{1,0:T(8,128)(2,1)}, bf16[256,384]{1,0:T(8,128)(2,1)}, bf16[256,384]{1,0:T(8,128)(2,1)}) custom-call(bf16[512,1024]{1,0:T(8,128)(2,1)} %get-tuple-element.83.x0_ref, bf16[512,1024]{1,0:T(8,128)(2,1)} %get-tuple-element.84.x1_ref, bf16[512,1024]{1,0:T(8,128)(2,1)} %after.38.refs_1_.g0_ref, ...), custom_call_target="tpu_custom_call" | custom-call | flops 1 | bytes 1 | tf_op jit(solution)/shard_map/attn_grad/pallas_call | solution.py:472
  269.2 2.8 add.222.refs_1_
  273.7 5.6 %all-to-all-start.6 = ((bf16[4,128,1024]{2,1,0:T(8,128)(2,1)}), bf16[4,128,1024]{2,1,0:T(8,128)(2,1)S(1)}, u32[]{:S(2)}, u32[]{:S(2)}) async-start(bf16[4,128,1024]{2,1,0:T(8,128)(2,1)} %bitcast.104), calls=%async_computation.6 | async-start | bytes 2097152 | tf_op jit(solution)/shard_map/sum_dxa/all_to_all | solution.py:638
  282.4 2.9 merge.1
  288.8 7.5 %collective-permute-done.37.refs_0_ = bf16[264,384]{1,0:T(8,128)(2,1)S(1)} collective-permute-done((bf16[264,384]{1,0:T(8,128)(2,1)S(1)}, bf16[264,384]{1,0:T(8,128)(2,1)S(1)}, u32[]{:S(2)}, u32[]{:S(2)}) %collective-permute-start.37) | collective-permute-done | bytes 202784 | tf_op jit(solution)/shard_map/grads_attn/ppermute | solution.py:57
  300.8 4.4 %all-to-all-start.7 = ((bf16[4,64,512]{2,1,0:T(8,128)(2,1)}), bf16[4,64,512]{2,1,0:T(8,128)(2,1)S(1)}, u32[]{:S(2)}, u32[]{:S(2)}) async-start(bf16[4,64,512]{2,1,0:T(8,128)(2,1)} %pad_maximum_fusion.7), calls=%async_computation.7 | async-start | bytes 524288 | tf_op jit(solution)/shard_map/grads/all_to_all | solution.py:913
  308.9 3.0 all-to-all-done.7.got_ref
  312.6 3.3 %final.1 = (f32[64,512]{1,0:T(8,128)}, f32[64,256]{1,0:T(8,128)}, f32[64,256]{1,0:T(8,128)}, f32[64,512]{1,0:T(8,128)}, f32[64,2304]{1,0:T(8,128)}, /*index=5*/f...) custom-call(s32[1]{0:T(128)} %bitcast.1.place_ref, bf16[4,64,512]{2,1,0:T(8,128)(2,1)} %copy-done.46, ...), custom_call_target="tpu_custom_call" | custom-call | flops 1 | bytes 1 | tf_op jit(solution)/shard_map/final/pallas_call | solution.py:544
  (393 shorter events, 127.0 us)
Async XLA Ops:
  17.2 25.7 %all-to-all-start = ((bf16[4,64,1792]{2,1,0:T(8,128)(2,1)}), bf16[4,64,1792]{2,1,0:T(8,128)(2,1)S(1)}, u32[]{:S(2)}, u32[]{:S(2)}) async-start(bf16[4,64,1792]{2,1,0:T(8,128)(2,1)} %pad_maximum_fusion.2), calls=%async_computation | async-start | bytes 1835008 | tf_op jit(solution)/shard_map/weights_ffn/all_to_all | solution.py:592
  21.4 21.4 %collective-permute-start.2 = (bf16[4,72,384]{2,1,0:T(8,128)(2,1)S(1)}, bf16[4,72,384]{2,1,0:T(8,128)(2,1)S(1)}, u32[]{:S(2)}, u32[]{:S(2)}) collective-permute-start(bf16[4,72,384]{2,1,0:T(8,128)(2,1)S(1)} %all-to-all-done.2), channel_id=1, source_target_pairs={{0,16},{16,0},{1,17},{17,1},{2,18},{18,2},{3,19},{19,3},{4,20},{20... | collective-permute-start | bytes 663560 | tf_op jit(solution)/shard_map/weights_attn/ppermute | solution.py:57
  22.9 15.2 %collective-permute-start.1 = (bf16[4,72,384]{2,1,0:T(8,128)(2,1)S(1)}, bf16[4,72,384]{2,1,0:T(8,128)(2,1)S(1)}, u32[]{:S(2)}, u32[]{:S(2)}) collective-permute-start(bf16[4,72,384]{2,1,0:T(8,128)(2,1)S(1)} %all-to-all-done.2), channel_id=1, source_target_pairs={{0,8},{8,0},{1,9},{9,1},{2,10},{10,2},{3,11},{11,3},{4,12},{12,4},... | collective-permute-start | bytes 663560 | tf_op jit(solution)/shard_map/weights_attn/ppermute | solution.py:57
  39.6 18.3 %collective-permute-start.4 = (bf16[128,1024]{1,0:T(8,128)(2,1)}, bf16[128,1024]{1,0:T(8,128)(2,1)S(1)}, u32[]{:S(2)}, u32[]{:S(2)}) collective-permute-start(bf16[128,1024]{1,0:T(8,128)(2,1)} %after.26), channel_id=1, source_target_pairs={{0,0},{1,8},{8,1},{9,9},{2,2},{3,10},{10,3},{11,11},{4,4},{5,12},{... | collective-permute-start | bytes 786440 | tf_op jit(solution)/shard_map/fetch_cot/ppermute | solution.py:621
  44.2 20.4 %all-to-all-start.1 = ((bf16[4,128,1024]{2,1,0:T(8,128)(2,1)}), bf16[4,128,1024]{2,1,0:T(8,128)(2,1)S(1)}, u32[]{:S(2)}, u32[]{:S(2)}) async-start(bf16[4,128,1024]{2,1,0:T(8,128)(2,1)} %after.25), calls=%async_computation.1 | async-start | bytes 2097152 | tf_op jit(solution)/shard_map/tokens_hidden/all_to_all | solution.py:634
  66.8 27.7 %collective-permute-start.7 = (bf16[256,1792]{1,0:T(8,128)(2,1)}, bf16[256,1792]{1,0:T(8,128)(2,1)S(1)}, u32[]{:S(2)}, u32[]{:S(2)}) collective-permute-start(bf16[256,1792]{1,0:T(8,128)(2,1)} %after.29), channel_id=1, source_target_pairs={{0,16},{16,0},{1,17},{17,1},{2,18},{18,2},{3,19},{19,3},{4,20},{20... | collective-permute-start | bytes 2752520 | tf_op jit(solution)/shard_map/weights_ffn/ppermute | solution.py:57
  69.0 25.4 %collective-permute-start.6 = (bf16[256,896]{1,0:T(8,128)(2,1)}, bf16[256,896]{1,0:T(8,128)(2,1)S(1)}, u32[]{:S(2)}, u32[]{:S(2)}) collective-permute-start(bf16[256,896]{1,0:T(8,128)(2,1)} %after.28), channel_id=1, source_target_pairs={{0,8},{8,0},{1,9},{9,1},{2,10},{10,2},{3,11},{11,3},{4,12},{12,4},... | collective-permute-start | bytes 1376264 | tf_op jit(solution)/shard_map/weights_ffn/ppermute | solution.py:57
  69.0 17.1 %collective-permute-start.10 = (bf16[128,1024]{1,0:T(8,128)(2,1)}, bf16[128,1024]{1,0:T(8,128)(2,1)S(1)}, u32[]{:S(2)}, u32[]{:S(2)}) collective-permute-start(bf16[128,1024]{1,0:T(8,128)(2,1)} %after.30), channel_id=1, source_target_pairs={{0,6},{2,4},{4,2},{6,0},{1,7},{3,5},{5,3},{7,1},{8,14},{10,12},{12... | collective-permute-start | bytes 786440 | tf_op jit(solution)/shard_map/tokens_cot/ppermute | solution.py:683
  71.3 23.2 %collective-permute-start.9 = (bf16[128,1024]{1,0:T(8,128)(2,1)}, bf16[128,1024]{1,0:T(8,128)(2,1)S(1)}, u32[]{:S(2)}, u32[]{:S(2)}) collective-permute-start(bf16[128,1024]{1,0:T(8,128)(2,1)} %after.30), channel_id=1, source_target_pairs={{0,4},{2,6},{4,0},{6,2},{1,5},{3,7},{5,1},{7,3},{8,12},{10,14},{12... | collective-permute-start | bytes 786440 | tf_op jit(solution)/shard_map/tokens_cot/ppermute | solution.py:683
  71.9 22.6 %collective-permute-start.8 = (bf16[128,1024]{1,0:T(8,128)(2,1)}, bf16[128,1024]{1,0:T(8,128)(2,1)}, u32[]{:S(2)}, u32[]{:S(2)}) collective-permute-start(bf16[128,1024]{1,0:T(8,128)(2,1)} %after.30), channel_id=1, source_target_pairs={{0,2},{2,0},{4,6},{6,4},{1,3},{3,1},{5,7},{7,5},{8,10},{10,8},{12,... | collective-permute-start | bytes 786440 | tf_op jit(solution)/shard_map/tokens_cot/ppermute | solution.py:683
  98.9 23.8 %collective-permute-start.15 = (bf16[256,896]{1,0:T(8,128)(2,1)}, bf16[256,896]{1,0:T(8,128)(2,1)S(1)}, u32[]{:S(2)}, u32[]{:S(2)}) collective-permute-start(bf16[256,896]{1,0:T(8,128)(2,1)} %after.32), channel_id=1, source_target_pairs={{0,8},{8,0},{1,9},{9,1},{2,10},{10,2},{3,11},{11,3},{4,12},{12,4},... | collective-permute-start | bytes 1376264 | tf_op jit(solution)/shard_map/weights_ffn/ppermute | solution.py:57
  100.5 22.3 %collective-permute-start.16 = (bf16[256,896]{1,0:T(8,128)(2,1)S(1)}, bf16[256,896]{1,0:T(8,128)(2,1)S(1)}, u32[]{:S(2)}, u32[]{:S(2)}) collective-permute-start(bf16[256,896]{1,0:T(8,128)(2,1)S(1)} %copy-done.16), channel_id=1, source_target_pairs={{0,16},{16,0},{1,17},{17,1},{2,18},{18,2},{3,19},{19,3},{4,20},{20... | collective-permute-start | bytes 1376264 | tf_op jit(solution)/shard_map/sum_attn/ppermute | solution.py:57
  105.3 19.0 %collective-permute-start.12 = (bf16[128,1024]{1,0:T(8,128)(2,1)}, bf16[128,1024]{1,0:T(8,128)(2,1)S(1)}, u32[]{:S(2)}, u32[]{:S(2)}) collective-permute-start(bf16[128,1024]{1,0:T(8,128)(2,1)} %get-tuple-element.62), channel_id=1, source_target_pairs={{0,2},{2,0},{4,6},{6,4},{1,3},{3,1},{5,7},{7,5},{8,10},{10,8},{12,... | collective-permute-start | bytes 786440 | tf_op jit(solution)/shard_map/sum_attn/ppermute | solution.py:792
  105.7 19.2 %collective-permute-start.13 = (bf16[128,1024]{1,0:T(8,128)(2,1)}, bf16[128,1024]{1,0:T(8,128)(2,1)S(1)}, u32[]{:S(2)}, u32[]{:S(2)}) collective-permute-start(bf16[128,1024]{1,0:T(8,128)(2,1)} %get-tuple-element.63), channel_id=1, source_target_pairs={{0,4},{2,6},{4,0},{6,2},{1,5},{3,7},{5,1},{7,3},{8,12},{10,14},{12... | collective-permute-start | bytes 786440 | tf_op jit(solution)/shard_map/sum_attn/ppermute | solution.py:792
  107.5 22.6 %collective-permute-start.14 = (bf16[128,1024]{1,0:T(8,128)(2,1)}, bf16[128,1024]{1,0:T(8,128)(2,1)S(1)}, u32[]{:S(2)}, u32[]{:S(2)}) collective-permute-start(bf16[128,1024]{1,0:T(8,128)(2,1)} %get-tuple-element.64), channel_id=1, source_target_pairs={{0,6},{2,4},{4,2},{6,0},{1,7},{3,5},{5,3},{7,1},{8,14},{10,12},{12... | collective-permute-start | bytes 786440 | tf_op jit(solution)/shard_map/sum_attn/ppermute | solution.py:792
  133.4 16.3 %all-to-all-start.3 = ((bf16[4,128,1024]{2,1,0:T(8,128)(2,1)}), bf16[4,128,1024]{2,1,0:T(8,128)(2,1)S(1)}, u32[]{:S(2)}, u32[]{:S(2)}) async-start(bf16[4,128,1024]{2,1,0:T(8,128)(2,1)} %broadcast_in_dim.19), calls=%async_computation.3 | async-start | bytes 2097152 | tf_op jit(solution)/shard_map/tokens_xf/all_to_all | solution.py:634
  182.8 17.8 %all-to-all-start.4 = ((bf16[4,128,1024]{2,1,0:T(8,128)(2,1)}), bf16[4,128,1024]{2,1,0:T(8,128)(2,1)S(1)}, u32[]{:S(2)}, u32[]{:S(2)}) async-start(bf16[4,128,1024]{2,1,0:T(8,128)(2,1)} %bitcast.39), calls=%async_computation.4 | async-start | bytes 2097152 | tf_op jit(solution)/shard_map/sum_dxf/all_to_all | solution.py:638
  186.4 13.4 %collective-permute-start.22 = (bf16[256,896]{1,0:T(8,128)(2,1)S(1)}, bf16[256,896]{1,0:T(8,128)(2,1)S(1)}, u32[]{:S(2)}, u32[]{:S(2)}) collective-permute-start(bf16[256,896]{1,0:T(8,128)(2,1)S(1)} %copy-done.64), channel_id=1, source_target_pairs={{0,16},{16,0},{1,17},{17,1},{2,18},{18,2},{3,19},{19,3},{4,20},{20... | collective-permute-start | bytes 1376264 | tf_op jit(solution)/shard_map/grads_ffn/ppermute | solution.py:57
  187.9 21.3 %collective-permute-start.27 = (bf16[256,896]{1,0:T(8,128)(2,1)}, bf16[256,896]{1,0:T(8,128)(2,1)}, u32[]{:S(2)}, u32[]{:S(2)}) collective-permute-start(bf16[256,896]{1,0:T(8,128)(2,1)} %get-tuple-element.77), channel_id=1, source_target_pairs={{0,16},{16,0},{1,17},{17,1},{2,18},{18,2},{3,19},{19,3},{4,20},{20... | collective-permute-start | bytes 1376264 | tf_op jit(solution)/shard_map/grads_ffn/ppermute | solution.py:57
  204.7 18.4 %collective-permute-start.24 = (bf16[128,1024]{1,0:T(8,128)(2,1)S(1)}, bf16[128,1024]{1,0:T(8,128)(2,1)S(1)}, u32[]{:S(2)}, u32[]{:S(2)}) collective-permute-start(bf16[128,1024]{1,0:T(8,128)(2,1)S(1)} %get-tuple-element.139), channel_id=1, source_target_pairs={{0,4},{2,6},{4,0},{6,2},{1,5},{3,7},{5,1},{7,3},{8,12},{10,14},{12... | collective-permute-start | bytes 786440 | tf_op jit(solution)/shard_map/tokens_dattn/ppermute | solution.py:683
  206.1 18.9 %collective-permute-start.23 = (bf16[128,1024]{1,0:T(8,128)(2,1)S(1)}, bf16[128,1024]{1,0:T(8,128)(2,1)S(1)}, u32[]{:S(2)}, u32[]{:S(2)}) collective-permute-start(bf16[128,1024]{1,0:T(8,128)(2,1)S(1)} %get-tuple-element.139), channel_id=1, source_target_pairs={{0,6},{2,4},{4,2},{6,0},{1,7},{3,5},{5,3},{7,1},{8,14},{10,12},{12... | collective-permute-start | bytes 786440 | tf_op jit(solution)/shard_map/tokens_dattn/ppermute | solution.py:683
  206.5 21.9 %collective-permute-start.26 = (bf16[256,896]{1,0:T(8,128)(2,1)S(1)}, bf16[256,896]{1,0:T(8,128)(2,1)S(1)}, u32[]{:S(2)}, u32[]{:S(2)}) collective-permute-start(bf16[256,896]{1,0:T(8,128)(2,1)S(1)} %add_convert_fusion.3), channel_id=1, source_target_pairs={{0,8},{8,0},{1,9},{9,1},{2,10},{10,2},{3,11},{11,3},{4,12},{12,4},... | collective-permute-start | bytes 1376264 | tf_op jit(solution)/shard_map/grads_ffn/ppermute | solution.py:57
  229.1 36.5 %all-to-all-start.5 = ((bf16[4,128,1024]{2,1,0:T(8,128)(2,1)}), bf16[4,128,1024]{2,1,0:T(8,128)(2,1)S(1)}, u32[]{:S(2)}, u32[]{:S(2)}) async-start(bf16[4,128,1024]{2,1,0:T(8,128)(2,1)} %bitcast.111), calls=%async_computation.5 | async-start | bytes 2097152 | tf_op jit(solution)/shard_map/sum_out/all_to_all | solution.py:836
  232.9 22.3 %collective-permute-start.29 = (bf16[256,896]{1,0:T(8,128)(2,1)}, bf16[256,896]{1,0:T(8,128)(2,1)}, u32[]{:S(2)}, u32[]{:S(2)}) collective-permute-start(bf16[256,896]{1,0:T(8,128)(2,1)} %add_convert_fusion.2.refs_2_), channel_id=1, source_target_pairs={{0,8},{8,0},{1,9},{9,1},{2,10},{10,2},{3,11},{11,3},{4,12},{12,4},... | collective-permute-start | bytes 1376264 | tf_op jit(solution)/shard_map/grads_ffn/ppermute | solution.py:57
  234.4 33.1 %collective-permute-start.32 = (bf16[256,1792]{1,0:T(8,128)(2,1)}, bf16[256,1792]{1,0:T(8,128)(2,1)S(1)}, u32[]{:S(2)}, u32[]{:S(2)}) collective-permute-start(bf16[256,1792]{1,0:T(8,128)(2,1)} %after.44), channel_id=1, source_target_pairs={{0,16},{16,0},{1,17},{17,1},{2,18},{18,2},{3,19},{19,3},{4,20},{20... | collective-permute-start | bytes 2752520 | tf_op jit(solution)/shard_map/grads_ffn/ppermute | solution.py:57
  265.1 33.8 %collective-permute-start.35 = (bf16[256,384]{1,0:T(8,128)(2,1)}, bf16[256,384]{1,0:T(8,128)(2,1)}, u32[]{:S(2)}, u32[]{:S(2)}) collective-permute-start(bf16[256,384]{1,0:T(8,128)(2,1)} %get-tuple-element.85.refs_2_), channel_id=1, source_target_pairs={{0,16},{16,0},{1,17},{17,1},{2,18},{18,2},{3,19},{19,3},{4,20},{20... | collective-permute-start | bytes 589832 | tf_op jit(solution)/shard_map/grads_attn/ppermute | solution.py:57
  273.7 24.1 %all-to-all-start.6 = ((bf16[4,128,1024]{2,1,0:T(8,128)(2,1)}), bf16[4,128,1024]{2,1,0:T(8,128)(2,1)S(1)}, u32[]{:S(2)}, u32[]{:S(2)}) async-start(bf16[4,128,1024]{2,1,0:T(8,128)(2,1)} %bitcast.104), calls=%async_computation.6 | async-start | bytes 2097152 | tf_op jit(solution)/shard_map/sum_dxa/all_to_all | solution.py:638
  279.4 16.9 %collective-permute-start.37 = (bf16[264,384]{1,0:T(8,128)(2,1)S(1)}, bf16[264,384]{1,0:T(8,128)(2,1)S(1)}, u32[]{:S(2)}, u32[]{:S(2)}) collective-permute-start(bf16[264,384]{1,0:T(8,128)(2,1)S(1)} %pad_maximum_fusion.10), channel_id=1, source_target_pairs={{0,8},{8,0},{1,9},{9,1},{2,10},{10,2},{3,11},{11,3},{4,12},{12,4},... | collective-permute-start | bytes 608264 | tf_op jit(solution)/shard_map/grads_attn/ppermute | solution.py:57
  285.3 21.0 %collective-permute-start.38 = (bf16[64,1792]{1,0:T(8,128)(2,1)}, bf16[64,1792]{1,0:T(8,128)(2,1)S(1)}, u32[]{:S(2)}, u32[]{:S(2)}) collective-permute-start(bf16[64,1792]{1,0:T(8,128)(2,1)} %get-tuple-element.94), channel_id=1, source_target_pairs={{0,2},{2,0},{4,6},{6,4},{1,3},{3,1},{5,7},{7,5},{8,10},{10,8},{12,... | collective-permute-start | bytes 688136 | tf_op jit(solution)/shard_map/grads_ffn/ppermute | solution.py:890
  287.3 19.1 %collective-permute-start.39 = (bf16[64,1792]{1,0:T(8,128)(2,1)}, bf16[64,1792]{1,0:T(8,128)(2,1)S(1)}, u32[]{:S(2)}, u32[]{:S(2)}) collective-permute-start(bf16[64,1792]{1,0:T(8,128)(2,1)} %get-tuple-element.95), channel_id=1, source_target_pairs={{0,4},{2,6},{4,0},{6,2},{1,5},{3,7},{5,1},{7,3},{8,12},{10,14},{12... | collective-permute-start | bytes 688136 | tf_op jit(solution)/shard_map/grads_ffn/ppermute | solution.py:890
  288.7 20.2 %collective-permute-start.40 = (bf16[64,1792]{1,0:T(8,128)(2,1)}, bf16[64,1792]{1,0:T(8,128)(2,1)S(1)}, u32[]{:S(2)}, u32[]{:S(2)}) collective-permute-start(bf16[64,1792]{1,0:T(8,128)(2,1)} %get-tuple-element.96), channel_id=1, source_target_pairs={{0,6},{2,4},{4,2},{6,0},{1,7},{3,5},{5,3},{7,1},{8,14},{10,12},{12... | collective-permute-start | bytes 688136 | tf_op jit(solution)/shard_map/grads_ffn/ppermute | solution.py:890
  305.6 13.3 %collective-permute-start.33 = (bf16[2,128,1024]{2,1,0:T(8,128)(2,1)S(1)}, bf16[2,128,1024]{2,1,0:T(8,128)(2,1)S(1)}, u32[]{:S(2)}, u32[]{:S(2)}) collective-permute-start(bf16[2,128,1024]{2,1,0:T(8,128)(2,1)S(1)} %pad_maximum_fusion.4), channel_id=1, source_target_pairs={{0,0},{1,8},{8,1},{9,9},{2,2},{3,10},{10,3},{11,11},{4,4},{5,12},{... | collective-permute-start | bytes 1572872 | tf_op jit(solution)/shard_map/return/ppermute | solution.py:625
  (99 other events, 786.5 us)

commit v3 on v2

--- a/solution.py
+++ b/solution.py
@@ -451,6 +451,47 @@
     )(place, a, b)
 
 
+def pack_kernel(qw, wq_ref, wk_ref, wv_ref, wo_ref, g0_ref, g1_ref, pos_ref, out_ref):
+    places, height, wide = out_ref.shape
+    shard = wq_ref.shape[0]
+
+    def row(*parts):
+        parts = [p.astype(F32) for p in parts]
+        parts.append(jnp.zeros((1, wide - sum(p.shape[1] for p in parts)), F32))
+        return jnp.concatenate(parts, 1)
+
+    pos = pos_ref[...]
+    high = lax.shift_right_logical(pos, 8)
+    low = pos - high * 256
+    index = lax.broadcasted_iota(jnp.int32, (height - shard, wide), 0)
+    extra = jnp.where(index == 0, row(g0_ref[...], g1_ref[...]), 0.0)
+    for n, part in ((1, high), (2, low)):
+        extra = jnp.where(index == n, row(*(part[m : m + 1] for m in range(part.shape[0]))), extra)
+    extra = extra.astype(BF)
+    for p in range(places):
+        wide_at = slice(p * qw, (p + 1) * qw)
+        at = slice(p * HEAD_DIM, (p + 1) * HEAD_DIM)
+        out_ref[p, :shard, :qw] = wq_ref[:, wide_at]
+        out_ref[p, :shard, qw : qw + 2 * HEAD_DIM] = jnp.concatenate(
+            [wk_ref[:, at], wv_ref[:, at]], 1
+        )
+        out_ref[p, :shard, qw + 2 * HEAD_DIM :] = wo_ref[:, wide_at]
+        out_ref[p, shard:, :] = extra
+
+
+def pack_call(qw, places, wide, *arrays):
+    vmem = pl.BlockSpec(memory_space=pltpu.VMEM)
+    return pl.pallas_call(
+        functools.partial(pack_kernel, qw),
+        in_specs=[vmem] * 7,
+        out_specs=vmem,
+        out_shape=jax.ShapeDtypeStruct((places, arrays[0].shape[0] + 8, wide), BF),
+        compiler_params=pltpu.CompilerParams(vmem_limit_bytes=VMEM_BYTES),
+        cost_estimate=SMALL_COST,
+        name="pack",
+    )(*arrays)
+
+
 def attn_grad_kernel(x0_ref, x1_ref, g0_ref, g1_ref, raw_ref, mixed_ref, *outs):
     side = x0_ref.shape[0]
     wide = raw_ref.shape[1]
@@ -643,30 +684,11 @@
     w_output_t = w_output.T
     w_down_t = w_down.T
     wide = 2 * qw + 2 * HEAD_DIM
-    pos = positions[:, 0].reshape(1, H * rows)
-    high = pos // 256
-    extra = [jnp.concatenate([attn_gain, ffn_gain])[None], high.astype(BF), (pos - high * 256).astype(BF)]
-    extra = [jnp.pad(e, ((0, 0), (0, wide - e.shape[1]))) for e in extra]
-    extra = jnp.pad(jnp.concatenate(extra, 0), ((0, 5), (0, 0)))
-    pack = [
-        jnp.concatenate(
-            [
-                jnp.concatenate(
-                    [
-                        cut(w_query, p, qw),
-                        cut(w_key, p, HEAD_DIM),
-                        cut(w_value, p, HEAD_DIM),
-                        cut(w_output_t, p, qw),
-                    ],
-                    1,
-                ),
-                extra,
-            ],
-            0,
-        )
-        for p in range(J)
-    ]
-    own = exchange("weights_attn", jnp.stack(pack))
+    gains = attn_gain[None], ffn_gain[None]
+    sent = pack_call(
+        qw, J, wide, w_query, w_key, w_value, w_output_t, *gains, positions.reshape(H, rows)
+    )
+    own = exchange("weights_attn", sent)
     pack = [
         jnp.pad(
             jnp.concatenate([cut(w_gate, p, fw), cut(w_up, p, fw), cut(w_down_t, p, fw)], 1),

time: 327 us -> 324 us (level)
    unnamed x165 -> x161, local copies, waits for them, and re-layouts: 18 us -> 18.8 us
  transfers between devices with their start and end apart: 50 -> 50, of which waited for: 20 -> 21; matrix products, arithmetic and copies ran while one was open for 14% -> 14% of each run, Pallas kernels for 19% -> 19%
where the time goes in v3:
time: 324 us; the launch traced here: 322 us
  waiting for transfers between devices  93.7 us (29%)
  starting transfers between devices  80.5 us (25%)
  Pallas kernels  73 us (23%)
  other arithmetic  35.2 us (11%)
  local copies, waits for them, and re-layouts  33.8 us (10%)
  matrix products  3.82 us (1%)
    ppermute x27, waiting for transfers between devices, swap(): return lax.ppermute(v, axis, [(0, 1), (1, 0)])  51 us
    ppermute x27, starting transfers between devices, swap(): return lax.ppermute(v, axis, [(0, 1), (1, 0)])  26.8 us
    ppermute x6, waiting for transfers between devices, share(): lax.ppermute(block, 'j', [(i, i ^ d) for i in range(J)])  21.8 us
    unnamed x161, local copies, waits for them, and re-layouts  18.8 us
    pallas_call x2, Pallas kernels, ffn_call(): pl.pallas_call(functools.partial(ffn_kernel, fw, part), grid=(count // ti...  17.2 us
    pallas_call x2, Pallas kernels, ffn_grad_call(): pl.pallas_call(functools.partial(ffn_grad_kernel, fw, width, whole), grid...  12.9 us
    pallas_call x1, Pallas kernels, attend_back_call(): pl.pallas_call(functools.partial(attend_back_kernel, tile, tiles), in_spe...  11.7 us
    all_to_all x2, starting transfers between devices, gather_half(): return lax.all_to_all(sent, 'j', 0, 0).reshape(side, d_model)  10.1 us
  transfers between devices with their start and end apart: 50, of which 21 were waited for; matrix products, arithmetic and copies ran while one was open for 14% of the time, Pallas kernels for 19%

profile of v3, /device:TPU:0, one launch (start us, length us, event | category | flops | bytes accessed | tf_op | source)
XLA Modules:
  0.0 321.9 jit_solution(10643426572957640427)
XLA Ops:
  2.5 5.2 %all-to-all-start.2 = ((bf16[4,72,384]{2,1,0:T(8,128)(2,1)}), bf16[4,72,384]{2,1,0:T(8,128)(2,1)S(1)}, u32[]{:S(2)}, u32[]{:S(2)}) async-start(bf16[4,72,384]{2,1,0:T(8,128)(2,1)} %pack.1), calls=%async_computation.2 | async-start | bytes 442368 | tf_op jit(solution)/shard_map/weights_attn/all_to_all | solution.py:633
  15.5 4.2 %all-to-all-start = ((bf16[4,64,1792]{2,1,0:T(8,128)(2,1)}), bf16[4,64,1792]{2,1,0:T(8,128)(2,1)S(1)}, u32[]{:S(2)}, u32[]{:S(2)}) async-start(bf16[4,64,1792]{2,1,0:T(8,128)(2,1)} %pad_maximum_fusion.2), calls=%async_computation | async-start | bytes 1835008 | tf_op jit(solution)/shard_map/weights_ffn/all_to_all | solution.py:633
  21.3 6.4 %collective-permute-start.1 = (bf16[4,72,384]{2,1,0:T(8,128)(2,1)S(1)}, bf16[4,72,384]{2,1,0:T(8,128)(2,1)S(1)}, u32[]{:S(2)}, u32[]{:S(2)}) collective-permute-start(bf16[4,72,384]{2,1,0:T(8,128)(2,1)S(1)} %all-to-all-done.2), channel_id=1, source_target_pairs={{0,8},{8,0},{1,9},{9,1},{2,10},{10,2},{3,11},{11,3},{4,12},{12,4},... | collective-permute-start | bytes 663560 | tf_op jit(solution)/shard_map/weights_attn/ppermute | solution.py:57
  27.7 7.6 %collective-permute-done.1.refs_1_ = bf16[4,72,384]{2,1,0:T(8,128)(2,1)S(1)} collective-permute-done((bf16[4,72,384]{2,1,0:T(8,128)(2,1)S(1)}, bf16[4,72,384]{2,1,0:T(8,128)(2,1)S(1)}, u32[]{:S(2)}, u32[]{:S(2)}) %collective-permute-start.1) | collective-permute-done | bytes 221216 | tf_op jit(solution)/shard_map/weights_attn/ppermute | solution.py:57
  41.4 6.4 %all-to-all-start.1 = ((bf16[4,128,1024]{2,1,0:T(8,128)(2,1)}), bf16[4,128,1024]{2,1,0:T(8,128)(2,1)S(1)}, u32[]{:S(2)}, u32[]{:S(2)}) async-start(bf16[4,128,1024]{2,1,0:T(8,128)(2,1)} %after.25), calls=%async_computation.1 | async-start | bytes 2097152 | tf_op jit(solution)/shard_map/tokens_hidden/all_to_all | solution.py:675
  47.9 3.1 multiply_sine_fusion
  56.1 6.5 %all-to-all-done.1 = bf16[4,128,1024]{2,1,0:T(8,128)(2,1)S(1)} async-done(((bf16[4,128,1024]{2,1,0:T(8,128)(2,1)}), bf16[4,128,1024]{2,1,0:T(8,128)(2,1)S(1)}, u32[]{:S(2)}, u32[]{:S(2)}) %all-to-all-start.1) | async-done | bytes 1048608 | tf_op jit(solution)/shard_map/tokens_hidden/all_to_all | solution.py:675
  71.3 6.1 %qkv.1 = (bf16[512,1024]{1,0:T(8,128)(2,1)}, bf16[512,1024]{1,0:T(8,128)(2,1)}, f32[1024,256]{1,0:T(8,128)}, bf16[1024,256]{1,0:T(8,128)(2,1)}) custom-call(bf16[512,1024]{1,0:T(8,128)(2,1)} %after.27.h0_ref.refs_1_, bf16[512,1024]{1,0:T(8,128)(2,1)} %collective-permute-done.5.h1_ref, f32[1,1024]{1,0:T(1,128)} %slice.290.gain_ref, ...), custom_call_target="tpu_custom_call" | custom-call | flops 1 | bytes 1 | tf_op jit(solution)/shard_map/qkv/pallas_call | solution.py:155
  77.4 6.3 %attend.1 = (bf16[1024,128]{1,0:T(8,128)(2,1)}, bf16[10,512,256]{2,1,0:T(8,128)(2,1)}) custom-call(s32[2]{0:T(128)} %pad_add_fusion.refs_6_.at_ref, bf16[1024,256]{1,0:T(8,128)(2,1)} %get-tuple-element.59.qkv_ref), custom_call_target="tpu_custom_call" | custom-call | flops 1 | bytes 1 | tf_op jit(solution)/shard_map/attend/pallas_call | solution.py:215
  84.0 7.8 %collective-permute-done.9.refs_4_ = bf16[128,1024]{1,0:T(8,128)(2,1)S(1)} collective-permute-done((bf16[128,1024]{1,0:T(8,128)(2,1)}, bf16[128,1024]{1,0:T(8,128)(2,1)S(1)}, u32[]{:S(2)}, u32[]{:S(2)}) %collective-permute-start.9) | collective-permute-done | bytes 262176 | tf_op jit(solution)/shard_map/tokens_cot/ppermute | solution.py:705
  100.0 2.7 add_cut.1
  106.9 13.2 %collective-permute-done.15.refs_1_.refs_4_ = bf16[256,896]{1,0:T(8,128)(2,1)S(1)} collective-permute-done((bf16[256,896]{1,0:T(8,128)(2,1)}, bf16[256,896]{1,0:T(8,128)(2,1)S(1)}, u32[]{:S(2)}, u32[]{:S(2)}) %collective-permute-start.15) | collective-permute-done | bytes 458784 | tf_op jit(solution)/shard_map/weights_ffn/ppermute | solution.py:57
  122.2 5.4 %collective-permute-done.14 = bf16[128,1024]{1,0:T(8,128)(2,1)S(1)} collective-permute-done((bf16[128,1024]{1,0:T(8,128)(2,1)}, bf16[128,1024]{1,0:T(8,128)(2,1)S(1)}, u32[]{:S(2)}, u32[]{:S(2)}) %collective-permute-start.14) | collective-permute-done | bytes 262176 | tf_op jit(solution)/shard_map/sum_attn/ppermute | solution.py:814
  130.9 3.7 %all-to-all-start.3 = ((bf16[4,128,1024]{2,1,0:T(8,128)(2,1)}), bf16[4,128,1024]{2,1,0:T(8,128)(2,1)S(1)}, u32[]{:S(2)}, u32[]{:S(2)}) async-start(bf16[4,128,1024]{2,1,0:T(8,128)(2,1)} %broadcast_in_dim.22), calls=%async_computation.3 | async-start | bytes 2097152 | tf_op jit(solution)/shard_map/tokens_xf/all_to_all | solution.py:675
  138.0 7.8 %collective-permute-done.17.refs_1_.refs_5_ = bf16[256,896]{1,0:T(8,128)(2,1)S(1)} collective-permute-done((bf16[256,896]{1,0:T(8,128)(2,1)S(1)}, bf16[256,896]{1,0:T(8,128)(2,1)S(1)}, u32[]{:S(2)}, u32[]{:S(2)}) %collective-permute-start.17) | collective-permute-done | bytes 458784 | tf_op jit(solution)/shard_map/weights_ffn/ppermute | solution.py:57
  150.4 8.6 %ffn.2 = (bf16[512,576]{1,0:T(8,128)(2,1)}, bf16[512,1152]{1,0:T(8,128)(2,1)}, bf16[512,1024]{1,0:T(8,128)(2,1)}, bf16[512,1024]{1,0:T(8,128)(2,1)}) custom-call(bf16[512,1024]{1,0:T(8,128)(2,1)} %after.34.x_ref.refs_0_, bf16[512,1024]{1,0:T(8,128)(2,1)} %copy-done.6, bf16[256,896]{1,0:T(8,128)(2,1)} %copy-done.14, bf16[256,896]{1,0:T(8,128)(2,1)} %copy-done.15, ...), custom_call_target="tpu_custom_call" | custom-call | flops 1 | bytes 1 | tf_op jit(solution)/shard_map/ffn/pallas_call | solution.py:352
  160.3 8.6 %ffn.3 = (bf16[512,576]{1,0:T(8,128)(2,1)}, bf16[512,1152]{1,0:T(8,128)(2,1)}, bf16[512,1024]{1,0:T(8,128)(2,1)}, bf16[512,1024]{1,0:T(8,128)(2,1)}) custom-call(bf16[512,1024]{1,0:T(8,128)(2,1)} %after.35.x_ref, bf16[512,1024]{1,0:T(8,128)(2,1)} %collective-permute-done.19.cot_ref.refs_3_, bf16[256,896]{1,0:T(8,128)(2,1)} %copy-done.14, ...), custom_call_target="tpu_custom_call" | custom-call | flops 1 | bytes 1 | tf_op jit(solution)/shard_map/ffn/pallas_call | solution.py:352
  169.4 6.5 %ffn_grad.2 = (bf16[256,1792]{1,0:T(8,128)(2,1)}, bf16[256,896]{1,0:T(8,128)(2,1)}, bf16[256,896]{1,0:T(8,128)(2,1)}) custom-call(bf16[512,1024]{1,0:T(8,128)(2,1)} %after.34.x_ref.refs_0_, bf16[512,1024]{1,0:T(8,128)(2,1)} %copy-done.9, bf16[512,1024]{1,0:T(8,128)(2,1)} %copy-done.6, bf16[512,1024]{1,0:T(8,128)(2,1)} %collective-permute-done.19.cot_ref.refs_3_, ...), custom_call_target="tpu_custom_call" | custom-call | flops 1 | bytes 1 | tf_op jit(solution)/shard_map/ffn_grad/pallas_call | solution.py:402
  180.2 3.5 %all-to-all-start.4 = ((bf16[4,128,1024]{2,1,0:T(8,128)(2,1)}), bf16[4,128,1024]{2,1,0:T(8,128)(2,1)S(1)}, u32[]{:S(2)}, u32[]{:S(2)}) async-start(bf16[4,128,1024]{2,1,0:T(8,128)(2,1)} %bitcast.36), calls=%async_computation.4 | async-start | bytes 2097152 | tf_op jit(solution)/shard_map/sum_dxf/all_to_all | solution.py:679
  185.9 6.5 %ffn_grad.3 = (bf16[256,896]{1,0:T(8,128)(2,1)}, bf16[256,896]{1,0:T(8,128)(2,1)}, bf16[256,896]{1,0:T(8,128)(2,1)}, bf16[256,896]{1,0:T(8,128)(2,1)}) custom-call(bf16[512,1024]{1,0:T(8,128)(2,1)} %after.34.x_ref.refs_0_, bf16[512,1024]{1,0:T(8,128)(2,1)} %copy-done.9, bf16[512,1024]{1,0:T(8,128)(2,1)} %copy-done.6, ...), custom_call_target="tpu_custom_call" | custom-call | flops 1 | bytes 1 | tf_op jit(solution)/shard_map/ffn_grad/pallas_call | solution.py:402
  208.6 11.8 %collective-permute-done.24 = bf16[128,1024]{1,0:T(8,128)(2,1)S(1)} collective-permute-done((bf16[128,1024]{1,0:T(8,128)(2,1)S(1)}, bf16[128,1024]{1,0:T(8,128)(2,1)S(1)}, u32[]{:S(2)}, u32[]{:S(2)}) %collective-permute-start.24) | collective-permute-done | bytes 262176 | tf_op jit(solution)/shard_map/tokens_dattn/ppermute | solution.py:705
  226.6 3.7 %all-to-all-start.5 = ((bf16[4,128,1024]{2,1,0:T(8,128)(2,1)}), bf16[4,128,1024]{2,1,0:T(8,128)(2,1)S(1)}, u32[]{:S(2)}, u32[]{:S(2)}) async-start(bf16[4,128,1024]{2,1,0:T(8,128)(2,1)} %bitcast.90), calls=%async_computation.5 | async-start | bytes 2097152 | tf_op jit(solution)/shard_map/sum_out/all_to_all | solution.py:858
  234.0 11.7 %attend_back.1 = (bf16[1024,256]{1,0:T(8,128)(2,1)}, f32[8,128]{1,0:T(8,128)}, bf16[256,1024]{1,0:T(8,128)(2,1)}, bf16[256,1024]{1,0:T(8,128)(2,1)}, bf16[512,1024]{1,0:T(8,128)(2,1)}) custom-call(s32[2]{0:T(128)} %pad_add_fusion.refs_6_.at_ref, bf16[1024,256]{1,0:T(8,128)(2,1)} %get-tuple-element.59.qkv_ref, bf16[1024,128]{1,0:T(8,128)(2,1)} %after.31.mixed_ref, ...), custom_call_target="tpu_custom_call" | custom-call | flops 1 | bytes 1 | tf_op jit(solution)/shard_map/attend_back/pallas_call | solution.py:300
  245.8 6.9 %collective-permute-done.29.refs_1_.got_a = bf16[256,896]{1,0:T(8,128)(2,1)} collective-permute-done((bf16[256,896]{1,0:T(8,128)(2,1)}, bf16[256,896]{1,0:T(8,128)(2,1)}, u32[]{:S(2)}, u32[]{:S(2)}) %collective-permute-start.29) | collective-permute-done | bytes 458784 | tf_op jit(solution)/shard_map/grads_ffn/ppermute | solution.py:57
  253.1 5.3 %attn_grad.1 = (bf16[256,384]{1,0:T(8,128)(2,1)}, bf16[256,384]{1,0:T(8,128)(2,1)}, bf16[256,384]{1,0:T(8,128)(2,1)}, bf16[256,384]{1,0:T(8,128)(2,1)}) custom-call(bf16[512,1024]{1,0:T(8,128)(2,1)} %get-tuple-element.83.x0_ref, bf16[512,1024]{1,0:T(8,128)(2,1)} %get-tuple-element.84.x1_ref, bf16[512,1024]{1,0:T(8,128)(2,1)} %after.38.refs_1_.g0_ref, ...), custom_call_target="tpu_custom_call" | custom-call | flops 1 | bytes 1 | tf_op jit(solution)/shard_map/attn_grad/pallas_call | solution.py:513
  266.6 2.8 add.201.refs_1_
  271.2 5.6 %all-to-all-start.6 = ((bf16[4,128,1024]{2,1,0:T(8,128)(2,1)}), bf16[4,128,1024]{2,1,0:T(8,128)(2,1)S(1)}, u32[]{:S(2)}, u32[]{:S(2)}) async-start(bf16[4,128,1024]{2,1,0:T(8,128)(2,1)} %bitcast.83), calls=%async_computation.6 | async-start | bytes 2097152 | tf_op jit(solution)/shard_map/sum_dxa/all_to_all | solution.py:679
  279.8 2.9 merge.1
  286.2 7.5 %collective-permute-done.37.refs_0_ = bf16[264,384]{1,0:T(8,128)(2,1)S(1)} collective-permute-done((bf16[264,384]{1,0:T(8,128)(2,1)S(1)}, bf16[264,384]{1,0:T(8,128)(2,1)S(1)}, u32[]{:S(2)}, u32[]{:S(2)}) %collective-permute-start.37) | collective-permute-done | bytes 202784 | tf_op jit(solution)/shard_map/grads_attn/ppermute | solution.py:57
  298.2 4.4 %all-to-all-start.7 = ((bf16[4,64,512]{2,1,0:T(8,128)(2,1)}), bf16[4,64,512]{2,1,0:T(8,128)(2,1)S(1)}, u32[]{:S(2)}, u32[]{:S(2)}) async-start(bf16[4,64,512]{2,1,0:T(8,128)(2,1)} %pad_maximum_fusion.7), calls=%async_computation.7 | async-start | bytes 524288 | tf_op jit(solution)/shard_map/grads/all_to_all | solution.py:935
  306.4 3.0 all-to-all-done.7.got_ref
  310.0 3.3 %final.1 = (f32[64,512]{1,0:T(8,128)}, f32[64,256]{1,0:T(8,128)}, f32[64,256]{1,0:T(8,128)}, f32[64,512]{1,0:T(8,128)}, f32[64,2304]{1,0:T(8,128)}, /*index=5*/f...) custom-call(s32[1]{0:T(128)} %bitcast.1.place_ref, bf16[4,64,512]{2,1,0:T(8,128)(2,1)} %copy-done.46, ...), custom_call_target="tpu_custom_call" | custom-call | flops 1 | bytes 1 | tf_op jit(solution)/shard_map/final/pallas_call | solution.py:585
  (381 shorter events, 125.3 us)
Async XLA Ops:
  15.5 24.6 %all-to-all-start = ((bf16[4,64,1792]{2,1,0:T(8,128)(2,1)}), bf16[4,64,1792]{2,1,0:T(8,128)(2,1)S(1)}, u32[]{:S(2)}, u32[]{:S(2)}) async-start(bf16[4,64,1792]{2,1,0:T(8,128)(2,1)} %pad_maximum_fusion.2), calls=%async_computation | async-start | bytes 1835008 | tf_op jit(solution)/shard_map/weights_ffn/all_to_all | solution.py:633
  19.7 20.3 %collective-permute-start.2 = (bf16[4,72,384]{2,1,0:T(8,128)(2,1)S(1)}, bf16[4,72,384]{2,1,0:T(8,128)(2,1)S(1)}, u32[]{:S(2)}, u32[]{:S(2)}) collective-permute-start(bf16[4,72,384]{2,1,0:T(8,128)(2,1)S(1)} %all-to-all-done.2), channel_id=1, source_target_pairs={{0,16},{16,0},{1,17},{17,1},{2,18},{18,2},{3,19},{19,3},{4,20},{20... | collective-permute-start | bytes 663560 | tf_op jit(solution)/shard_map/weights_attn/ppermute | solution.py:57
  21.3 14.0 %collective-permute-start.1 = (bf16[4,72,384]{2,1,0:T(8,128)(2,1)S(1)}, bf16[4,72,384]{2,1,0:T(8,128)(2,1)S(1)}, u32[]{:S(2)}, u32[]{:S(2)}) collective-permute-start(bf16[4,72,384]{2,1,0:T(8,128)(2,1)S(1)} %all-to-all-done.2), channel_id=1, source_target_pairs={{0,8},{8,0},{1,9},{9,1},{2,10},{10,2},{3,11},{11,3},{4,12},{12,4},... | collective-permute-start | bytes 663560 | tf_op jit(solution)/shard_map/weights_attn/ppermute | solution.py:57
  36.8 18.4 %collective-permute-start.4 = (bf16[128,1024]{1,0:T(8,128)(2,1)}, bf16[128,1024]{1,0:T(8,128)(2,1)S(1)}, u32[]{:S(2)}, u32[]{:S(2)}) collective-permute-start(bf16[128,1024]{1,0:T(8,128)(2,1)} %after.26), channel_id=1, source_target_pairs={{0,0},{1,8},{8,1},{9,9},{2,2},{3,10},{10,3},{11,11},{4,4},{5,12},{... | collective-permute-start | bytes 786440 | tf_op jit(solution)/shard_map/fetch_cot/ppermute | solution.py:662
  41.4 21.2 %all-to-all-start.1 = ((bf16[4,128,1024]{2,1,0:T(8,128)(2,1)}), bf16[4,128,1024]{2,1,0:T(8,128)(2,1)S(1)}, u32[]{:S(2)}, u32[]{:S(2)}) async-start(bf16[4,128,1024]{2,1,0:T(8,128)(2,1)} %after.25), calls=%async_computation.1 | async-start | bytes 2097152 | tf_op jit(solution)/shard_map/tokens_hidden/all_to_all | solution.py:675
  64.9 26.9 %collective-permute-start.7 = (bf16[256,1792]{1,0:T(8,128)(2,1)}, bf16[256,1792]{1,0:T(8,128)(2,1)S(1)}, u32[]{:S(2)}, u32[]{:S(2)}) collective-permute-start(bf16[256,1792]{1,0:T(8,128)(2,1)} %after.29), channel_id=1, source_target_pairs={{0,16},{16,0},{1,17},{17,1},{2,18},{18,2},{3,19},{19,3},{4,20},{20... | collective-permute-start | bytes 2752520 | tf_op jit(solution)/shard_map/weights_ffn/ppermute | solution.py:57
  66.7 25.0 %collective-permute-start.6 = (bf16[256,896]{1,0:T(8,128)(2,1)}, bf16[256,896]{1,0:T(8,128)(2,1)S(1)}, u32[]{:S(2)}, u32[]{:S(2)}) collective-permute-start(bf16[256,896]{1,0:T(8,128)(2,1)} %after.28), channel_id=1, source_target_pairs={{0,8},{8,0},{1,9},{9,1},{2,10},{10,2},{3,11},{11,3},{4,12},{12,4},... | collective-permute-start | bytes 1376264 | tf_op jit(solution)/shard_map/weights_ffn/ppermute | solution.py:57
  67.1 16.9 %collective-permute-start.10 = (bf16[128,1024]{1,0:T(8,128)(2,1)}, bf16[128,1024]{1,0:T(8,128)(2,1)S(1)}, u32[]{:S(2)}, u32[]{:S(2)}) collective-permute-start(bf16[128,1024]{1,0:T(8,128)(2,1)} %after.30), channel_id=1, source_target_pairs={{0,6},{2,4},{4,2},{6,0},{1,7},{3,5},{5,3},{7,1},{8,14},{10,12},{12... | collective-permute-start | bytes 786440 | tf_op jit(solution)/shard_map/tokens_cot/ppermute | solution.py:705
  68.6 23.1 %collective-permute-start.9 = (bf16[128,1024]{1,0:T(8,128)(2,1)}, bf16[128,1024]{1,0:T(8,128)(2,1)S(1)}, u32[]{:S(2)}, u32[]{:S(2)}) collective-permute-start(bf16[128,1024]{1,0:T(8,128)(2,1)} %after.30), channel_id=1, source_target_pairs={{0,4},{2,6},{4,0},{6,2},{1,5},{3,7},{5,1},{7,3},{8,12},{10,14},{12... | collective-permute-start | bytes 786440 | tf_op jit(solution)/shard_map/tokens_cot/ppermute | solution.py:705
  69.8 22.0 %collective-permute-start.8 = (bf16[128,1024]{1,0:T(8,128)(2,1)}, bf16[128,1024]{1,0:T(8,128)(2,1)}, u32[]{:S(2)}, u32[]{:S(2)}) collective-permute-start(bf16[128,1024]{1,0:T(8,128)(2,1)} %after.30), channel_id=1, source_target_pairs={{0,2},{2,0},{4,6},{6,4},{1,3},{3,1},{5,7},{7,5},{8,10},{10,8},{12,... | collective-permute-start | bytes 786440 | tf_op jit(solution)/shard_map/tokens_cot/ppermute | solution.py:705
  96.1 23.9 %collective-permute-start.15 = (bf16[256,896]{1,0:T(8,128)(2,1)}, bf16[256,896]{1,0:T(8,128)(2,1)S(1)}, u32[]{:S(2)}, u32[]{:S(2)}) collective-permute-start(bf16[256,896]{1,0:T(8,128)(2,1)} %after.32), channel_id=1, source_target_pairs={{0,8},{8,0},{1,9},{9,1},{2,10},{10,2},{3,11},{11,3},{4,12},{12,4},... | collective-permute-start | bytes 1376264 | tf_op jit(solution)/shard_map/weights_ffn/ppermute | solution.py:57
  97.8 22.2 %collective-permute-start.16 = (bf16[256,896]{1,0:T(8,128)(2,1)S(1)}, bf16[256,896]{1,0:T(8,128)(2,1)S(1)}, u32[]{:S(2)}, u32[]{:S(2)}) collective-permute-start(bf16[256,896]{1,0:T(8,128)(2,1)S(1)} %copy-done.16), channel_id=1, source_target_pairs={{0,16},{16,0},{1,17},{17,1},{2,18},{18,2},{3,19},{19,3},{4,20},{20... | collective-permute-start | bytes 1376264 | tf_op jit(solution)/shard_map/sum_attn/ppermute | solution.py:57
  102.7 18.9 %collective-permute-start.12 = (bf16[128,1024]{1,0:T(8,128)(2,1)}, bf16[128,1024]{1,0:T(8,128)(2,1)S(1)}, u32[]{:S(2)}, u32[]{:S(2)}) collective-permute-start(bf16[128,1024]{1,0:T(8,128)(2,1)} %get-tuple-element.62), channel_id=1, source_target_pairs={{0,2},{2,0},{4,6},{6,4},{1,3},{3,1},{5,7},{7,5},{8,10},{10,8},{12,... | collective-permute-start | bytes 786440 | tf_op jit(solution)/shard_map/sum_attn/ppermute | solution.py:814
  103.0 19.1 %collective-permute-start.13 = (bf16[128,1024]{1,0:T(8,128)(2,1)}, bf16[128,1024]{1,0:T(8,128)(2,1)S(1)}, u32[]{:S(2)}, u32[]{:S(2)}) collective-permute-start(bf16[128,1024]{1,0:T(8,128)(2,1)} %get-tuple-element.63), channel_id=1, source_target_pairs={{0,4},{2,6},{4,0},{6,2},{1,5},{3,7},{5,1},{7,3},{8,12},{10,14},{12... | collective-permute-start | bytes 786440 | tf_op jit(solution)/shard_map/sum_attn/ppermute | solution.py:814
  104.9 22.6 %collective-permute-start.14 = (bf16[128,1024]{1,0:T(8,128)(2,1)}, bf16[128,1024]{1,0:T(8,128)(2,1)S(1)}, u32[]{:S(2)}, u32[]{:S(2)}) collective-permute-start(bf16[128,1024]{1,0:T(8,128)(2,1)} %get-tuple-element.64), channel_id=1, source_target_pairs={{0,6},{2,4},{4,2},{6,0},{1,7},{3,5},{5,3},{7,1},{8,14},{10,12},{12... | collective-permute-start | bytes 786440 | tf_op jit(solution)/shard_map/sum_attn/ppermute | solution.py:814
  130.9 16.3 %all-to-all-start.3 = ((bf16[4,128,1024]{2,1,0:T(8,128)(2,1)}), bf16[4,128,1024]{2,1,0:T(8,128)(2,1)S(1)}, u32[]{:S(2)}, u32[]{:S(2)}) async-start(bf16[4,128,1024]{2,1,0:T(8,128)(2,1)} %broadcast_in_dim.22), calls=%async_computation.3 | async-start | bytes 2097152 | tf_op jit(solution)/shard_map/tokens_xf/all_to_all | solution.py:675
  180.2 17.8 %all-to-all-start.4 = ((bf16[4,128,1024]{2,1,0:T(8,128)(2,1)}), bf16[4,128,1024]{2,1,0:T(8,128)(2,1)S(1)}, u32[]{:S(2)}, u32[]{:S(2)}) async-start(bf16[4,128,1024]{2,1,0:T(8,128)(2,1)} %bitcast.36), calls=%async_computation.4 | async-start | bytes 2097152 | tf_op jit(solution)/shard_map/sum_dxf/all_to_all | solution.py:679
  183.8 13.4 %collective-permute-start.22 = (bf16[256,896]{1,0:T(8,128)(2,1)S(1)}, bf16[256,896]{1,0:T(8,128)(2,1)S(1)}, u32[]{:S(2)}, u32[]{:S(2)}) collective-permute-start(bf16[256,896]{1,0:T(8,128)(2,1)S(1)} %copy-done.64), channel_id=1, source_target_pairs={{0,16},{16,0},{1,17},{17,1},{2,18},{18,2},{3,19},{19,3},{4,20},{20... | collective-permute-start | bytes 1376264 | tf_op jit(solution)/shard_map/grads_ffn/ppermute | solution.py:57
  185.1 21.5 %collective-permute-start.27 = (bf16[256,896]{1,0:T(8,128)(2,1)}, bf16[256,896]{1,0:T(8,128)(2,1)}, u32[]{:S(2)}, u32[]{:S(2)}) collective-permute-start(bf16[256,896]{1,0:T(8,128)(2,1)} %get-tuple-element.77), channel_id=1, source_target_pairs={{0,16},{16,0},{1,17},{17,1},{2,18},{18,2},{3,19},{19,3},{4,20},{20... | collective-permute-start | bytes 1376264 | tf_op jit(solution)/shard_map/grads_ffn/ppermute | solution.py:57
  202.1 18.3 %collective-permute-start.24 = (bf16[128,1024]{1,0:T(8,128)(2,1)S(1)}, bf16[128,1024]{1,0:T(8,128)(2,1)S(1)}, u32[]{:S(2)}, u32[]{:S(2)}) collective-permute-start(bf16[128,1024]{1,0:T(8,128)(2,1)S(1)} %get-tuple-element.139), channel_id=1, source_target_pairs={{0,4},{2,6},{4,0},{6,2},{1,5},{3,7},{5,1},{7,3},{8,12},{10,14},{12... | collective-permute-start | bytes 786440 | tf_op jit(solution)/shard_map/tokens_dattn/ppermute | solution.py:705
  203.6 18.8 %collective-permute-start.23 = (bf16[128,1024]{1,0:T(8,128)(2,1)S(1)}, bf16[128,1024]{1,0:T(8,128)(2,1)S(1)}, u32[]{:S(2)}, u32[]{:S(2)}) collective-permute-start(bf16[128,1024]{1,0:T(8,128)(2,1)S(1)} %get-tuple-element.139), channel_id=1, source_target_pairs={{0,6},{2,4},{4,2},{6,0},{1,7},{3,5},{5,3},{7,1},{8,14},{10,12},{12... | collective-permute-start | bytes 786440 | tf_op jit(solution)/shard_map/tokens_dattn/ppermute | solution.py:705
  203.9 21.9 %collective-permute-start.26 = (bf16[256,896]{1,0:T(8,128)(2,1)S(1)}, bf16[256,896]{1,0:T(8,128)(2,1)S(1)}, u32[]{:S(2)}, u32[]{:S(2)}) collective-permute-start(bf16[256,896]{1,0:T(8,128)(2,1)S(1)} %add_convert_fusion.3), channel_id=1, source_target_pairs={{0,8},{8,0},{1,9},{9,1},{2,10},{10,2},{3,11},{11,3},{4,12},{12,4},... | collective-permute-start | bytes 1376264 | tf_op jit(solution)/shard_map/grads_ffn/ppermute | solution.py:57
  226.6 36.5 %all-to-all-start.5 = ((bf16[4,128,1024]{2,1,0:T(8,128)(2,1)}), bf16[4,128,1024]{2,1,0:T(8,128)(2,1)S(1)}, u32[]{:S(2)}, u32[]{:S(2)}) async-start(bf16[4,128,1024]{2,1,0:T(8,128)(2,1)} %bitcast.90), calls=%async_computation.5 | async-start | bytes 2097152 | tf_op jit(solution)/shard_map/sum_out/all_to_all | solution.py:858
  230.3 22.3 %collective-permute-start.29 = (bf16[256,896]{1,0:T(8,128)(2,1)}, bf16[256,896]{1,0:T(8,128)(2,1)}, u32[]{:S(2)}, u32[]{:S(2)}) collective-permute-start(bf16[256,896]{1,0:T(8,128)(2,1)} %add_convert_fusion.2.refs_2_), channel_id=1, source_target_pairs={{0,8},{8,0},{1,9},{9,1},{2,10},{10,2},{3,11},{11,3},{4,12},{12,4},... | collective-permute-start | bytes 1376264 | tf_op jit(solution)/shard_map/grads_ffn/ppermute | solution.py:57
  231.8 33.1 %collective-permute-start.32 = (bf16[256,1792]{1,0:T(8,128)(2,1)}, bf16[256,1792]{1,0:T(8,128)(2,1)S(1)}, u32[]{:S(2)}, u32[]{:S(2)}) collective-permute-start(bf16[256,1792]{1,0:T(8,128)(2,1)} %after.44), channel_id=1, source_target_pairs={{0,16},{16,0},{1,17},{17,1},{2,18},{18,2},{3,19},{19,3},{4,20},{20... | collective-permute-start | bytes 2752520 | tf_op jit(solution)/shard_map/grads_ffn/ppermute | solution.py:57
  262.3 34.0 %collective-permute-start.35 = (bf16[256,384]{1,0:T(8,128)(2,1)}, bf16[256,384]{1,0:T(8,128)(2,1)}, u32[]{:S(2)}, u32[]{:S(2)}) collective-permute-start(bf16[256,384]{1,0:T(8,128)(2,1)} %get-tuple-element.85.refs_2_), channel_id=1, source_target_pairs={{0,16},{16,0},{1,17},{17,1},{2,18},{18,2},{3,19},{19,3},{4,20},{20... | collective-permute-start | bytes 589832 | tf_op jit(solution)/shard_map/grads_attn/ppermute | solution.py:57
  271.2 24.1 %all-to-all-start.6 = ((bf16[4,128,1024]{2,1,0:T(8,128)(2,1)}), bf16[4,128,1024]{2,1,0:T(8,128)(2,1)S(1)}, u32[]{:S(2)}, u32[]{:S(2)}) async-start(bf16[4,128,1024]{2,1,0:T(8,128)(2,1)} %bitcast.83), calls=%async_computation.6 | async-start | bytes 2097152 | tf_op jit(solution)/shard_map/sum_dxa/all_to_all | solution.py:679
  276.8 16.9 %collective-permute-start.37 = (bf16[264,384]{1,0:T(8,128)(2,1)S(1)}, bf16[264,384]{1,0:T(8,128)(2,1)S(1)}, u32[]{:S(2)}, u32[]{:S(2)}) collective-permute-start(bf16[264,384]{1,0:T(8,128)(2,1)S(1)} %pad_maximum_fusion.9), channel_id=1, source_target_pairs={{0,8},{8,0},{1,9},{9,1},{2,10},{10,2},{3,11},{11,3},{4,12},{12,4},... | collective-permute-start | bytes 608264 | tf_op jit(solution)/shard_map/grads_attn/ppermute | solution.py:57
  282.7 21.0 %collective-permute-start.38 = (bf16[64,1792]{1,0:T(8,128)(2,1)}, bf16[64,1792]{1,0:T(8,128)(2,1)S(1)}, u32[]{:S(2)}, u32[]{:S(2)}) collective-permute-start(bf16[64,1792]{1,0:T(8,128)(2,1)} %get-tuple-element.94), channel_id=1, source_target_pairs={{0,2},{2,0},{4,6},{6,4},{1,3},{3,1},{5,7},{7,5},{8,10},{10,8},{12,... | collective-permute-start | bytes 688136 | tf_op jit(solution)/shard_map/grads_ffn/ppermute | solution.py:912
  284.7 19.1 %collective-permute-start.39 = (bf16[64,1792]{1,0:T(8,128)(2,1)}, bf16[64,1792]{1,0:T(8,128)(2,1)S(1)}, u32[]{:S(2)}, u32[]{:S(2)}) collective-permute-start(bf16[64,1792]{1,0:T(8,128)(2,1)} %get-tuple-element.95), channel_id=1, source_target_pairs={{0,4},{2,6},{4,0},{6,2},{1,5},{3,7},{5,1},{7,3},{8,12},{10,14},{12... | collective-permute-start | bytes 688136 | tf_op jit(solution)/shard_map/grads_ffn/ppermute | solution.py:912
  286.2 20.2 %collective-permute-start.40 = (bf16[64,1792]{1,0:T(8,128)(2,1)}, bf16[64,1792]{1,0:T(8,128)(2,1)S(1)}, u32[]{:S(2)}, u32[]{:S(2)}) collective-permute-start(bf16[64,1792]{1,0:T(8,128)(2,1)} %get-tuple-element.96), channel_id=1, source_target_pairs={{0,6},{2,4},{4,2},{6,0},{1,7},{3,5},{5,3},{7,1},{8,14},{10,12},{12... | collective-permute-start | bytes 688136 | tf_op jit(solution)/shard_map/grads_ffn/ppermute | solution.py:912
  303.1 13.3 %collective-permute-start.33 = (bf16[2,128,1024]{2,1,0:T(8,128)(2,1)S(1)}, bf16[2,128,1024]{2,1,0:T(8,128)(2,1)S(1)}, u32[]{:S(2)}, u32[]{:S(2)}) collective-permute-start(bf16[2,128,1024]{2,1,0:T(8,128)(2,1)S(1)} %pad_maximum_fusion.4), channel_id=1, source_target_pairs={{0,0},{1,8},{8,1},{9,9},{2,2},{3,10},{10,3},{11,11},{4,4},{5,12},{... | collective-permute-start | bytes 1572872 | tf_op jit(solution)/shard_map/return/ppermute | solution.py:666
  (97 other events, 756.6 us)

commit v4 on v3

--- a/solution.py
+++ b/solution.py
@@ -713,7 +713,7 @@
     half = gather_half("tokens_hidden", hidden_own, ffn_own)
     with jax.named_scope("weights_attn"):
         across = swap(beside, "dp")
-    cot_own = relative(fetch("fetch_cot", grad_out, beside))
+    cot_own = relative(fetch("fetch_cot", grad_out))
     with jax.named_scope("weights_attn"):
         parts = [own, beside, opposite, across]
         wa = jnp.stack([p[:, :shard] for p in parts]).reshape(d_model, wide)

time: 324 us -> 320 us (0.988)
  starting transfers between devices: 80.5 us -> 86.8 us
  local copies, waits for them, and re-layouts: 33.8 us -> 28.6 us
  waiting for transfers between devices: 93.7 us -> 89.3 us
    ppermute x27, starting transfers between devices: 26.8 us -> 34.1 us  [swap(): return lax.ppermute(v, axis, [(0, 1), (1, 0)])]
    unnamed x161 -> x157, local copies, waits for them, and re-layouts: 18.8 us -> 18.3 us
  transfers between devices with their start and end apart: 50 -> 50, of which waited for: 21 -> 22; matrix products, arithmetic and copies ran while one was open for 14% -> 13% of each run, Pallas kernels for 19% -> 20%
where the time goes in v4:
time: 320 us; the launch traced here: 319 us
  waiting for transfers between devices  89.3 us (28%)
  starting transfers between devices  86.8 us (27%)
  Pallas kernels  73.1 us (23%)
  other arithmetic  35.2 us (11%)
  local copies, waits for them, and re-layouts  28.6 us (9%)
  matrix products  3.84 us (1%)
    ppermute x27, waiting for transfers between devices, swap(): return lax.ppermute(v, axis, [(0, 1), (1, 0)])  52.1 us
    ppermute x27, starting transfers between devices, swap(): return lax.ppermute(v, axis, [(0, 1), (1, 0)])  34.1 us
    ppermute x6, waiting for transfers between devices, share(): lax.ppermute(block, 'j', [(i, i ^ d) for i in range(J)])  19.1 us
    unnamed x157, local copies, waits for them, and re-layouts  18.3 us
    pallas_call x2, Pallas kernels, ffn_call(): pl.pallas_call(functools.partial(ffn_kernel, fw, part), grid=(count // ti...  17.2 us
    pallas_call x2, Pallas kernels, ffn_grad_call(): pl.pallas_call(functools.partial(ffn_grad_kernel, fw, width, whole), grid...  12.9 us
    pallas_call x1, Pallas kernels, attend_back_call(): pl.pallas_call(functools.partial(attend_back_kernel, tile, tiles), in_spe...  11.7 us
    all_to_all x2, starting transfers between devices, gather_half(): return lax.all_to_all(sent, 'j', 0, 0).reshape(side, d_model)  9.96 us
  transfers between devices with their start and end apart: 50, of which 22 were waited for; matrix products, arithmetic and copies ran while one was open for 13% of the time, Pallas kernels for 20%

profile of v4, /device:TPU:0, one launch (start us, length us, event | category | flops | bytes accessed | tf_op | source)
XLA Modules:
  0.0 318.7 jit_solution(14106492946126030223)
XLA Ops:
  2.5 5.2 %all-to-all-start.2 = ((bf16[4,72,384]{2,1,0:T(8,128)(2,1)}), bf16[4,72,384]{2,1,0:T(8,128)(2,1)S(1)}, u32[]{:S(2)}, u32[]{:S(2)}) async-start(bf16[4,72,384]{2,1,0:T(8,128)(2,1)} %pack.1), calls=%async_computation.2 | async-start | bytes 442368 | tf_op jit(solution)/shard_map/weights_attn/all_to_all | solution.py:633
  16.4 4.2 %all-to-all-start = ((bf16[4,64,1792]{2,1,0:T(8,128)(2,1)}), bf16[4,64,1792]{2,1,0:T(8,128)(2,1)S(1)}, u32[]{:S(2)}, u32[]{:S(2)}) async-start(bf16[4,64,1792]{2,1,0:T(8,128)(2,1)} %pad_maximum_fusion.2), calls=%async_computation | async-start | bytes 1835008 | tf_op jit(solution)/shard_map/weights_ffn/all_to_all | solution.py:633
  22.2 11.2 %collective-permute-start.1 = (bf16[4,72,384]{2,1,0:T(8,128)(2,1)S(1)}, bf16[4,72,384]{2,1,0:T(8,128)(2,1)S(1)}, u32[]{:S(2)}, u32[]{:S(2)}) collective-permute-start(bf16[4,72,384]{2,1,0:T(8,128)(2,1)S(1)} %all-to-all-done.2), channel_id=1, source_target_pairs={{0,8},{8,0},{1,9},{9,1},{2,10},{10,2},{3,11},{11,3},{4,12},{12,4},... | collective-permute-start | bytes 663560 | tf_op jit(solution)/shard_map/weights_attn/ppermute | solution.py:57
  33.4 7.2 %collective-permute-done.1 = bf16[4,72,384]{2,1,0:T(8,128)(2,1)S(1)} collective-permute-done((bf16[4,72,384]{2,1,0:T(8,128)(2,1)S(1)}, bf16[4,72,384]{2,1,0:T(8,128)(2,1)S(1)}, u32[]{:S(2)}, u32[]{:S(2)}) %collective-permute-start.1) | collective-permute-done | bytes 221216 | tf_op jit(solution)/shard_map/weights_attn/ppermute | solution.py:57
  42.1 6.3 %all-to-all-start.1 = ((bf16[4,128,1024]{2,1,0:T(8,128)(2,1)}), bf16[4,128,1024]{2,1,0:T(8,128)(2,1)S(1)}, u32[]{:S(2)}, u32[]{:S(2)}) async-start(bf16[4,128,1024]{2,1,0:T(8,128)(2,1)} %after.24), calls=%async_computation.1 | async-start | bytes 2097152 | tf_op jit(solution)/shard_map/tokens_hidden/all_to_all | solution.py:675
  49.0 3.1 multiply_sine_fusion
  56.1 3.6 %all-to-all-done.1 = bf16[4,128,1024]{2,1,0:T(8,128)(2,1)S(1)} async-done(((bf16[4,128,1024]{2,1,0:T(8,128)(2,1)}), bf16[4,128,1024]{2,1,0:T(8,128)(2,1)S(1)}, u32[]{:S(2)}, u32[]{:S(2)}) %all-to-all-start.1) | async-done | bytes 1048608 | tf_op jit(solution)/shard_map/tokens_hidden/all_to_all | solution.py:675
  70.4 6.1 %qkv.1 = (bf16[512,1024]{1,0:T(8,128)(2,1)}, bf16[512,1024]{1,0:T(8,128)(2,1)}, f32[1024,256]{1,0:T(8,128)}, bf16[1024,256]{1,0:T(8,128)(2,1)}) custom-call(bf16[512,1024]{1,0:T(8,128)(2,1)} %after.25.h0_ref.refs_1_, bf16[512,1024]{1,0:T(8,128)(2,1)} %collective-permute-done.5.h1_ref, f32[1,1024]{1,0:T(1,128)} %slice.290.gain_ref, ...), custom_call_target="tpu_custom_call" | custom-call | flops 1 | bytes 1 | tf_op jit(solution)/shard_map/qkv/pallas_call | solution.py:155
  76.5 6.4 %attend.1 = (bf16[1024,128]{1,0:T(8,128)(2,1)}, bf16[10,512,256]{2,1,0:T(8,128)(2,1)}) custom-call(s32[2]{0:T(128)} %pad_add_fusion.refs_6_.at_ref, bf16[1024,256]{1,0:T(8,128)(2,1)} %get-tuple-element.59.qkv_ref), custom_call_target="tpu_custom_call" | custom-call | flops 1 | bytes 1 | tf_op jit(solution)/shard_map/attend/pallas_call | solution.py:215
  83.1 5.1 %collective-permute-done.9.refs_4_ = bf16[128,1024]{1,0:T(8,128)(2,1)S(1)} collective-permute-done((bf16[128,1024]{1,0:T(8,128)(2,1)}, bf16[128,1024]{1,0:T(8,128)(2,1)S(1)}, u32[]{:S(2)}, u32[]{:S(2)}) %collective-permute-start.9) | collective-permute-done | bytes 262176 | tf_op jit(solution)/shard_map/tokens_cot/ppermute | solution.py:705
  96.6 2.8 add_cut.1
  103.5 13.1 %collective-permute-done.15.refs_1_.refs_4_ = bf16[256,896]{1,0:T(8,128)(2,1)S(1)} collective-permute-done((bf16[256,896]{1,0:T(8,128)(2,1)}, bf16[256,896]{1,0:T(8,128)(2,1)S(1)}, u32[]{:S(2)}, u32[]{:S(2)}) %collective-permute-start.15) | collective-permute-done | bytes 458784 | tf_op jit(solution)/shard_map/weights_ffn/ppermute | solution.py:57
  118.7 5.6 %collective-permute-done.14 = bf16[128,1024]{1,0:T(8,128)(2,1)S(1)} collective-permute-done((bf16[128,1024]{1,0:T(8,128)(2,1)}, bf16[128,1024]{1,0:T(8,128)(2,1)S(1)}, u32[]{:S(2)}, u32[]{:S(2)}) %collective-permute-start.14) | collective-permute-done | bytes 262176 | tf_op jit(solution)/shard_map/sum_attn/ppermute | solution.py:814
  127.6 3.7 %all-to-all-start.3 = ((bf16[4,128,1024]{2,1,0:T(8,128)(2,1)}), bf16[4,128,1024]{2,1,0:T(8,128)(2,1)S(1)}, u32[]{:S(2)}, u32[]{:S(2)}) async-start(bf16[4,128,1024]{2,1,0:T(8,128)(2,1)} %broadcast_in_dim.22), calls=%async_computation.3 | async-start | bytes 2097152 | tf_op jit(solution)/shard_map/tokens_xf/all_to_all | solution.py:675
  135.1 7.5 %collective-permute-done.17.refs_1_.refs_5_ = bf16[256,896]{1,0:T(8,128)(2,1)S(1)} collective-permute-done((bf16[256,896]{1,0:T(8,128)(2,1)S(1)}, bf16[256,896]{1,0:T(8,128)(2,1)S(1)}, u32[]{:S(2)}, u32[]{:S(2)}) %collective-permute-start.17) | collective-permute-done | bytes 458784 | tf_op jit(solution)/shard_map/weights_ffn/ppermute | solution.py:57
  147.1 8.6 %ffn.2 = (bf16[512,576]{1,0:T(8,128)(2,1)}, bf16[512,1152]{1,0:T(8,128)(2,1)}, bf16[512,1024]{1,0:T(8,128)(2,1)}, bf16[512,1024]{1,0:T(8,128)(2,1)}) custom-call(bf16[512,1024]{1,0:T(8,128)(2,1)} %after.32.x_ref.refs_0_, bf16[512,1024]{1,0:T(8,128)(2,1)} %copy-done.6, bf16[256,896]{1,0:T(8,128)(2,1)} %copy-done.14, bf16[256,896]{1,0:T(8,128)(2,1)} %copy-done.15, ...), custom_call_target="tpu_custom_call" | custom-call | flops 1 | bytes 1 | tf_op jit(solution)/shard_map/ffn/pallas_call | solution.py:352
  157.1 8.6 %ffn.3 = (bf16[512,576]{1,0:T(8,128)(2,1)}, bf16[512,1152]{1,0:T(8,128)(2,1)}, bf16[512,1024]{1,0:T(8,128)(2,1)}, bf16[512,1024]{1,0:T(8,128)(2,1)}) custom-call(bf16[512,1024]{1,0:T(8,128)(2,1)} %after.33.x_ref, bf16[512,1024]{1,0:T(8,128)(2,1)} %collective-permute-done.19.cot_ref.refs_3_, bf16[256,896]{1,0:T(8,128)(2,1)} %copy-done.14, ...), custom_call_target="tpu_custom_call" | custom-call | flops 1 | bytes 1 | tf_op jit(solution)/shard_map/ffn/pallas_call | solution.py:352
  166.2 6.5 %ffn_grad.2 = (bf16[256,1792]{1,0:T(8,128)(2,1)}, bf16[256,896]{1,0:T(8,128)(2,1)}, bf16[256,896]{1,0:T(8,128)(2,1)}) custom-call(bf16[512,1024]{1,0:T(8,128)(2,1)} %after.32.x_ref.refs_0_, bf16[512,1024]{1,0:T(8,128)(2,1)} %copy-done.9, bf16[512,1024]{1,0:T(8,128)(2,1)} %copy-done.6, bf16[512,1024]{1,0:T(8,128)(2,1)} %collective-permute-done.19.cot_ref.refs_3_, ...), custom_call_target="tpu_custom_call" | custom-call | flops 1 | bytes 1 | tf_op jit(solution)/shard_map/ffn_grad/pallas_call | solution.py:402
  176.9 3.5 %all-to-all-start.4 = ((bf16[4,128,1024]{2,1,0:T(8,128)(2,1)}), bf16[4,128,1024]{2,1,0:T(8,128)(2,1)S(1)}, u32[]{:S(2)}, u32[]{:S(2)}) async-start(bf16[4,128,1024]{2,1,0:T(8,128)(2,1)} %bitcast.36), calls=%async_computation.4 | async-start | bytes 2097152 | tf_op jit(solution)/shard_map/sum_dxf/all_to_all | solution.py:679
  182.6 6.5 %ffn_grad.3 = (bf16[256,896]{1,0:T(8,128)(2,1)}, bf16[256,896]{1,0:T(8,128)(2,1)}, bf16[256,896]{1,0:T(8,128)(2,1)}, bf16[256,896]{1,0:T(8,128)(2,1)}) custom-call(bf16[512,1024]{1,0:T(8,128)(2,1)} %after.32.x_ref.refs_0_, bf16[512,1024]{1,0:T(8,128)(2,1)} %copy-done.9, bf16[512,1024]{1,0:T(8,128)(2,1)} %copy-done.6, ...), custom_call_target="tpu_custom_call" | custom-call | flops 1 | bytes 1 | tf_op jit(solution)/shard_map/ffn_grad/pallas_call | solution.py:402
  205.3 11.7 %collective-permute-done.24 = bf16[128,1024]{1,0:T(8,128)(2,1)S(1)} collective-permute-done((bf16[128,1024]{1,0:T(8,128)(2,1)S(1)}, bf16[128,1024]{1,0:T(8,128)(2,1)S(1)}, u32[]{:S(2)}, u32[]{:S(2)}) %collective-permute-start.24) | collective-permute-done | bytes 262176 | tf_op jit(solution)/shard_map/tokens_dattn/ppermute | solution.py:705
  223.3 3.7 %all-to-all-start.5 = ((bf16[4,128,1024]{2,1,0:T(8,128)(2,1)}), bf16[4,128,1024]{2,1,0:T(8,128)(2,1)S(1)}, u32[]{:S(2)}, u32[]{:S(2)}) async-start(bf16[4,128,1024]{2,1,0:T(8,128)(2,1)} %bitcast.90), calls=%async_computation.5 | async-start | bytes 2097152 | tf_op jit(solution)/shard_map/sum_out/all_to_all | solution.py:858
  231.2 11.7 %attend_back.1 = (bf16[1024,256]{1,0:T(8,128)(2,1)}, f32[8,128]{1,0:T(8,128)}, bf16[256,1024]{1,0:T(8,128)(2,1)}, bf16[256,1024]{1,0:T(8,128)(2,1)}, bf16[512,1024]{1,0:T(8,128)(2,1)}) custom-call(s32[2]{0:T(128)} %pad_add_fusion.refs_6_.at_ref, bf16[1024,256]{1,0:T(8,128)(2,1)} %get-tuple-element.59.qkv_ref, bf16[1024,128]{1,0:T(8,128)(2,1)} %after.29.mixed_ref, ...), custom_call_target="tpu_custom_call" | custom-call | flops 1 | bytes 1 | tf_op jit(solution)/shard_map/attend_back/pallas_call | solution.py:300
  242.9 6.5 %collective-permute-done.29.refs_1_.got_a = bf16[256,896]{1,0:T(8,128)(2,1)} collective-permute-done((bf16[256,896]{1,0:T(8,128)(2,1)}, bf16[256,896]{1,0:T(8,128)(2,1)}, u32[]{:S(2)}, u32[]{:S(2)}) %collective-permute-start.29) | collective-permute-done | bytes 458784 | tf_op jit(solution)/shard_map/grads_ffn/ppermute | solution.py:57
  249.9 5.3 %attn_grad.1 = (bf16[256,384]{1,0:T(8,128)(2,1)}, bf16[256,384]{1,0:T(8,128)(2,1)}, bf16[256,384]{1,0:T(8,128)(2,1)}, bf16[256,384]{1,0:T(8,128)(2,1)}) custom-call(bf16[512,1024]{1,0:T(8,128)(2,1)} %get-tuple-element.83.x0_ref, bf16[512,1024]{1,0:T(8,128)(2,1)} %get-tuple-element.84.x1_ref, bf16[512,1024]{1,0:T(8,128)(2,1)} %after.36.refs_1_.g0_ref, ...), custom_call_target="tpu_custom_call" | custom-call | flops 1 | bytes 1 | tf_op jit(solution)/shard_map/attn_grad/pallas_call | solution.py:513
  263.4 2.8 add.201.refs_1_
  268.0 5.6 %all-to-all-start.6 = ((bf16[4,128,1024]{2,1,0:T(8,128)(2,1)}), bf16[4,128,1024]{2,1,0:T(8,128)(2,1)S(1)}, u32[]{:S(2)}, u32[]{:S(2)}) async-start(bf16[4,128,1024]{2,1,0:T(8,128)(2,1)} %bitcast.83), calls=%async_computation.6 | async-start | bytes 2097152 | tf_op jit(solution)/shard_map/sum_dxa/all_to_all | solution.py:679
  276.6 2.9 merge.1
  283.0 7.5 %collective-permute-done.37.refs_0_ = bf16[264,384]{1,0:T(8,128)(2,1)S(1)} collective-permute-done((bf16[264,384]{1,0:T(8,128)(2,1)S(1)}, bf16[264,384]{1,0:T(8,128)(2,1)S(1)}, u32[]{:S(2)}, u32[]{:S(2)}) %collective-permute-start.37) | collective-permute-done | bytes 202784 | tf_op jit(solution)/shard_map/grads_attn/ppermute | solution.py:57
  295.0 4.4 %all-to-all-start.7 = ((bf16[4,64,512]{2,1,0:T(8,128)(2,1)}), bf16[4,64,512]{2,1,0:T(8,128)(2,1)S(1)}, u32[]{:S(2)}, u32[]{:S(2)}) async-start(bf16[4,64,512]{2,1,0:T(8,128)(2,1)} %pad_maximum_fusion.7), calls=%async_computation.7 | async-start | bytes 524288 | tf_op jit(solution)/shard_map/grads/all_to_all | solution.py:935
  303.1 2.9 all-to-all-done.7.got_ref
  306.8 3.3 %final.1 = (f32[64,512]{1,0:T(8,128)}, f32[64,256]{1,0:T(8,128)}, f32[64,256]{1,0:T(8,128)}, f32[64,512]{1,0:T(8,128)}, f32[64,2304]{1,0:T(8,128)}, /*index=5*/f...) custom-call(s32[1]{0:T(128)} %bitcast.1.place_ref, bf16[4,64,512]{2,1,0:T(8,128)(2,1)} %copy-done.46, ...), custom_call_target="tpu_custom_call" | custom-call | flops 1 | bytes 1 | tf_op jit(solution)/shard_map/final/pallas_call | solution.py:585
  (376 shorter events, 123.9 us)
Async XLA Ops:
  2.5 13.9 %all-to-all-start.2 = ((bf16[4,72,384]{2,1,0:T(8,128)(2,1)}), bf16[4,72,384]{2,1,0:T(8,128)(2,1)S(1)}, u32[]{:S(2)}, u32[]{:S(2)}) async-start(bf16[4,72,384]{2,1,0:T(8,128)(2,1)} %pack.1), calls=%async_computation.2 | async-start | bytes 442368 | tf_op jit(solution)/shard_map/weights_attn/all_to_all | solution.py:633
  16.4 24.3 %all-to-all-start = ((bf16[4,64,1792]{2,1,0:T(8,128)(2,1)}), bf16[4,64,1792]{2,1,0:T(8,128)(2,1)S(1)}, u32[]{:S(2)}, u32[]{:S(2)}) async-start(bf16[4,64,1792]{2,1,0:T(8,128)(2,1)} %pad_maximum_fusion.2), calls=%async_computation | async-start | bytes 1835008 | tf_op jit(solution)/shard_map/weights_ffn/all_to_all | solution.py:633
  20.6 28.4 %collective-permute-start.2 = (bf16[4,72,384]{2,1,0:T(8,128)(2,1)S(1)}, bf16[4,72,384]{2,1,0:T(8,128)(2,1)S(1)}, u32[]{:S(2)}, u32[]{:S(2)}) collective-permute-start(bf16[4,72,384]{2,1,0:T(8,128)(2,1)S(1)} %all-to-all-done.2), channel_id=1, source_target_pairs={{0,16},{16,0},{1,17},{17,1},{2,18},{18,2},{3,19},{19,3},{4,20},{20... | collective-permute-start | bytes 663560 | tf_op jit(solution)/shard_map/weights_attn/ppermute | solution.py:57
  22.2 18.4 %collective-permute-start.1 = (bf16[4,72,384]{2,1,0:T(8,128)(2,1)S(1)}, bf16[4,72,384]{2,1,0:T(8,128)(2,1)S(1)}, u32[]{:S(2)}, u32[]{:S(2)}) collective-permute-start(bf16[4,72,384]{2,1,0:T(8,128)(2,1)S(1)} %all-to-all-done.2), channel_id=1, source_target_pairs={{0,8},{8,0},{1,9},{9,1},{2,10},{10,2},{3,11},{11,3},{4,12},{12,4},... | collective-permute-start | bytes 663560 | tf_op jit(solution)/shard_map/weights_attn/ppermute | solution.py:57
  42.1 17.7 %all-to-all-start.1 = ((bf16[4,128,1024]{2,1,0:T(8,128)(2,1)}), bf16[4,128,1024]{2,1,0:T(8,128)(2,1)S(1)}, u32[]{:S(2)}, u32[]{:S(2)}) async-start(bf16[4,128,1024]{2,1,0:T(8,128)(2,1)} %after.24), calls=%async_computation.1 | async-start | bytes 2097152 | tf_op jit(solution)/shard_map/tokens_hidden/all_to_all | solution.py:675
  62.0 26.2 %collective-permute-start.7 = (bf16[256,1792]{1,0:T(8,128)(2,1)}, bf16[256,1792]{1,0:T(8,128)(2,1)S(1)}, u32[]{:S(2)}, u32[]{:S(2)}) collective-permute-start(bf16[256,1792]{1,0:T(8,128)(2,1)} %after.27), channel_id=1, source_target_pairs={{0,16},{16,0},{1,17},{17,1},{2,18},{18,2},{3,19},{19,3},{4,20},{20... | collective-permute-start | bytes 2752520 | tf_op jit(solution)/shard_map/weights_ffn/ppermute | solution.py:57
  64.4 23.9 %collective-permute-start.6 = (bf16[256,896]{1,0:T(8,128)(2,1)}, bf16[256,896]{1,0:T(8,128)(2,1)S(1)}, u32[]{:S(2)}, u32[]{:S(2)}) collective-permute-start(bf16[256,896]{1,0:T(8,128)(2,1)} %after.26), channel_id=1, source_target_pairs={{0,8},{8,0},{1,9},{9,1},{2,10},{10,2},{3,11},{11,3},{4,12},{12,4},... | collective-permute-start | bytes 1376264 | tf_op jit(solution)/shard_map/weights_ffn/ppermute | solution.py:57
  66.2 16.9 %collective-permute-start.10 = (bf16[128,1024]{1,0:T(8,128)(2,1)}, bf16[128,1024]{1,0:T(8,128)(2,1)S(1)}, u32[]{:S(2)}, u32[]{:S(2)}) collective-permute-start(bf16[128,1024]{1,0:T(8,128)(2,1)} %after.28), channel_id=1, source_target_pairs={{0,6},{2,4},{4,2},{6,0},{1,7},{3,5},{5,3},{7,1},{8,14},{10,12},{12... | collective-permute-start | bytes 786440 | tf_op jit(solution)/shard_map/tokens_cot/ppermute | solution.py:705
  67.7 20.5 %collective-permute-start.9 = (bf16[128,1024]{1,0:T(8,128)(2,1)}, bf16[128,1024]{1,0:T(8,128)(2,1)S(1)}, u32[]{:S(2)}, u32[]{:S(2)}) collective-permute-start(bf16[128,1024]{1,0:T(8,128)(2,1)} %after.28), channel_id=1, source_target_pairs={{0,4},{2,6},{4,0},{6,2},{1,5},{3,7},{5,1},{7,3},{8,12},{10,14},{12... | collective-permute-start | bytes 786440 | tf_op jit(solution)/shard_map/tokens_cot/ppermute | solution.py:705
  68.7 19.5 %collective-permute-start.8 = (bf16[128,1024]{1,0:T(8,128)(2,1)}, bf16[128,1024]{1,0:T(8,128)(2,1)}, u32[]{:S(2)}, u32[]{:S(2)}) collective-permute-start(bf16[128,1024]{1,0:T(8,128)(2,1)} %after.28), channel_id=1, source_target_pairs={{0,2},{2,0},{4,6},{6,4},{1,3},{3,1},{5,7},{7,5},{8,10},{10,8},{12,... | collective-permute-start | bytes 786440 | tf_op jit(solution)/shard_map/tokens_cot/ppermute | solution.py:705
  92.6 24.0 %collective-permute-start.15 = (bf16[256,896]{1,0:T(8,128)(2,1)}, bf16[256,896]{1,0:T(8,128)(2,1)S(1)}, u32[]{:S(2)}, u32[]{:S(2)}) collective-permute-start(bf16[256,896]{1,0:T(8,128)(2,1)} %after.30), channel_id=1, source_target_pairs={{0,8},{8,0},{1,9},{9,1},{2,10},{10,2},{3,11},{11,3},{4,12},{12,4},... | collective-permute-start | bytes 1376264 | tf_op jit(solution)/shard_map/weights_ffn/ppermute | solution.py:57
  94.7 21.9 %collective-permute-start.16 = (bf16[256,896]{1,0:T(8,128)(2,1)S(1)}, bf16[256,896]{1,0:T(8,128)(2,1)S(1)}, u32[]{:S(2)}, u32[]{:S(2)}) collective-permute-start(bf16[256,896]{1,0:T(8,128)(2,1)S(1)} %copy-done.16), channel_id=1, source_target_pairs={{0,16},{16,0},{1,17},{17,1},{2,18},{18,2},{3,19},{19,3},{4,20},{20... | collective-permute-start | bytes 1376264 | tf_op jit(solution)/shard_map/sum_attn/ppermute | solution.py:57
  99.4 18.8 %collective-permute-start.12 = (bf16[128,1024]{1,0:T(8,128)(2,1)}, bf16[128,1024]{1,0:T(8,128)(2,1)S(1)}, u32[]{:S(2)}, u32[]{:S(2)}) collective-permute-start(bf16[128,1024]{1,0:T(8,128)(2,1)} %get-tuple-element.62), channel_id=1, source_target_pairs={{0,2},{2,0},{4,6},{6,4},{1,3},{3,1},{5,7},{7,5},{8,10},{10,8},{12,... | collective-permute-start | bytes 786440 | tf_op jit(solution)/shard_map/sum_attn/ppermute | solution.py:814
  99.8 18.9 %collective-permute-start.13 = (bf16[128,1024]{1,0:T(8,128)(2,1)}, bf16[128,1024]{1,0:T(8,128)(2,1)S(1)}, u32[]{:S(2)}, u32[]{:S(2)}) collective-permute-start(bf16[128,1024]{1,0:T(8,128)(2,1)} %get-tuple-element.63), channel_id=1, source_target_pairs={{0,4},{2,6},{4,0},{6,2},{1,5},{3,7},{5,1},{7,3},{8,12},{10,14},{12... | collective-permute-start | bytes 786440 | tf_op jit(solution)/shard_map/sum_attn/ppermute | solution.py:814
  102.2 22.1 %collective-permute-start.14 = (bf16[128,1024]{1,0:T(8,128)(2,1)}, bf16[128,1024]{1,0:T(8,128)(2,1)S(1)}, u32[]{:S(2)}, u32[]{:S(2)}) collective-permute-start(bf16[128,1024]{1,0:T(8,128)(2,1)} %get-tuple-element.64), channel_id=1, source_target_pairs={{0,6},{2,4},{4,2},{6,0},{1,7},{3,5},{5,3},{7,1},{8,14},{10,12},{12... | collective-permute-start | bytes 786440 | tf_op jit(solution)/shard_map/sum_attn/ppermute | solution.py:814
  127.6 16.3 %all-to-all-start.3 = ((bf16[4,128,1024]{2,1,0:T(8,128)(2,1)}), bf16[4,128,1024]{2,1,0:T(8,128)(2,1)S(1)}, u32[]{:S(2)}, u32[]{:S(2)}) async-start(bf16[4,128,1024]{2,1,0:T(8,128)(2,1)} %broadcast_in_dim.22), calls=%async_computation.3 | async-start | bytes 2097152 | tf_op jit(solution)/shard_map/tokens_xf/all_to_all | solution.py:675
  176.9 17.8 %all-to-all-start.4 = ((bf16[4,128,1024]{2,1,0:T(8,128)(2,1)}), bf16[4,128,1024]{2,1,0:T(8,128)(2,1)S(1)}, u32[]{:S(2)}, u32[]{:S(2)}) async-start(bf16[4,128,1024]{2,1,0:T(8,128)(2,1)} %bitcast.36), calls=%async_computation.4 | async-start | bytes 2097152 | tf_op jit(solution)/shard_map/sum_dxf/all_to_all | solution.py:679
  180.6 13.4 %collective-permute-start.22 = (bf16[256,896]{1,0:T(8,128)(2,1)S(1)}, bf16[256,896]{1,0:T(8,128)(2,1)S(1)}, u32[]{:S(2)}, u32[]{:S(2)}) collective-permute-start(bf16[256,896]{1,0:T(8,128)(2,1)S(1)} %copy-done.63), channel_id=1, source_target_pairs={{0,16},{16,0},{1,17},{17,1},{2,18},{18,2},{3,19},{19,3},{4,20},{20... | collective-permute-start | bytes 1376264 | tf_op jit(solution)/shard_map/grads_ffn/ppermute | solution.py:57
  182.3 21.2 %collective-permute-start.27 = (bf16[256,896]{1,0:T(8,128)(2,1)}, bf16[256,896]{1,0:T(8,128)(2,1)}, u32[]{:S(2)}, u32[]{:S(2)}) collective-permute-start(bf16[256,896]{1,0:T(8,128)(2,1)} %get-tuple-element.77), channel_id=1, source_target_pairs={{0,16},{16,0},{1,17},{17,1},{2,18},{18,2},{3,19},{19,3},{4,20},{20... | collective-permute-start | bytes 1376264 | tf_op jit(solution)/shard_map/grads_ffn/ppermute | solution.py:57
  198.9 18.2 %collective-permute-start.24 = (bf16[128,1024]{1,0:T(8,128)(2,1)S(1)}, bf16[128,1024]{1,0:T(8,128)(2,1)S(1)}, u32[]{:S(2)}, u32[]{:S(2)}) collective-permute-start(bf16[128,1024]{1,0:T(8,128)(2,1)S(1)} %get-tuple-element.139), channel_id=1, source_target_pairs={{0,4},{2,6},{4,0},{6,2},{1,5},{3,7},{5,1},{7,3},{8,12},{10,14},{12... | collective-permute-start | bytes 786440 | tf_op jit(solution)/shard_map/tokens_dattn/ppermute | solution.py:705
  200.3 18.8 %collective-permute-start.23 = (bf16[128,1024]{1,0:T(8,128)(2,1)S(1)}, bf16[128,1024]{1,0:T(8,128)(2,1)S(1)}, u32[]{:S(2)}, u32[]{:S(2)}) collective-permute-start(bf16[128,1024]{1,0:T(8,128)(2,1)S(1)} %get-tuple-element.139), channel_id=1, source_target_pairs={{0,6},{2,4},{4,2},{6,0},{1,7},{3,5},{5,3},{7,1},{8,14},{10,12},{12... | collective-permute-start | bytes 786440 | tf_op jit(solution)/shard_map/tokens_dattn/ppermute | solution.py:705
  200.6 21.9 %collective-permute-start.26 = (bf16[256,896]{1,0:T(8,128)(2,1)S(1)}, bf16[256,896]{1,0:T(8,128)(2,1)S(1)}, u32[]{:S(2)}, u32[]{:S(2)}) collective-permute-start(bf16[256,896]{1,0:T(8,128)(2,1)S(1)} %add_convert_fusion.3), channel_id=1, source_target_pairs={{0,8},{8,0},{1,9},{9,1},{2,10},{10,2},{3,11},{11,3},{4,12},{12,4},... | collective-permute-start | bytes 1376264 | tf_op jit(solution)/shard_map/grads_ffn/ppermute | solution.py:57
  223.3 36.5 %all-to-all-start.5 = ((bf16[4,128,1024]{2,1,0:T(8,128)(2,1)}), bf16[4,128,1024]{2,1,0:T(8,128)(2,1)S(1)}, u32[]{:S(2)}, u32[]{:S(2)}) async-start(bf16[4,128,1024]{2,1,0:T(8,128)(2,1)} %bitcast.90), calls=%async_computation.5 | async-start | bytes 2097152 | tf_op jit(solution)/shard_map/sum_out/all_to_all | solution.py:858
  227.1 22.3 %collective-permute-start.29 = (bf16[256,896]{1,0:T(8,128)(2,1)}, bf16[256,896]{1,0:T(8,128)(2,1)}, u32[]{:S(2)}, u32[]{:S(2)}) collective-permute-start(bf16[256,896]{1,0:T(8,128)(2,1)} %add_convert_fusion.2.refs_2_), channel_id=1, source_target_pairs={{0,8},{8,0},{1,9},{9,1},{2,10},{10,2},{3,11},{11,3},{4,12},{12,4},... | collective-permute-start | bytes 1376264 | tf_op jit(solution)/shard_map/grads_ffn/ppermute | solution.py:57
  228.6 33.1 %collective-permute-start.32 = (bf16[256,1792]{1,0:T(8,128)(2,1)}, bf16[256,1792]{1,0:T(8,128)(2,1)S(1)}, u32[]{:S(2)}, u32[]{:S(2)}) collective-permute-start(bf16[256,1792]{1,0:T(8,128)(2,1)} %after.42), channel_id=1, source_target_pairs={{0,16},{16,0},{1,17},{17,1},{2,18},{18,2},{3,19},{19,3},{4,20},{20... | collective-permute-start | bytes 2752520 | tf_op jit(solution)/shard_map/grads_ffn/ppermute | solution.py:57
  259.5 33.7 %collective-permute-start.35 = (bf16[256,384]{1,0:T(8,128)(2,1)}, bf16[256,384]{1,0:T(8,128)(2,1)}, u32[]{:S(2)}, u32[]{:S(2)}) collective-permute-start(bf16[256,384]{1,0:T(8,128)(2,1)} %get-tuple-element.85.refs_2_), channel_id=1, source_target_pairs={{0,16},{16,0},{1,17},{17,1},{2,18},{18,2},{3,19},{19,3},{4,20},{20... | collective-permute-start | bytes 589832 | tf_op jit(solution)/shard_map/grads_attn/ppermute | solution.py:57
  268.0 24.1 %all-to-all-start.6 = ((bf16[4,128,1024]{2,1,0:T(8,128)(2,1)}), bf16[4,128,1024]{2,1,0:T(8,128)(2,1)S(1)}, u32[]{:S(2)}, u32[]{:S(2)}) async-start(bf16[4,128,1024]{2,1,0:T(8,128)(2,1)} %bitcast.83), calls=%async_computation.6 | async-start | bytes 2097152 | tf_op jit(solution)/shard_map/sum_dxa/all_to_all | solution.py:679
  273.6 16.9 %collective-permute-start.37 = (bf16[264,384]{1,0:T(8,128)(2,1)S(1)}, bf16[264,384]{1,0:T(8,128)(2,1)S(1)}, u32[]{:S(2)}, u32[]{:S(2)}) collective-permute-start(bf16[264,384]{1,0:T(8,128)(2,1)S(1)} %pad_maximum_fusion.9), channel_id=1, source_target_pairs={{0,8},{8,0},{1,9},{9,1},{2,10},{10,2},{3,11},{11,3},{4,12},{12,4},... | collective-permute-start | bytes 608264 | tf_op jit(solution)/shard_map/grads_attn/ppermute | solution.py:57
  279.5 21.0 %collective-permute-start.38 = (bf16[64,1792]{1,0:T(8,128)(2,1)}, bf16[64,1792]{1,0:T(8,128)(2,1)S(1)}, u32[]{:S(2)}, u32[]{:S(2)}) collective-permute-start(bf16[64,1792]{1,0:T(8,128)(2,1)} %get-tuple-element.94), channel_id=1, source_target_pairs={{0,2},{2,0},{4,6},{6,4},{1,3},{3,1},{5,7},{7,5},{8,10},{10,8},{12,... | collective-permute-start | bytes 688136 | tf_op jit(solution)/shard_map/grads_ffn/ppermute | solution.py:912
  281.5 19.1 %collective-permute-start.39 = (bf16[64,1792]{1,0:T(8,128)(2,1)}, bf16[64,1792]{1,0:T(8,128)(2,1)S(1)}, u32[]{:S(2)}, u32[]{:S(2)}) collective-permute-start(bf16[64,1792]{1,0:T(8,128)(2,1)} %get-tuple-element.95), channel_id=1, source_target_pairs={{0,4},{2,6},{4,0},{6,2},{1,5},{3,7},{5,1},{7,3},{8,12},{10,14},{12... | collective-permute-start | bytes 688136 | tf_op jit(solution)/shard_map/grads_ffn/ppermute | solution.py:912
  283.0 20.2 %collective-permute-start.40 = (bf16[64,1792]{1,0:T(8,128)(2,1)}, bf16[64,1792]{1,0:T(8,128)(2,1)S(1)}, u32[]{:S(2)}, u32[]{:S(2)}) collective-permute-start(bf16[64,1792]{1,0:T(8,128)(2,1)} %get-tuple-element.96), channel_id=1, source_target_pairs={{0,6},{2,4},{4,2},{6,0},{1,7},{3,5},{5,3},{7,1},{8,14},{10,12},{12... | collective-permute-start | bytes 688136 | tf_op jit(solution)/shard_map/grads_ffn/ppermute | solution.py:912
  299.8 13.3 %collective-permute-start.33 = (bf16[2,128,1024]{2,1,0:T(8,128)(2,1)S(1)}, bf16[2,128,1024]{2,1,0:T(8,128)(2,1)S(1)}, u32[]{:S(2)}, u32[]{:S(2)}) collective-permute-start(bf16[2,128,1024]{2,1,0:T(8,128)(2,1)S(1)} %pad_maximum_fusion.4), channel_id=1, source_target_pairs={{0,0},{1,8},{8,1},{9,9},{2,2},{3,10},{10,3},{11,11},{4,4},{5,12},{... | collective-permute-start | bytes 1572872 | tf_op jit(solution)/shard_map/return/ppermute | solution.py:666
  (95 other events, 714.1 us)
